TPU v7x, 512 devices: a whole 4x4x16 slice. The times are simulated.
512 devices in a mesh: ctx: 32 (over z, core), head: 16 (over y, x).
Axes of the slice: x: 4, y: 4, z: 16, core: 2. Of those that a mesh axis runs over, the one named last changes fastest.
Arguments:
- tokens: bfloat16 [16384, 4096], P('ctx', 'head'), may hold values from -8 to 8
- norm_gain: bfloat16 [4096], P('head'), may hold values from 0.099609375 to 1.8984375
- w_qkv: bfloat16 [3, 4096, 2048], P(None, None, 'head'), may hold values from -2 to 2
- doc_lengths: int32 [2], replicated, may hold values from 1 to 15360, 16384 in all
- span_start: int32 [8], replicated, may hold values from 0 to 16383, as said below
- span_len: int32 [8], replicated, may hold values from 256 to 1024, as said below
Outputs:
- attended: bfloat16 [16384, 2048], P('ctx', 'head')
Inputs may be any that keep to these rules, and one draw needn't show every extreme that they name: `span_start`: image k lies inside positions k * 2048 to (k + 1) * 2048 - 1; images don't intersect. `span_len`: one image has exactly 1024 tokens. `doc_lengths`: the lengths sum to 16384.
All inputs are finite; a program needn't handle non-finite values.
Results may differ from a plain program's by a relative error of at most 0.012.
The roundings to bfloat16 on the way count: a program that leaves them out, or rounds other values in their place, can miss the bound.
Values may be sent and summed in bfloat16 or wider, within the bound.
No kernel may reach another device: no remote copies, remote signals or barrier semaphores. Data moves between devices by JAX's collectives and lax.ppermute only.
A program may use at most 64 MiB of HBM per device.

v0:
```python
import jax
import jax.numpy as jnp
from jax import lax
from jax.sharding import PartitionSpec as P

D = 4096
HD = 128


EPS = 1e-05
NEG = -1e30


def row_meta(idx, doc_lengths, span_start, span_len):
    starts = jnp.cumsum(doc_lengths) - doc_lengths
    after = (idx[:, None] >= starts[None, :]).astype(jnp.int32)
    doc = jnp.sum(after, axis=1) - 1
    ranks = jnp.arange(doc_lengths.shape[0], dtype=jnp.int32)
    doc_start = jnp.sum(jnp.where(doc[:, None] == ranks[None, :], starts[None, :], 0), axis=1)
    ends = span_start + span_len
    inside = (idx[:, None] >= span_start[None, :]) & (idx[:, None] < ends[None, :])
    images = jnp.arange(span_start.shape[0], dtype=jnp.int32)
    image = jnp.sum(jnp.where(inside, images[None, :] + 1, 0), axis=1) - 1
    reach = jnp.maximum(idx, jnp.max(jnp.where(inside, ends[None, :] - 1, 0), axis=1))
    return (doc, doc_start, image, reach)


def rotate(values, pos):
    half = values.shape[-1] // 2
    freqs = jnp.power(
        jnp.float32(500000.0), -2.0 * jnp.arange(half, dtype=jnp.float32) / values.shape[-1]
    )
    angle = pos.astype(jnp.float32)[:, None] * freqs[None, :]
    cosine = jnp.cos(angle)
    sine = jnp.sin(angle)
    first = values[:, :half]
    second = values[:, half:]
    return jnp.concatenate([first * cosine - second * sine, second * cosine + first * sine], axis=1)


def body(tokens, norm_gain, w_qkv, doc_lengths, span_start, span_len):
    rows = tokens.shape[0]
    half = rows // 2
    width = w_qkv.shape[2]
    ctx_index = lax.axis_index("ctx")
    own_idx = ctx_index * rows + jnp.arange(rows, dtype=jnp.int32)
    tokf = tokens.astype(jnp.float32)
    squares = lax.psum(jnp.sum(tokf * tokf, axis=1), "head")
    scale = lax.rsqrt(squares / D + EPS)
    normed = (tokf * scale[:, None] * norm_gain.astype(jnp.float32)[None, :]).astype(jnp.bfloat16)
    qkv = jnp.einsum(
        "td,sdh->sth",
        lax.all_gather(normed, "head", axis=1, tiled=True),
        w_qkv,
        preferred_element_type=jnp.float32,
    )
    own_doc, own_start, own_img, own_reach = row_meta(own_idx, doc_lengths, span_start, span_len)
    query = rotate(qkv[0], own_idx - own_start).astype(jnp.bfloat16)
    keys = rotate(qkv[1], own_idx - own_start).astype(jnp.bfloat16)
    values = qkv[2].astype(jnp.bfloat16)
    groups = [(query[:half], own_idx[:half]), (query[half:], own_idx[half:])]
    infos = []
    for rows_q, idx_q in groups:
        q_doc, q_start, q_img, q_reach = row_meta(idx_q, doc_lengths, span_start, span_len)
        infos.append((rows_q, idx_q, q_doc, q_img, jnp.min(q_start), jnp.max(q_reach)))
    empty = (
        jnp.full((half,), NEG, jnp.float32),
        jnp.zeros((half,), jnp.float32),
        jnp.zeros((half, width), jnp.float32),
    )
    carry = (empty, empty)
    start = jnp.int32(0)
    k_piece = lax.all_gather(keys, "ctx", axis=0, tiled=True)
    v_piece = lax.all_gather(values, "ctx", axis=0, tiled=True)
    count = k_piece.shape[0]
    k_idx = jnp.arange(count, dtype=jnp.int32)
    k_doc, k_start, k_img, k_reach = row_meta(k_idx, doc_lengths, span_start, span_len)
    updated = []
    for state, info in zip(carry, infos):
        rows_q, idx_q, q_doc, q_img, lowest, highest = info

        def update(current):
            top_old, total_old, acc_old = current
            scores = jnp.dot(rows_q, k_piece.T, preferred_element_type=jnp.float32) * HD ** (-0.5)
            allowed = (q_doc[:, None] == k_doc[None, :]) & (
                (k_idx[None, :] <= idx_q[:, None])
                | (q_img[:, None] == k_img[None, :]) & (q_img[:, None] >= 0)
            )
            top_new = jnp.maximum(top_old, jnp.max(jnp.where(allowed, scores, NEG), axis=1))
            weights = jnp.where(allowed, jnp.exp(scores - top_new[:, None]), 0.0)
            total_new = jnp.sum(weights, axis=1)
            acc_new = jnp.dot(
                weights.astype(jnp.bfloat16), v_piece, preferred_element_type=jnp.float32
            )
            return (top_new, total_new, acc_new)

        needed = (start <= highest) & (start + count - 1 >= lowest)
        updated.append(lax.cond(needed, update, lambda current: current, state))
    finals = tuple(updated)
    outputs = [(acc / total[:, None]).astype(jnp.bfloat16) for top, total, acc in finals]
    return jnp.concatenate(outputs, axis=0)


def solution(mesh):
    return jax.shard_map(
        body,
        mesh=mesh,
        in_specs=(P("ctx", "head"), P("head"), P(None, None, "head"), P(), P(), P()),
        out_specs=P("ctx", "head"),
        check_vma=False,
    )
```

profile of v0, /device:TPU:1, one launch (start us, length us, event | category | flops | bytes accessed | tf_op | source)
XLA Modules:
  0.0 345.7 jit_solution(15582127042153818789)
XLA Ops:
  6.5 1.1 fusion.16
  7.7 34.3 %psum.7 = f32[512]{0:T(512)S(1)} all-reduce(f32[512]{0:T(512)S(1)} %fusion.16), channel_id=1, replica_groups=mesh['ctx'=32,'head'=16] {'head'}, use_global_device_ids=true, to_apply=%region_7.8 | all-reduce | flops 512 | bytes 4096 | tf_op jit(solution)/shard_map/psum | solution.py:48
  41.9 0.7 convert_element_type.59
  42.6 1.8 fusion.18
  44.4 3.2 copy.14
  47.7 0.8 reduce-window.9
  49.3 73.8 %all-gather.5.cloned.1.call-done = bf16[512,4096]{1,0:T(8,128)(2,1)} async-done(((bf16[512,256]{1,0:T(8,128)(2,1)}), bf16[512,4096]{1,0:T(8,128)(2,1)}) %all-gather.5.cloned.1.call-update) | async-done | bytes 4194320 | tf_op jit(solution)/shard_map/all_gather | solution.py:53
  123.2 4.0 %fusion.44 = f32[512,384]{0,1:S(1)} fusion(bf16[512,4096]{1,0:T(8,128)(2,1)} %all-gather.5.cloned.1.call-done, bf16[4096,384]{0,1:T(8,128)(2,1)S(1)} %bitcast.20), kind=kOutput, calls=%fused_computation.100 | convolution fusion | flops 1610612736 | bytes 8126464
  128.1 0.7 pad_maximum_fusion.1
  128.8 1.6 slice.73
  130.6 0.7 maximum_reduce_fusion.1
  132.1 0.7 reduce_min.18
  134.2 0.7 reduce_min.19
  136.3 67.2 %all-gather.7.cloned.1.call-done = bf16[16384,128]{0,1:T(8,128)(2,1)} async-done(((bf16[512,128]{0,1:T(8,128)(2,1)}), bf16[16384,128]{0,1:T(8,128)(2,1)}) %all-gather.7.cloned.1.call-update) | async-done | bytes 4194320 | tf_op jit(solution)/shard_map/all_gather | solution.py:73
  203.5 73.1 %all-gather.9.cloned.1.call-done = bf16[1,16384,128]{1,2,0:T(8,128)(2,1)} async-done(((bf16[1,512,128]{1,2,0:T(8,128)(2,1)}), bf16[1,16384,128]{1,2,0:T(8,128)(2,1)}) %all-gather.9.cloned.1.call-update) | async-done | bytes 4194320 | tf_op jit(solution)/shard_map/all_gather | solution.py:74
  276.6 31.0 %conditional.2 = (f32[256]{0:T(256)S(1)}, f32[256,128]{1,0:T(8,128)S(1)}) conditional(s32[]{:T(128)} %convert_element_type.56, () %tuple.27, (s32[256]{0:T(256)S(1)}, s32[16384]{0:T(1024)S(1)}, s32[16384]{0:T(1024)S(1)}, s32[256]{0:T(256)S(1)}, s32[8]{0:T(128)S(1)}, /*index=5*/pred[256,8]{0,1:T(8,128)(4,1)S(1)}, s32[256,8]{0,1:T(8,128)S(1)}, ...), branch_computations={%region_12.13_spmd, %region_13.17_spmd} | conditional | flops 2260734464 | bytes 59801904 | solution.py:98
  277.2 10.4 %select_reduce_fusion = (f32[256]{0:T(256)S(1)}, f32[256,16384]{1,0:T(8,128)S(1)}) fusion(pred[256]{0:T(512)(128)(4,1)S(1)} %broadcast_compare_fusion, s32[16384]{0:T(1024)S(1)} %get-tuple-element.128, s32[256]{0:T(256)S(1)} %get-tuple-element.205, s32[256]{0:T(256)S(1)} %get-tuple-element.124, s32[16384]{0:T(1024)S(1)} %get-tuple-element.123, ...), kind=kOutput, calls=%fused_computation.2 | convolution fusion | flops 1111490304 | bytes 21238272 | tf_op jit(solution)/shard_map/cond/branch_1_fun/dot_general | solution.py:84
  287.6 10.5 %fusion.2 = f32[256,128]{1,0:T(8,128)S(1)} fusion(bf16[16384,128]{0,1:T(8,128)(2,1)} %get-tuple-element.183, f32[256,16384]{1,0:T(8,128)S(1)} %get-tuple-element.204, f32[256]{0:T(256)S(1)} %broadcast_maximum_fusion, s32[16384]{0:T(1024)S(1)} %get-tuple-element.128, s32[16384]{0:T(1024)S(1)} %get-tuple-element.123, s32[16384]{0:T(1024)S(1)} %get-tuple-element.122, ...), kind=kOutput, calls=%fused_computation.6 | convolution fusion | flops 1111490560 | bytes 21303552 | tf_op jit(solution)/shard_map/cond/branch_1_fun/dot_general | solution.py:92
  298.1 9.4 %fusion.1 = f32[256]{0:T(256)S(1)} fusion(f32[256,16384]{1,0:T(8,128)S(1)} %get-tuple-element.204, f32[256]{0:T(256)S(1)} %broadcast_maximum_fusion, pred[256]{0:T(512)(128)(4,1)S(1)} %broadcast_compare_fusion, s32[16384]{0:T(1024)S(1)} %get-tuple-element.128, s32[256]{0:T(256)S(1)} %get-tuple-element.205, s32[256]{0:T(256)S(1)} %get-tuple-element.124, ...), kind=kLoop, calls=%fused_computation.5 | loop fusion | flops 37748480 | bytes 16979200 | tf_op jit(solution)/shard_map/cond/branch_1_fun/reduce_sum | solution.py:91
  307.7 30.4 %conditional.3 = (f32[256]{0:T(256)S(1)}, f32[256,128]{1,0:T(8,128)S(1)}) conditional(s32[]{:T(128)} %convert_element_type.66, () %tuple.29, (s32[256]{0:T(256)S(1)}, s32[16384]{0:T(1024)S(1)}, s32[16384]{0:T(1024)S(1)}, s32[256]{0:T(256)S(1)}, s32[8]{0:T(128)S(1)}, /*index=5*/pred[256,8]{0,1:T(8,128)(4,1)S(1)}, s32[256,8]{0,1:T(8,128)S(1)}, ...), branch_computations={%region_22.23_spmd, %region_23.27_spmd} | conditional | flops 2260734464 | bytes 59801904 | solution.py:98
  308.0 10.4 %select_reduce_fusion.2 = (f32[256]{0:T(256)S(1)}, f32[256,16384]{1,0:T(8,128)S(1)}) fusion(pred[256]{0:T(512)(128)(4,1)S(1)} %broadcast_compare_fusion.1, s32[16384]{0:T(1024)S(1)} %get-tuple-element.139, s32[256]{0:T(256)S(1)} %get-tuple-element.209, s32[256]{0:T(256)S(1)} %get-tuple-element.135, s32[16384]{0:T(1024)S(1)} %get-tuple-element.134, ...), kind=kOutput, calls=%fused_computation.18 | convolution fusion | flops 1111490304 | bytes 21238272 | tf_op jit(solution)/shard_map/cond/branch_1_fun/dot_general | solution.py:84
  318.4 10.1 %fusion.10 = f32[256,128]{1,0:T(8,128)S(1)} fusion(bf16[16384,128]{0,1:T(8,128)(2,1)} %get-tuple-element.194, f32[256,16384]{1,0:T(8,128)S(1)} %get-tuple-element.208, f32[256]{0:T(256)S(1)} %broadcast_maximum_fusion.1, s32[16384]{0:T(1024)S(1)} %get-tuple-element.139, s32[16384]{0:T(1024)S(1)} %get-tuple-element.134, s32[16384]{0:T(1024)S(1)} %get-tuple-element.133, ...), kind=kOutput, calls=%fused_computation.22 | convolution fusion | flops 1111490560 | bytes 21303552 | tf_op jit(solution)/shard_map/cond/branch_1_fun/dot_general | solution.py:92
  328.5 9.3 %fusion.9 = f32[256]{0:T(256)S(1)} fusion(f32[256,16384]{1,0:T(8,128)S(1)} %get-tuple-element.208, f32[256]{0:T(256)S(1)} %broadcast_maximum_fusion.1, pred[256]{0:T(512)(128)(4,1)S(1)} %broadcast_compare_fusion.1, s32[16384]{0:T(1024)S(1)} %get-tuple-element.139, s32[256]{0:T(256)S(1)} %get-tuple-element.209, s32[256]{0:T(256)S(1)} %get-tuple-element.135, ...), kind=kLoop, calls=%fused_computation.21 | loop fusion | flops 37748480 | bytes 16979200 | tf_op jit(solution)/shard_map/cond/branch_1_fun/reduce_sum | solution.py:91
  338.2 0.7 pad_maximum_fusion.2
  (51 shorter events, 3.6 us)
Async XLA Ops:
  6.5 123.9 %copy-start.1 = (s32[8]{0:T(128)S(1)}, s32[8]{0:T(128)}, u32[]{:S(2)}) copy-start(s32[8]{0:T(128)} %param.14) | copy-start | bytes 100
  6.5 123.9 %copy-start.2 = (s32[8]{0:T(128)S(1)}, s32[8]{0:T(128)}, u32[]{:S(2)}) copy-start(s32[8]{0:T(128)} %param.15) | copy-start | bytes 100
  6.5 116.6 %all-gather.5.cloned.1.call-start = ((), (), s32[]{:S(2)}) async-start(), calls=%async_computation | async-start | bytes 4456448 | tf_op jit(solution)/shard_map/all_gather | solution.py:53
  44.4 159.1 %all-gather.7.cloned.1.call-start = ((), (), s32[]{:S(2)}) async-start(), calls=%async_computation.1 | async-start | bytes 4325376 | tf_op jit(solution)/shard_map/all_gather | solution.py:73
  127.2 0.9 copy-start
  128.7 147.9 %all-gather.9.cloned.1.call-start = ((), (), s32[]{:S(2)}) async-start(), calls=%async_computation.2 | async-start | bytes 4325376 | tf_op jit(solution)/shard_map/all_gather | solution.py:74
Sparse Core Ops, SparseCore 0:
  44.5 78.6 all-gather.4
  128.9 74.5 all-gather.6
  205.6 70.9 all-gather.8
where the time goes:
time: 350 us; the launch traced here: 346 us
  waiting for transfers between devices  214 us (61%)
  matrix products  45.4 us (13%)
  blocking collectives  34.3 us (10%)
  other arithmetic  29.5 us (8%)
  between operations  16.2 us (5%)
  local copies, waits for them, and re-layouts  5.35 us (2%)
    all_gather x1, waiting for transfers between devices, body(): lax.all_gather(normed, 'head', axis=1, tiled=True)  73.8 us
    all_gather x1, waiting for transfers between devices, body(): v_piece = lax.all_gather(values, 'ctx', axis=0, tiled=True)  73.1 us
    all_gather x1, waiting for transfers between devices, body(): k_piece = lax.all_gather(keys, 'ctx', axis=0, tiled=True)  67.2 us
    psum x1, blocking collectives, body(): squares = lax.psum(jnp.sum(tokf * tokf, axis=1), 'head')  34.3 us
    dot_general x2, matrix products, update(): jnp.dot(rows_q, k_piece.T, preferred_element_type=jnp.float32)  20.8 us
    dot_general x2, matrix products, update(): jnp.dot(weights.astype(jnp.bfloat16), v_piece, preferred_element_type=jnp...  20.6 us
    reduce_sum x2, other arithmetic, update(): total_new = jnp.sum(weights, axis=1)  18.7 us
  transfers between devices with their start and end apart: 3, of which 3 were waited for; matrix products, arithmetic and copies ran while one was open for 3% of the time, Pallas kernels for 0%

commit v1 on v0

v1 whole, which is shorter than its diff:
```python
import functools
import math

import jax
import jax.numpy as jnp
from jax import lax
from jax.experimental import pallas as pl
from jax.experimental.pallas import tpu as pltpu
from jax.sharding import Mesh, PartitionSpec as P

D = 4096
HD = 128
EPS = 1e-05
NEG = -1e30
ROWS = 512
FEAT = 256
PAD = 16
NZ = 16
C2 = math.log2(math.e) * HD**-0.5
STEPS = (0, 1, -1, 2)


def row_meta(idx, doc_lengths, span_start, span_len):
    starts = jnp.cumsum(doc_lengths) - doc_lengths
    mine = (idx[:, None] >= starts[None, :]) & (idx[:, None] < (starts + doc_lengths)[None, :])
    first = jnp.sum(jnp.where(mine, starts[None, :], 0), axis=1)
    last = jnp.sum(jnp.where(mine, (starts + doc_lengths)[None, :], 0), axis=1) - 1
    ends = span_start + span_len
    inside = (idx[:, None] >= span_start[None, :]) & (idx[:, None] < ends[None, :])
    reach = jnp.maximum(idx, jnp.max(jnp.where(inside, ends[None, :] - 1, 0), axis=1))
    return first, jnp.minimum(reach, last)


def angles(pos):
    half = HD // 2
    freqs = jnp.power(jnp.float32(500000.0), -2.0 * jnp.arange(half, dtype=jnp.float32) / HD)
    angle = pos.astype(jnp.float32)[:, None] * freqs[None, :]
    cosine = jnp.cos(angle)
    sine = jnp.sin(angle)
    return (
        jnp.concatenate([cosine, cosine], axis=1),
        jnp.concatenate([-sine, sine], axis=1),
    )


def qkv_kernel(blk_ref, *refs):
    sets, (w_ref, cos_ref, sin_ref, q_ref, kv_ref, nrm) = refs[:8], refs[8:]
    tile = 64

    def norm_rows(i, carry):
        r = pl.multiple_of(i * tile, tile)
        acc = jnp.zeros((tile, FEAT), jnp.float32)
        for b in range(16):
            x = sets[b // 2][b % 2, pl.ds(r, tile), :].astype(jnp.float32)
            acc = acc + x * x
        scale = lax.rsqrt(jnp.sum(acc, axis=1, keepdims=True) / D + EPS)
        for b in range(16):
            x = sets[b // 2][b % 2, pl.ds(r, tile), :].astype(jnp.float32)
            gain = sets[b // 2][b % 2, ROWS : ROWS + 1, :].astype(jnp.float32)
            col = pl.multiple_of(blk_ref[b] * FEAT, FEAT)
            nrm[pl.ds(r, tile), pl.ds(col, FEAT)] = (x * scale * gain).astype(jnp.bfloat16)
        return carry

    lax.fori_loop(0, ROWS // tile, norm_rows, 0)
    out = jnp.dot(nrm[...], w_ref[...], preferred_element_type=jnp.float32)
    cosine, sine = cos_ref[...], sin_ref[...]

    def rotate(v):
        return (v * cosine + pltpu.roll(v, HD // 2, 1) * sine).astype(jnp.bfloat16)

    q_ref[...] = rotate(out[:, :HD])
    kv_ref[:ROWS, :] = rotate(out[:, HD : 2 * HD])
    vt = out[:, 2 * HD :].T.astype(jnp.bfloat16)
    for b in range(ROWS // HD):
        kv_ref[ROWS + b * HD : ROWS + (b + 1) * HD, :] = vt[:, b * HD : (b + 1) * HD]


def project(blk, sets, w, cosine, sine):
    vmem = pl.BlockSpec(memory_space=pltpu.VMEM)
    return pl.pallas_call(
        qkv_kernel,
        out_shape=(
            jax.ShapeDtypeStruct((ROWS, HD), jnp.bfloat16),
            jax.ShapeDtypeStruct((2 * ROWS, HD), jnp.bfloat16),
        ),
        in_specs=[pl.BlockSpec(memory_space=pltpu.SMEM)] + [vmem] * 11,
        out_specs=(vmem, vmem),
        scratch_shapes=[pltpu.VMEM((ROWS, D), jnp.bfloat16)],
        compiler_params=pltpu.CompilerParams(vmem_limit_bytes=40 * 2**20),
        cost_estimate=pl.CostEstimate(
            flops=2 * ROWS * D * 3 * HD, bytes_accessed=8 * 2**20, transcendentals=0
        ),
        name="norm_qkv",
    )(blk, *sets, w, cosine, sine)


def attend_kernel(offs, fresh, meta_ref, q_ref, lo_ref, hi_ref, *refs):
    n = len(offs)
    kvs, st = refs[:n], refs[-1]
    if fresh:
        row = lax.broadcasted_iota(jnp.int32, st.shape, 1)
        st[...] = jnp.where(row == HD, NEG, 0.0)
    else:
        st[...] = refs[n][...]
    wide = 256
    per = ROWS // wide
    firsts = [
        (lax.rem(meta_ref[8] + (off + NZ), NZ) * 2 + meta_ref[9]) * ROWS for off in offs
    ]

    def part(js, masked, i, carry):
        t = i // per
        cols = pl.ds(pl.multiple_of((i % per) * wide, wide), wide)
        query = q_ref[t, cols, :]
        ss = [
            lax.dot_general(
                kvs[j][:ROWS, :], query, (((1,), (1,)), ((), ())), preferred_element_type=jnp.float32
            )
            for j in js
        ]
        oks = [None] * len(js)
        if masked:
            lo, hi = lo_ref[t, :, cols], hi_ref[t, :, cols]
            row = lax.broadcasted_iota(jnp.int32, ss[0].shape, 0)
            oks = [(row >= lo - firsts[j]) & (row <= hi - firsts[j]) for j in js]
            ss = [jnp.where(ok, s, NEG) for ok, s in zip(oks, ss)]
        m_old = st[t, HD : HD + 1, cols]
        m_new = m_old
        for s in ss:
            m_new = jnp.maximum(m_new, jnp.max(s, axis=0, keepdims=True))
        alpha = jnp.exp2((m_old - m_new) * C2)
        total = st[t, HD + 1 : HD + 2, cols] * alpha
        acc = st[t, :HD, cols] * alpha
        shift = m_new * C2
        for j, s, ok in zip(js, ss, oks):
            p = jnp.exp2(s * C2 - shift)
            if masked:
                p = jnp.where(ok, p, 0.0)
            total = total + jnp.sum(p, axis=0, keepdims=True)
            vt = jnp.concatenate(
                [kvs[j][ROWS + b * HD : ROWS + (b + 1) * HD, :] for b in range(ROWS // HD)], axis=1
            )
            acc = acc + jnp.dot(vt, p.astype(jnp.bfloat16), preferred_element_type=jnp.float32)
        st[t, HD : HD + 1, cols] = m_new
        st[t, HD + 1 : HD + 2, cols] = total
        st[t, :HD, cols] = acc
        return carry

    needed, whole = {}, []
    for j in range(n):
        last = firsts[j] + ROWS - 1
        for t in range(2):
            needed[j, t] = (firsts[j] <= meta_ref[4 * t + 3]) & (last >= meta_ref[4 * t])
            whole.append((firsts[j] >= meta_ref[4 * t + 1]) & (last <= meta_ref[4 * t + 2]))
    every = functools.reduce(jnp.logical_and, whole)

    @pl.when(every)
    def _():
        lax.fori_loop(0, 2 * per, functools.partial(part, range(n), False), 0)

    for j in range(n):

        @pl.when(jnp.logical_not(every) & (needed[j, 0] | needed[j, 1]))
        def _(j=j):
            begin = jnp.where(needed[j, 0], 0, per)
            end = jnp.where(needed[j, 1], 2 * per, per)
            lax.fori_loop(begin, end, functools.partial(part, [j], True), 0)


def attend(meta, q, lo, hi, kvs, offs, state):
    n = len(kvs)
    vmem = pl.BlockSpec(memory_space=pltpu.VMEM)
    state = [] if state is None else [state]
    pairs = 2 * ROWS * ROWS * n
    return pl.pallas_call(
        functools.partial(attend_kernel, offs, not state),
        out_shape=jax.ShapeDtypeStruct((2, HD + 8, ROWS), jnp.float32),
        in_specs=[pl.BlockSpec(memory_space=pltpu.SMEM)] + [vmem] * (3 + n + len(state)),
        out_specs=vmem,
        input_output_aliases={4 + n: 0} if state else {},
        compiler_params=pltpu.CompilerParams(vmem_limit_bytes=40 * 2**20),
        cost_estimate=pl.CostEstimate(
            flops=4 * pairs * HD, bytes_accessed=2 * 2**20, transcendentals=pairs
        ),
        name="attend",
    )(meta, q, lo, hi, *kvs, *state)


def merge_kernel(a_ref, b_ref, o_ref):
    ma, mb = a_ref[HD : HD + 1, :], b_ref[HD : HD + 1, :]
    m = jnp.maximum(ma, mb)
    wa, wb = jnp.exp2((ma - m) * C2), jnp.exp2((mb - m) * C2)
    total = a_ref[HD + 1 : HD + 2, :] * wa + b_ref[HD + 1 : HD + 2, :] * wb
    out = (a_ref[:HD, :] * wa + b_ref[:HD, :] * wb) / total
    o_ref[...] = out.T.astype(jnp.bfloat16)


def merge(a, b):
    return pl.pallas_call(
        merge_kernel, out_shape=jax.ShapeDtypeStruct((ROWS, HD), jnp.bfloat16), name="merge"
    )(a, b)


def plane_perm(d, first):
    out = []
    for c in range(2):
        for y in range(4):
            for x in range(4):
                if (c == 0) == first:
                    to = (y, (x + d) % 4)
                else:
                    to = ((y + d) % 4, x)
                out.append(((c * 4 + y) * 4 + x, (c * 4 + to[0]) * 4 + to[1]))
    return out


def ring(n, d):
    return [(i, (i + d) % n) for i in range(n)]


def body(tokens, norm_gain, w_qkv, doc_lengths, span_start, span_len):
    z, core = lax.axis_index("z"), lax.axis_index("core")
    y, x = lax.axis_index("y"), lax.axis_index("x")
    plane = ("core", "y", "x")

    mine = jnp.concatenate([tokens, jnp.broadcast_to(norm_gain[None, :], (PAD, FEAT))], axis=0)
    side = {d: lax.ppermute(mine, plane, plane_perm(d, True)) for d in (1, -1, 2)}
    a, b = jnp.stack([mine, side[1]]), jnp.stack([side[-1], side[2]])
    far = lambda v, d: lax.ppermute(v, plane, plane_perm(d, False))
    left_a, right_b = far(a, 1), far(b, -1)
    left_b, right_a = far(b, 1), far(a, -1)
    sets = [a, b, left_a, left_b, right_a, right_b, far(left_a, 1), far(right_b, -1)]
    dk = jnp.array([k for k in STEPS for j in STEPS], jnp.int32)
    dj = jnp.array([j for k in STEPS for j in STEPS], jnp.int32)
    on_x = jnp.where(core == 0, dj, dk)
    on_y = jnp.where(core == 0, dk, dj)
    blk = ((y - on_y + 4) % 4) * 4 + (x - on_x + 4) % 4

    offs = jnp.arange(ROWS, dtype=jnp.int32)
    first_of = lambda c: (z * 2 + c) * ROWS
    lows, highs = [], []
    for c in (core, 1 - core):
        low, high = row_meta(first_of(c) + offs, doc_lengths, span_start, span_len)
        lows.append(low)
        highs.append(high)
    cosine, sine = angles(first_of(core) + offs - lows[0])
    lo, hi = jnp.stack(lows)[:, None, :], jnp.stack(highs)[:, None, :]
    slot = jnp.arange(16, dtype=jnp.int32)
    at = first_of(jnp.where(slot < 4, core, 1 - core)) + (slot % 2) * (ROWS - 1)
    low, high = row_meta(at, doc_lengths, span_start, span_len)
    meta = jnp.where(slot % 4 < 2, low, high)
    meta = jnp.where(slot == 8, z, jnp.where(slot == 9, core, meta)).astype(jnp.int32)

    w = jnp.concatenate([w_qkv[0], w_qkv[1], w_qkv[2]], axis=1)
    q, kv = project(blk, sets, w, cosine, sine)

    up = down = kv
    q2 = jnp.stack([q, lax.ppermute(q, "core", ring(2, 1))], axis=0)
    state = None
    arrived, sources = [kv], [0]
    for i in range(1, NZ // 2 + 1):
        up = lax.ppermute(up, "z", ring(NZ, 1))
        new, src = [up], [-i]
        if i < NZ // 2:
            down = lax.ppermute(down, "z", ring(NZ, -1))
            new, src = new + [down], src + [i]
        state = attend(meta, q2, lo, hi, arrived, sources, state)
        up, state = lax.optimization_barrier((up, state))
        new[0] = up
        arrived, sources = new, src
    state = attend(meta, q2, lo, hi, arrived, sources, state)
    other = lax.ppermute(state[1], "core", ring(2, 1))
    return merge(state[0], other)


def solution(mesh):
    fine = Mesh(mesh.devices.reshape(NZ, 2, 4, 4), ("z", "core", "y", "x"))
    both, plane = ("z", "core"), ("y", "x")
    return jax.shard_map(
        body,
        mesh=fine,
        in_specs=(P(both, plane), P(plane), P(None, None, plane), P(), P(), P()),
        out_specs=P(both, plane),
        check_vma=False,
    )
```

time: 350 us -> 158 us (0.45)
  waiting for transfers between devices: 214 us -> 28.6 us
  starting transfers between devices: 0.09 us -> 97.8 us
  matrix products: 45.4 us -> 0 us
  blocking collectives: 34.3 us -> 0 us
  other arithmetic: 29.5 us -> 10.4 us
  between operations: 16.2 us -> 0.57 us
  Pallas kernels: 0 us -> 15.3 us
    all_gather x3 -> x0, waiting for transfers between devices: 214 us -> none  [the longest x1 73.8 us: body(): lax.all_gather(normed, 'head', axis=1, tiled=True)]
    ppermute x0 -> x26, starting transfers between devices: none -> 97.8 us  [the longest x7 36.9 us: body(): down = lax.ppermute(down, 'z', ring(NZ, -1))]
    dot_general x4 -> x0, matrix products: 41.4 us -> none  [the longest x2 20.8 us: update(): jnp.dot(rows_q, k_piece.T, preferred_element_type=jnp.float32)]
    psum x1 -> x0, blocking collectives: 34.3 us -> none  [body(): squares = lax.psum(jnp.sum(tokf * tokf, axis=1), 'head')]
    ppermute x0 -> x26, waiting for transfers between devices: none -> 28.6 us  [the longest x8 18.2 us: body(): up = lax.ppermute(up, 'z', ring(NZ, 1))]
    reduce_sum x12 -> x2, other arithmetic: 21.1 us -> 0.19 us  [row_meta(): jnp.sum(jnp.where(mine, (starts + doc_lengths)[None, :], 0), axis=1) - 1]
    pallas_call x0 -> x11, Pallas kernels: none -> 15.3 us  [the longest x9 8.22 us: attend(): pl.pallas_call(functools.partial(attend_kernel, offs, not state), out_sha...]
    unnamed x1 -> x0, matrix products: 4 us -> none
  transfers between devices with their start and end apart: 3 -> 26, of which waited for: 3 -> 12; matrix products, arithmetic and copies ran while one was open for 3% -> 7% of each run, Pallas kernels for 0% -> 5%
where the time goes in v1:
time: 158 us; the launch traced here: 157 us
  starting transfers between devices  97.8 us (62%)
  waiting for transfers between devices  28.6 us (18%)
  Pallas kernels  15.3 us (10%)
  other arithmetic  10.4 us (7%)
  local copies, waits for them, and re-layouts  4.23 us (3%)
    ppermute x7, starting transfers between devices, body(): down = lax.ppermute(down, 'z', ring(NZ, -1))  36.9 us
    ppermute x8, waiting for transfers between devices, body(): up = lax.ppermute(up, 'z', ring(NZ, 1))  18.2 us
    ppermute x6, starting transfers between devices, body(): far = lambda v, d: lax.ppermute(v, plane, plane_perm(d, False))  18.1 us
    ppermute x8, starting transfers between devices, body(): up = lax.ppermute(up, 'z', ring(NZ, 1))  16.9 us
    ppermute x3, starting transfers between devices, body(): lax.ppermute(mine, plane, plane_perm(d, True))  10.3 us
    ppermute x1, starting transfers between devices, body(): other = lax.ppermute(state[1], 'core', ring(2, 1))  9.95 us
    ppermute x6, waiting for transfers between devices, body(): far = lambda v, d: lax.ppermute(v, plane, plane_perm(d, False))  9.22 us
    pallas_call x9, Pallas kernels, attend(): pl.pallas_call(functools.partial(attend_kernel, offs, not state), out_sha...  8.22 us
  transfers between devices with their start and end apart: 26, of which 12 were waited for; matrix products, arithmetic and copies ran while one was open for 7% of the time, Pallas kernels for 5%

profile of v1, /device:TPU:1, one launch (start us, length us, event | category | flops | bytes accessed | tf_op | source)
XLA Modules:
  0.0 156.9 jit_solution(8733580209972945943)
XLA Ops:
  2.3 5.5 %collective-permute-start.1 = (bf16[528,256]{1,0:T(8,128)(2,1)}, bf16[528,256]{1,0:T(8,128)(2,1)}, u32[]{:S(2)}, u32[]{:S(2)}) collective-permute-start(bf16[528,256]{1,0:T(8,128)(2,1)} %get-tuple-element.59), channel_id=1, source_target_pairs={{0,3},{1,0},{2,1},{3,2},{4,7},{5,4},{6,5},{7,6},{8,11},{9,8},{10,9... | collective-permute-start | bytes 811016 | tf_op jit(solution)/shard_map/ppermute | solution.py:227
  7.8 2.3 %collective-permute-start.2 = (bf16[528,256]{1,0:T(8,128)(2,1)}, bf16[528,256]{1,0:T(8,128)(2,1)}, u32[]{:S(2)}, u32[]{:S(2)}) collective-permute-start(bf16[528,256]{1,0:T(8,128)(2,1)} %get-tuple-element.59), channel_id=1, source_target_pairs={{0,2},{1,3},{2,0},{3,1},{4,6},{5,7},{6,4},{7,5},{8,10},{9,11},{10,... | collective-permute-start | bytes 811016 | tf_op jit(solution)/shard_map/ppermute | solution.py:227
  10.1 2.6 %collective-permute-start = (bf16[528,256]{1,0:T(8,128)(2,1)}, bf16[528,256]{1,0:T(8,128)(2,1)}, u32[]{:S(2)}, u32[]{:S(2)}) collective-permute-start(bf16[528,256]{1,0:T(8,128)(2,1)} %get-tuple-element.59), channel_id=1, source_target_pairs={{0,1},{1,2},{2,3},{3,0},{4,5},{5,6},{6,7},{7,4},{8,9},{9,10},{10,1... | collective-permute-start | bytes 811016 | tf_op jit(solution)/shard_map/ppermute | solution.py:227
  19.8 4.4 %collective-permute-start.6 = (bf16[2,528,256]{2,1,0:T(8,128)(2,1)S(1)}, bf16[2,528,256]{2,1,0:T(8,128)(2,1)S(1)}, u32[]{:S(2)}, u32[]{:S(2)}) collective-permute-start(bf16[2,528,256]{2,1,0:T(8,128)(2,1)S(1)} %pad_maximum_fusion.2.refs_1_), channel_id=1, source_target_pairs={{0,12},{1,13},{2,14},{3,15},{4,0},{5,1},{6,2},{7,3},{8,4},{9,5},{1... | collective-permute-start | bytes 1622024 | tf_op jit(solution)/shard_map/ppermute | solution.py:229
  29.5 2.1 %collective-permute-start.4 = (bf16[2,528,256]{2,1,0:T(8,128)(2,1)S(1)}, bf16[2,528,256]{2,1,0:T(8,128)(2,1)S(1)}, u32[]{:S(2)}, u32[]{:S(2)}) collective-permute-start(bf16[2,528,256]{2,1,0:T(8,128)(2,1)S(1)} %pad_maximum_fusion.2.refs_1_), channel_id=1, source_target_pairs={{0,4},{1,5},{2,6},{3,7},{4,8},{5,9},{6,10},{7,11},{8,12},{9,13},{1... | collective-permute-start | bytes 1622024 | tf_op jit(solution)/shard_map/ppermute | solution.py:229
  31.7 4.4 %collective-permute-start.5 = (bf16[2,528,256]{2,1,0:T(8,128)(2,1)S(1)}, bf16[2,528,256]{2,1,0:T(8,128)(2,1)S(1)}, u32[]{:S(2)}, u32[]{:S(2)}) collective-permute-start(bf16[2,528,256]{2,1,0:T(8,128)(2,1)S(1)} %pad_maximum_fusion.1.refs_0_), channel_id=1, source_target_pairs={{0,12},{1,13},{2,14},{3,15},{4,0},{5,1},{6,2},{7,3},{8,4},{9,5},{1... | collective-permute-start | bytes 1622024 | tf_op jit(solution)/shard_map/ppermute | solution.py:229
  36.1 3.4 %collective-permute-start.8 = (bf16[2,528,256]{2,1,0:T(8,128)(2,1)S(1)}, bf16[2,528,256]{2,1,0:T(8,128)(2,1)S(1)}, u32[]{:S(2)}, u32[]{:S(2)}) collective-permute-start(bf16[2,528,256]{2,1,0:T(8,128)(2,1)S(1)} %collective-permute-done.6.refs_5_), channel_id=1, source_target_pairs={{0,12},{1,13},{2,14},{3,15},{4,0},{5,1},{6,2},{7,3},{8,4},{9,5},{1... | collective-permute-start | bytes 1622024 | tf_op jit(solution)/shard_map/ppermute | solution.py:229
  42.6 5.5 %collective-permute-done.8.refs_7_ = bf16[2,528,256]{2,1,0:T(8,128)(2,1)S(1)} collective-permute-done((bf16[2,528,256]{2,1,0:T(8,128)(2,1)S(1)}, bf16[2,528,256]{2,1,0:T(8,128)(2,1)S(1)}, u32[]{:S(2)}, u32[]{:S(2)}) %collective-permute-start.8) | collective-permute-done | bytes 540704 | tf_op jit(solution)/shard_map/ppermute | solution.py:229
  48.1 2.9 %collective-permute-done.7.refs_6_ = bf16[2,528,256]{2,1,0:T(8,128)(2,1)S(1)} collective-permute-done((bf16[2,528,256]{2,1,0:T(8,128)(2,1)S(1)}, bf16[2,528,256]{2,1,0:T(8,128)(2,1)S(1)}, u32[]{:S(2)}, u32[]{:S(2)}) %collective-permute-start.7) | collective-permute-done | bytes 540704 | tf_op jit(solution)/shard_map/ppermute | solution.py:229
  51.1 5.3 %norm_qkv.1 = (bf16[512,128]{1,0:T(8,128)(2,1)S(1)}, bf16[1024,128]{1,0:T(8,128)(2,1)S(1)}) custom-call(s32[16]{0:T(128)S(1)} %fusion.1.blk_ref, bf16[2,528,256]{2,1,0:T(8,128)(2,1)S(1)} %pad_maximum_fusion.1.refs_0_, bf16[2,528,256]{2,1,0:T(8,128)(2,1)S(1)} %pad_maximum_fusion.2.refs_1_, bf16[2,528,256]{2,1,0:T(8,128)(2,1)S(1)} %collective-permute-done.3.refs_2_, ...), custom_call_target="tpu_custom_call" | custom-call | flops 1610612736 | bytes 8388608 | tf_op jit(solution)/shard_map/norm_qkv/pallas_call | solution.py:80
  56.3 5.6 %collective-permute-start.9 = (bf16[512,128]{1,0:T(8,128)(2,1)S(1)}, bf16[512,128]{1,0:T(8,128)(2,1)S(1)}, u32[]{:S(2)}, u32[]{:S(2)}) collective-permute-start(bf16[512,128]{1,0:T(8,128)(2,1)S(1)} %get-tuple-element.23), channel_id=1, source_target_pairs={{0,16},{16,0},{1,17},{17,1},{2,18},{18,2},{3,19},{19,3},{4,20},{20... | collective-permute-start | bytes 393224 | tf_op jit(solution)/shard_map/ppermute | solution.py:258
  61.9 3.5 %collective-permute-start.10 = (bf16[1024,128]{1,0:T(8,128)(2,1)S(1)}, bf16[1024,128]{1,0:T(8,128)(2,1)S(1)}, u32[]{:S(2)}, u32[]{:S(2)}) collective-permute-start(bf16[1024,128]{1,0:T(8,128)(2,1)S(1)} %get-tuple-element.24.refs_0_), channel_id=1, source_target_pairs={{0,32},{32,64},{64,96},{96,128},{128,160},{160,192},{192,224},{224... | collective-permute-start | bytes 786440 | tf_op jit(solution)/shard_map/ppermute | solution.py:262
  65.5 9.5 %collective-permute-start.12 = (bf16[1024,128]{1,0:T(8,128)(2,1)S(1)}, bf16[1024,128]{1,0:T(8,128)(2,1)S(1)}, u32[]{:S(2)}, u32[]{:S(2)}) collective-permute-start(bf16[1024,128]{1,0:T(8,128)(2,1)S(1)} %get-tuple-element.24.refs_0_), channel_id=1, source_target_pairs={{0,480},{32,0},{64,32},{96,64},{128,96},{160,128},{192,160},{224,1... | collective-permute-start | bytes 786440 | tf_op jit(solution)/shard_map/ppermute | solution.py:265
  75.1 2.9 %attend.9.refs_2_ = f32[2,136,512]{2,1,0:T(8,128)S(1)} custom-call(s32[16]{0:T(128)S(1)} %compare_select_fusion.7.meta_ref, bf16[2,512,128]{2,1,0:T(8,128)(2,1)S(1)} %pad_maximum_fusion.6.q_ref, s32[2,1,512]{2,1,0:T(1,128)S(1)} %broadcast_in_dim.132.lo_ref, s32[2,1,512]{2,1,0:T(1,128)S(1)} %broadcast_in_dim.135.hi_ref, ...), custom_call_target="tpu_custom_call" | custom-call | flops 268435456 | bytes 2097152 | tf_op jit(solution)/shard_map/attend/pallas_call | solution.py:175
  81.6 4.6 %collective-permute-start.14 = (bf16[1024,128]{1,0:T(8,128)(2,1)S(1)}, bf16[1024,128]{1,0:T(8,128)(2,1)S(1)}, u32[]{:S(2)}, u32[]{:S(2)}) collective-permute-start(bf16[1024,128]{1,0:T(8,128)(2,1)S(1)} %collective-permute-done.12.refs_1_), channel_id=1, source_target_pairs={{0,480},{32,0},{64,32},{96,64},{128,96},{160,128},{192,160},{224,1... | collective-permute-start | bytes 786440 | tf_op jit(solution)/shard_map/ppermute | solution.py:265
  86.9 3.2 %collective-permute-done.11.refs_0_ = bf16[1024,128]{1,0:T(8,128)(2,1)S(1)} collective-permute-done((bf16[1024,128]{1,0:T(8,128)(2,1)S(1)}, bf16[1024,128]{1,0:T(8,128)(2,1)S(1)}, u32[]{:S(2)}, u32[]{:S(2)}) %collective-permute-start.11) | collective-permute-done | bytes 262176 | tf_op jit(solution)/shard_map/ppermute | solution.py:262
  92.0 4.6 %collective-permute-start.16 = (bf16[1024,128]{1,0:T(8,128)(2,1)S(1)}, bf16[1024,128]{1,0:T(8,128)(2,1)S(1)}, u32[]{:S(2)}, u32[]{:S(2)}) collective-permute-start(bf16[1024,128]{1,0:T(8,128)(2,1)S(1)} %collective-permute-done.14.refs_1_), channel_id=1, source_target_pairs={{0,480},{32,0},{64,32},{96,64},{128,96},{160,128},{192,160},{224,1... | collective-permute-start | bytes 786440 | tf_op jit(solution)/shard_map/ppermute | solution.py:265
  97.2 2.3 %collective-permute-done.13.refs_0_ = bf16[1024,128]{1,0:T(8,128)(2,1)S(1)} collective-permute-done((bf16[1024,128]{1,0:T(8,128)(2,1)S(1)}, bf16[1024,128]{1,0:T(8,128)(2,1)S(1)}, u32[]{:S(2)}, u32[]{:S(2)}) %collective-permute-start.13) | collective-permute-done | bytes 262176 | tf_op jit(solution)/shard_map/ppermute | solution.py:262
  101.4 4.6 %collective-permute-start.18 = (bf16[1024,128]{1,0:T(8,128)(2,1)S(1)}, bf16[1024,128]{1,0:T(8,128)(2,1)S(1)}, u32[]{:S(2)}, u32[]{:S(2)}) collective-permute-start(bf16[1024,128]{1,0:T(8,128)(2,1)S(1)} %collective-permute-done.16.refs_1_), channel_id=1, source_target_pairs={{0,480},{32,0},{64,32},{96,64},{128,96},{160,128},{192,160},{224,1... | collective-permute-start | bytes 786440 | tf_op jit(solution)/shard_map/ppermute | solution.py:265
  109.8 4.6 %collective-permute-start.20 = (bf16[1024,128]{1,0:T(8,128)(2,1)S(1)}, bf16[1024,128]{1,0:T(8,128)(2,1)S(1)}, u32[]{:S(2)}, u32[]{:S(2)}) collective-permute-start(bf16[1024,128]{1,0:T(8,128)(2,1)S(1)} %collective-permute-done.18.refs_1_), channel_id=1, source_target_pairs={{0,480},{32,0},{64,32},{96,64},{128,96},{160,128},{192,160},{224,1... | collective-permute-start | bytes 786440 | tf_op jit(solution)/shard_map/ppermute | solution.py:265
  118.1 4.6 %collective-permute-start.22 = (bf16[1024,128]{1,0:T(8,128)(2,1)S(1)}, bf16[1024,128]{1,0:T(8,128)(2,1)S(1)}, u32[]{:S(2)}, u32[]{:S(2)}) collective-permute-start(bf16[1024,128]{1,0:T(8,128)(2,1)S(1)} %collective-permute-done.20.refs_1_), channel_id=1, source_target_pairs={{0,480},{32,0},{64,32},{96,64},{128,96},{160,128},{192,160},{224,1... | collective-permute-start | bytes 786440 | tf_op jit(solution)/shard_map/ppermute | solution.py:265
  126.4 4.6 %collective-permute-start.24 = (bf16[1024,128]{1,0:T(8,128)(2,1)S(1)}, bf16[1024,128]{1,0:T(8,128)(2,1)S(1)}, u32[]{:S(2)}, u32[]{:S(2)}) collective-permute-start(bf16[1024,128]{1,0:T(8,128)(2,1)S(1)} %collective-permute-done.22.refs_1_), channel_id=1, source_target_pairs={{0,480},{32,0},{64,32},{96,64},{128,96},{160,128},{192,160},{224,1... | collective-permute-start | bytes 786440 | tf_op jit(solution)/shard_map/ppermute | solution.py:265
  135.4 6.5 %collective-permute-done.23.refs_0_ = bf16[1024,128]{1,0:T(8,128)(2,1)S(1)} collective-permute-done((bf16[1024,128]{1,0:T(8,128)(2,1)S(1)}, bf16[1024,128]{1,0:T(8,128)(2,1)S(1)}, u32[]{:S(2)}, u32[]{:S(2)}) %collective-permute-start.23) | collective-permute-done | bytes 262176 | tf_op jit(solution)/shard_map/ppermute | solution.py:262
  143.3 9.9 %collective-permute-start.25 = (f32[136,512]{1,0:T(8,128)S(1)}, f32[136,512]{1,0:T(8,128)S(1)}, u32[]{:S(2)}, u32[]{:S(2)}) collective-permute-start(f32[136,512]{1,0:T(8,128)S(1)} %get-tuple-element.56), channel_id=1, source_target_pairs={{0,16},{16,0},{1,17},{17,1},{2,18},{18,2},{3,19},{19,3},{4,20},{20... | collective-permute-start | bytes 835592 | tf_op jit(solution)/shard_map/ppermute | solution.py:272
  (81 shorter events, 47.2 us)
Async XLA Ops:
  2.3 16.4 %collective-permute-start.1 = (bf16[528,256]{1,0:T(8,128)(2,1)}, bf16[528,256]{1,0:T(8,128)(2,1)}, u32[]{:S(2)}, u32[]{:S(2)}) collective-permute-start(bf16[528,256]{1,0:T(8,128)(2,1)} %get-tuple-element.59), channel_id=1, source_target_pairs={{0,3},{1,0},{2,1},{3,2},{4,7},{5,4},{6,5},{7,6},{8,11},{9,8},{10,9... | collective-permute-start | bytes 811016 | tf_op jit(solution)/shard_map/ppermute | solution.py:227
  7.8 10.9 %collective-permute-start.2 = (bf16[528,256]{1,0:T(8,128)(2,1)}, bf16[528,256]{1,0:T(8,128)(2,1)}, u32[]{:S(2)}, u32[]{:S(2)}) collective-permute-start(bf16[528,256]{1,0:T(8,128)(2,1)} %get-tuple-element.59), channel_id=1, source_target_pairs={{0,2},{1,3},{2,0},{3,1},{4,6},{5,7},{6,4},{7,5},{8,10},{9,11},{10,... | collective-permute-start | bytes 811016 | tf_op jit(solution)/shard_map/ppermute | solution.py:227
  10.1 14.1 %collective-permute-start = (bf16[528,256]{1,0:T(8,128)(2,1)}, bf16[528,256]{1,0:T(8,128)(2,1)}, u32[]{:S(2)}, u32[]{:S(2)}) collective-permute-start(bf16[528,256]{1,0:T(8,128)(2,1)} %get-tuple-element.59), channel_id=1, source_target_pairs={{0,1},{1,2},{2,3},{3,0},{4,5},{5,6},{6,7},{7,4},{8,9},{9,10},{10,1... | collective-permute-start | bytes 811016 | tf_op jit(solution)/shard_map/ppermute | solution.py:227
  19.8 16.3 %collective-permute-start.6 = (bf16[2,528,256]{2,1,0:T(8,128)(2,1)S(1)}, bf16[2,528,256]{2,1,0:T(8,128)(2,1)S(1)}, u32[]{:S(2)}, u32[]{:S(2)}) collective-permute-start(bf16[2,528,256]{2,1,0:T(8,128)(2,1)S(1)} %pad_maximum_fusion.2.refs_1_), channel_id=1, source_target_pairs={{0,12},{1,13},{2,14},{3,15},{4,0},{5,1},{6,2},{7,3},{8,4},{9,5},{1... | collective-permute-start | bytes 1622024 | tf_op jit(solution)/shard_map/ppermute | solution.py:229
  25.2 14.2 %collective-permute-start.3 = (bf16[2,528,256]{2,1,0:T(8,128)(2,1)S(1)}, bf16[2,528,256]{2,1,0:T(8,128)(2,1)S(1)}, u32[]{:S(2)}, u32[]{:S(2)}) collective-permute-start(bf16[2,528,256]{2,1,0:T(8,128)(2,1)S(1)} %pad_maximum_fusion.1.refs_0_), channel_id=1, source_target_pairs={{0,4},{1,5},{2,6},{3,7},{4,8},{5,9},{6,10},{7,11},{8,12},{9,13},{1... | collective-permute-start | bytes 1622024 | tf_op jit(solution)/shard_map/ppermute | solution.py:229
  29.5 13.1 %collective-permute-start.4 = (bf16[2,528,256]{2,1,0:T(8,128)(2,1)S(1)}, bf16[2,528,256]{2,1,0:T(8,128)(2,1)S(1)}, u32[]{:S(2)}, u32[]{:S(2)}) collective-permute-start(bf16[2,528,256]{2,1,0:T(8,128)(2,1)S(1)} %pad_maximum_fusion.2.refs_1_), channel_id=1, source_target_pairs={{0,4},{1,5},{2,6},{3,7},{4,8},{5,9},{6,10},{7,11},{8,12},{9,13},{1... | collective-permute-start | bytes 1622024 | tf_op jit(solution)/shard_map/ppermute | solution.py:229
  31.7 11.0 %collective-permute-start.5 = (bf16[2,528,256]{2,1,0:T(8,128)(2,1)S(1)}, bf16[2,528,256]{2,1,0:T(8,128)(2,1)S(1)}, u32[]{:S(2)}, u32[]{:S(2)}) collective-permute-start(bf16[2,528,256]{2,1,0:T(8,128)(2,1)S(1)} %pad_maximum_fusion.1.refs_0_), channel_id=1, source_target_pairs={{0,12},{1,13},{2,14},{3,15},{4,0},{5,1},{6,2},{7,3},{8,4},{9,5},{1... | collective-permute-start | bytes 1622024 | tf_op jit(solution)/shard_map/ppermute | solution.py:229
  36.1 12.1 %collective-permute-start.8 = (bf16[2,528,256]{2,1,0:T(8,128)(2,1)S(1)}, bf16[2,528,256]{2,1,0:T(8,128)(2,1)S(1)}, u32[]{:S(2)}, u32[]{:S(2)}) collective-permute-start(bf16[2,528,256]{2,1,0:T(8,128)(2,1)S(1)} %collective-permute-done.6.refs_5_), channel_id=1, source_target_pairs={{0,12},{1,13},{2,14},{3,15},{4,0},{5,1},{6,2},{7,3},{8,4},{9,5},{1... | collective-permute-start | bytes 1622024 | tf_op jit(solution)/shard_map/ppermute | solution.py:229
  39.4 11.6 %collective-permute-start.7 = (bf16[2,528,256]{2,1,0:T(8,128)(2,1)S(1)}, bf16[2,528,256]{2,1,0:T(8,128)(2,1)S(1)}, u32[]{:S(2)}, u32[]{:S(2)}) collective-permute-start(bf16[2,528,256]{2,1,0:T(8,128)(2,1)S(1)} %collective-permute-done.3.refs_2_), channel_id=1, source_target_pairs={{0,4},{1,5},{2,6},{3,7},{4,8},{5,9},{6,10},{7,11},{8,12},{9,13},{1... | collective-permute-start | bytes 1622024 | tf_op jit(solution)/shard_map/ppermute | solution.py:229
  56.3 18.7 %collective-permute-start.9 = (bf16[512,128]{1,0:T(8,128)(2,1)S(1)}, bf16[512,128]{1,0:T(8,128)(2,1)S(1)}, u32[]{:S(2)}, u32[]{:S(2)}) collective-permute-start(bf16[512,128]{1,0:T(8,128)(2,1)S(1)} %get-tuple-element.23), channel_id=1, source_target_pairs={{0,16},{16,0},{1,17},{17,1},{2,18},{18,2},{3,19},{19,3},{4,20},{20... | collective-permute-start | bytes 393224 | tf_op jit(solution)/shard_map/ppermute | solution.py:258
  61.9 17.8 %collective-permute-start.10 = (bf16[1024,128]{1,0:T(8,128)(2,1)S(1)}, bf16[1024,128]{1,0:T(8,128)(2,1)S(1)}, u32[]{:S(2)}, u32[]{:S(2)}) collective-permute-start(bf16[1024,128]{1,0:T(8,128)(2,1)S(1)} %get-tuple-element.24.refs_0_), channel_id=1, source_target_pairs={{0,32},{32,64},{64,96},{96,128},{128,160},{160,192},{192,224},{224... | collective-permute-start | bytes 786440 | tf_op jit(solution)/shard_map/ppermute | solution.py:262
  65.5 16.1 %collective-permute-start.12 = (bf16[1024,128]{1,0:T(8,128)(2,1)S(1)}, bf16[1024,128]{1,0:T(8,128)(2,1)S(1)}, u32[]{:S(2)}, u32[]{:S(2)}) collective-permute-start(bf16[1024,128]{1,0:T(8,128)(2,1)S(1)} %get-tuple-element.24.refs_0_), channel_id=1, source_target_pairs={{0,480},{32,0},{64,32},{96,64},{128,96},{160,128},{192,160},{224,1... | collective-permute-start | bytes 786440 | tf_op jit(solution)/shard_map/ppermute | solution.py:265
  79.7 10.4 %collective-permute-start.11 = (bf16[1024,128]{1,0:T(8,128)(2,1)S(1)}, bf16[1024,128]{1,0:T(8,128)(2,1)S(1)}, u32[]{:S(2)}, u32[]{:S(2)}) collective-permute-start(bf16[1024,128]{1,0:T(8,128)(2,1)S(1)} %collective-permute-done.10.refs_0_), channel_id=1, source_target_pairs={{0,32},{32,64},{64,96},{96,128},{128,160},{160,192},{192,224},{224... | collective-permute-start | bytes 786440 | tf_op jit(solution)/shard_map/ppermute | solution.py:262
  81.6 10.4 %collective-permute-start.14 = (bf16[1024,128]{1,0:T(8,128)(2,1)S(1)}, bf16[1024,128]{1,0:T(8,128)(2,1)S(1)}, u32[]{:S(2)}, u32[]{:S(2)}) collective-permute-start(bf16[1024,128]{1,0:T(8,128)(2,1)S(1)} %collective-permute-done.12.refs_1_), channel_id=1, source_target_pairs={{0,480},{32,0},{64,32},{96,64},{128,96},{160,128},{192,160},{224,1... | collective-permute-start | bytes 786440 | tf_op jit(solution)/shard_map/ppermute | solution.py:265
  90.1 9.4 %collective-permute-start.13 = (bf16[1024,128]{1,0:T(8,128)(2,1)S(1)}, bf16[1024,128]{1,0:T(8,128)(2,1)S(1)}, u32[]{:S(2)}, u32[]{:S(2)}) collective-permute-start(bf16[1024,128]{1,0:T(8,128)(2,1)S(1)} %collective-permute-done.11.refs_0_), channel_id=1, source_target_pairs={{0,32},{32,64},{64,96},{96,128},{128,160},{160,192},{192,224},{224... | collective-permute-start | bytes 786440 | tf_op jit(solution)/shard_map/ppermute | solution.py:262
  92.0 9.4 %collective-permute-start.16 = (bf16[1024,128]{1,0:T(8,128)(2,1)S(1)}, bf16[1024,128]{1,0:T(8,128)(2,1)S(1)}, u32[]{:S(2)}, u32[]{:S(2)}) collective-permute-start(bf16[1024,128]{1,0:T(8,128)(2,1)S(1)} %collective-permute-done.14.refs_1_), channel_id=1, source_target_pairs={{0,480},{32,0},{64,32},{96,64},{128,96},{160,128},{192,160},{224,1... | collective-permute-start | bytes 786440 | tf_op jit(solution)/shard_map/ppermute | solution.py:265
  99.5 8.3 %collective-permute-start.15 = (bf16[1024,128]{1,0:T(8,128)(2,1)S(1)}, bf16[1024,128]{1,0:T(8,128)(2,1)S(1)}, u32[]{:S(2)}, u32[]{:S(2)}) collective-permute-start(bf16[1024,128]{1,0:T(8,128)(2,1)S(1)} %collective-permute-done.13.refs_0_), channel_id=1, source_target_pairs={{0,32},{32,64},{64,96},{96,128},{128,160},{160,192},{192,224},{224... | collective-permute-start | bytes 786440 | tf_op jit(solution)/shard_map/ppermute | solution.py:262
  101.4 8.3 %collective-permute-start.18 = (bf16[1024,128]{1,0:T(8,128)(2,1)S(1)}, bf16[1024,128]{1,0:T(8,128)(2,1)S(1)}, u32[]{:S(2)}, u32[]{:S(2)}) collective-permute-start(bf16[1024,128]{1,0:T(8,128)(2,1)S(1)} %collective-permute-done.16.refs_1_), channel_id=1, source_target_pairs={{0,480},{32,0},{64,32},{96,64},{128,96},{160,128},{192,160},{224,1... | collective-permute-start | bytes 786440 | tf_op jit(solution)/shard_map/ppermute | solution.py:265
  107.8 8.3 %collective-permute-start.17 = (bf16[1024,128]{1,0:T(8,128)(2,1)S(1)}, bf16[1024,128]{1,0:T(8,128)(2,1)S(1)}, u32[]{:S(2)}, u32[]{:S(2)}) collective-permute-start(bf16[1024,128]{1,0:T(8,128)(2,1)S(1)} %collective-permute-done.15.refs_0_), channel_id=1, source_target_pairs={{0,32},{32,64},{64,96},{96,128},{128,160},{160,192},{192,224},{224... | collective-permute-start | bytes 786440 | tf_op jit(solution)/shard_map/ppermute | solution.py:262
  109.8 8.3 %collective-permute-start.20 = (bf16[1024,128]{1,0:T(8,128)(2,1)S(1)}, bf16[1024,128]{1,0:T(8,128)(2,1)S(1)}, u32[]{:S(2)}, u32[]{:S(2)}) collective-permute-start(bf16[1024,128]{1,0:T(8,128)(2,1)S(1)} %collective-permute-done.18.refs_1_), channel_id=1, source_target_pairs={{0,480},{32,0},{64,32},{96,64},{128,96},{160,128},{192,160},{224,1... | collective-permute-start | bytes 786440 | tf_op jit(solution)/shard_map/ppermute | solution.py:265
  116.1 8.3 %collective-permute-start.19 = (bf16[1024,128]{1,0:T(8,128)(2,1)S(1)}, bf16[1024,128]{1,0:T(8,128)(2,1)S(1)}, u32[]{:S(2)}, u32[]{:S(2)}) collective-permute-start(bf16[1024,128]{1,0:T(8,128)(2,1)S(1)} %collective-permute-done.17.refs_0_), channel_id=1, source_target_pairs={{0,32},{32,64},{64,96},{96,128},{128,160},{160,192},{192,224},{224... | collective-permute-start | bytes 786440 | tf_op jit(solution)/shard_map/ppermute | solution.py:262
  124.5 8.3 %collective-permute-start.21 = (bf16[1024,128]{1,0:T(8,128)(2,1)S(1)}, bf16[1024,128]{1,0:T(8,128)(2,1)S(1)}, u32[]{:S(2)}, u32[]{:S(2)}) collective-permute-start(bf16[1024,128]{1,0:T(8,128)(2,1)S(1)} %collective-permute-done.19.refs_0_), channel_id=1, source_target_pairs={{0,32},{32,64},{64,96},{96,128},{128,160},{160,192},{192,224},{224... | collective-permute-start | bytes 786440 | tf_op jit(solution)/shard_map/ppermute | solution.py:262
  132.8 9.1 %collective-permute-start.23 = (bf16[1024,128]{1,0:T(8,128)(2,1)S(1)}, bf16[1024,128]{1,0:T(8,128)(2,1)S(1)}, u32[]{:S(2)}, u32[]{:S(2)}) collective-permute-start(bf16[1024,128]{1,0:T(8,128)(2,1)S(1)} %collective-permute-done.21.refs_0_), channel_id=1, source_target_pairs={{0,32},{32,64},{64,96},{96,128},{128,160},{160,192},{192,224},{224... | collective-permute-start | bytes 786440 | tf_op jit(solution)/shard_map/ppermute | solution.py:262
  143.3 11.1 %collective-permute-start.25 = (f32[136,512]{1,0:T(8,128)S(1)}, f32[136,512]{1,0:T(8,128)S(1)}, u32[]{:S(2)}, u32[]{:S(2)}) collective-permute-start(f32[136,512]{1,0:T(8,128)S(1)} %get-tuple-element.56), channel_id=1, source_target_pairs={{0,16},{16,0},{1,17},{17,1},{2,18},{18,2},{3,19},{19,3},{4,20},{20... | collective-permute-start | bytes 835592 | tf_op jit(solution)/shard_map/ppermute | solution.py:272
  (7 other events, 52.0 us)

commit v2 on v1

--- a/solution.py
+++ b/solution.py
@@ -94,7 +94,7 @@
     )(blk, *sets, w, cosine, sine)
 
 
-def attend_kernel(offs, fresh, meta_ref, q_ref, lo_ref, hi_ref, *refs):
+def attend_kernel(offs, fresh, last_call, meta_ref, q_ref, lo_ref, hi_ref, *refs):
     n = len(offs)
     kvs, st = refs[:n], refs[-1]
     if fresh:
@@ -102,10 +102,11 @@
         st[...] = jnp.where(row == HD, NEG, 0.0)
     else:
         st[...] = refs[n][...]
-    wide = 256
+    wide = 512
     per = ROWS // wide
+    z, core = meta_ref[8], meta_ref[9]
     firsts = [
-        (lax.rem(meta_ref[8] + (off + NZ), NZ) * 2 + meta_ref[9]) * ROWS for off in offs
+        (lax.rem(z + off + NZ, NZ) * 2 + core) * ROWS for off in offs
     ]
 
     def part(js, masked, i, carry):
@@ -167,17 +168,25 @@
             lax.fori_loop(begin, end, functools.partial(part, [j], True), 0)
 
 
-def attend(meta, q, lo, hi, kvs, offs, state):
+    if last_call:
+        for t in range(2):
+            refs[-3 + t][...] = st[t]
+
+
+def attend(meta, q, lo, hi, kvs, offs, state, last_call=False):
     n = len(kvs)
     vmem = pl.BlockSpec(memory_space=pltpu.VMEM)
     state = [] if state is None else [state]
     pairs = 2 * ROWS * ROWS * n
+    full = (2, HD + 8, ROWS)
+    part = jax.ShapeDtypeStruct(full[1:], jnp.float32)
     return pl.pallas_call(
-        functools.partial(attend_kernel, offs, not state),
-        out_shape=jax.ShapeDtypeStruct((2, HD + 8, ROWS), jnp.float32),
+        functools.partial(attend_kernel, offs, not state, last_call),
+        out_shape=(part, part) if last_call else jax.ShapeDtypeStruct(full, jnp.float32),
         in_specs=[pl.BlockSpec(memory_space=pltpu.SMEM)] + [vmem] * (3 + n + len(state)),
-        out_specs=vmem,
-        input_output_aliases={4 + n: 0} if state else {},
+        out_specs=(vmem, vmem) if last_call else vmem,
+        scratch_shapes=[pltpu.VMEM(full, jnp.float32)] if last_call else [],
+        input_output_aliases={4 + n: 0} if state and not last_call else {},
         compiler_params=pltpu.CompilerParams(vmem_limit_bytes=40 * 2**20),
         cost_estimate=pl.CostEstimate(
             flops=4 * pairs * HD, bytes_accessed=2 * 2**20, transcendentals=pairs
@@ -254,23 +263,23 @@
     w = jnp.concatenate([w_qkv[0], w_qkv[1], w_qkv[2]], axis=1)
     q, kv = project(blk, sets, w, cosine, sine)
 
-    up = down = kv
+    half = NZ // 2
+    z_step = lambda v, d: lax.ppermute(v, "z", ring(NZ, d))
+    put = lambda kvs, offs, state, **kw: attend(meta, q2, lo, hi, kvs, offs, state, **kw)
+    up, down = z_step(kv, 1), z_step(kv, -1)
+    up, q = lax.optimization_barrier((up, q))
     q2 = jnp.stack([q, lax.ppermute(q, "core", ring(2, 1))], axis=0)
-    state = None
-    arrived, sources = [kv], [0]
-    for i in range(1, NZ // 2 + 1):
-        up = lax.ppermute(up, "z", ring(NZ, 1))
-        new, src = [up], [-i]
-        if i < NZ // 2:
-            down = lax.ppermute(down, "z", ring(NZ, -1))
-            new, src = new + [down], src + [i]
-        state = attend(meta, q2, lo, hi, arrived, sources, state)
+    state, waiting = None, [([kv], [0])]
+    for i in range(2, half + 1):
+        waiting.append(([up, down], [1 - i, i - 1]))
+        up = z_step(up, 1)
+        if i < half:
+            down = z_step(down, -1)
+        for _ in range(1 if i < half else 2):
+            state = put(*waiting.pop(0), state)
         up, state = lax.optimization_barrier((up, state))
-        new[0] = up
-        arrived, sources = new, src
-    state = attend(meta, q2, lo, hi, arrived, sources, state)
-    other = lax.ppermute(state[1], "core", ring(2, 1))
-    return merge(state[0], other)
+    own, other = put([up], [-half], state, last_call=True)
+    return merge(own, lax.ppermute(other, "core", ring(2, 1)))
 
 
 def solution(mesh):

time: 158 us -> 151 us (0.956)
  other arithmetic: 10.4 us -> 4.76 us
    another operation x3, other arithmetic: 3.78 us -> 1.09 us  [body(): a, b = (jnp.stack([mine, side[1]]), jnp.stack([side[-1], side[2]]))]
  transfers between devices with their start and end apart: 26 -> 26, of which waited for: 12 -> 12; matrix products, arithmetic and copies ran while one was open for 7% -> 4% of each run, Pallas kernels for 5% -> 5%
where the time goes in v2:
time: 151 us; the launch traced here: 150 us
  starting transfers between devices  97.8 us (65%)
  waiting for transfers between devices  27.1 us (18%)
  Pallas kernels  15.1 us (10%)
  other arithmetic  4.76 us (3%)
  local copies, waits for them, and re-layouts  4.2 us (3%)
    ppermute x15, starting transfers between devices, body(): z_step = lambda v, d: lax.ppermute(v, 'z', ring(NZ, d))  53.8 us
    ppermute x6, starting transfers between devices, body(): far = lambda v, d: lax.ppermute(v, plane, plane_perm(d, False))  18.1 us
    ppermute x15, waiting for transfers between devices, body(): z_step = lambda v, d: lax.ppermute(v, 'z', ring(NZ, d))  16.8 us
    ppermute x3, starting transfers between devices, body(): lax.ppermute(mine, plane, plane_perm(d, True))  10.3 us
    ppermute x6, waiting for transfers between devices, body(): far = lambda v, d: lax.ppermute(v, plane, plane_perm(d, False))  9.18 us
    ppermute x1, starting transfers between devices, body(): return merge(own, lax.ppermute(other, 'core', ring(2, 1)))  9.1 us
    pallas_call x9, Pallas kernels, attend(): pl.pallas_call(functools.partial(attend_kernel, offs, not state, last_cal...  8.05 us
    ppermute x1, starting transfers between devices, body(): q2 = jnp.stack([q, lax.ppermute(q, 'core', ring(2, 1))], axis=0)  6.46 us
  transfers between devices with their start and end apart: 26, of which 12 were waited for; matrix products, arithmetic and copies ran while one was open for 4% of the time, Pallas kernels for 5%

profile of v2, /device:TPU:1, one launch (start us, length us, event | category | flops | bytes accessed | tf_op | source)
XLA Modules:
  0.0 149.7 jit_solution(7936771887785899610)
XLA Ops:
  1.6 5.5 %collective-permute-start.1 = (bf16[528,256]{1,0:T(8,128)(2,1)S(1)}, bf16[528,256]{1,0:T(8,128)(2,1)S(1)}, u32[]{:S(2)}, u32[]{:S(2)}) collective-permute-start(bf16[528,256]{1,0:T(8,128)(2,1)S(1)} %get-tuple-element.61), channel_id=1, source_target_pairs={{0,3},{1,0},{2,1},{3,2},{4,7},{5,4},{6,5},{7,6},{8,11},{9,8},{10,9... | collective-permute-start | bytes 811016 | tf_op jit(solution)/shard_map/ppermute | solution.py:236
  7.1 2.3 %collective-permute-start.2 = (bf16[528,256]{1,0:T(8,128)(2,1)S(1)}, bf16[528,256]{1,0:T(8,128)(2,1)S(1)}, u32[]{:S(2)}, u32[]{:S(2)}) collective-permute-start(bf16[528,256]{1,0:T(8,128)(2,1)S(1)} %get-tuple-element.61), channel_id=1, source_target_pairs={{0,2},{1,3},{2,0},{3,1},{4,6},{5,7},{6,4},{7,5},{8,10},{9,11},{10,... | collective-permute-start | bytes 811016 | tf_op jit(solution)/shard_map/ppermute | solution.py:236
  9.4 2.6 %collective-permute-start = (bf16[528,256]{1,0:T(8,128)(2,1)S(1)}, bf16[528,256]{1,0:T(8,128)(2,1)S(1)}, u32[]{:S(2)}, u32[]{:S(2)}) collective-permute-start(bf16[528,256]{1,0:T(8,128)(2,1)S(1)} %get-tuple-element.61), channel_id=1, source_target_pairs={{0,1},{1,2},{2,3},{3,0},{4,5},{5,6},{6,7},{7,4},{8,9},{9,10},{10,1... | collective-permute-start | bytes 811016 | tf_op jit(solution)/shard_map/ppermute | solution.py:236
  13.6 2.1 %slice_bitcast_fusion.2 = (bf16[4096,128]{1,0:T(8,128)(2,1)S(1)}, bf16[4096,128]{1,0:T(8,128)(2,1)S(1)}, bf16[4096,128]{1,0:T(8,128)(2,1)S(1)}) fusion(bf16[3,4096,128]{2,1,0:T(8,128)(2,1)} %param.10), kind=kLoop, calls=%fused_computation.3 | loop fusion | bytes 6291456 | tf_op jit(solution)/shard_map/squeeze | solution.py:263
  17.3 4.4 %collective-permute-start.6 = (bf16[2,528,256]{2,1,0:T(8,128)(2,1)S(1)}, bf16[2,528,256]{2,1,0:T(8,128)(2,1)S(1)}, u32[]{:S(2)}, u32[]{:S(2)}) collective-permute-start(bf16[2,528,256]{2,1,0:T(8,128)(2,1)S(1)} %pad_maximum_fusion.2.refs_1_), channel_id=1, source_target_pairs={{0,12},{1,13},{2,14},{3,15},{4,0},{5,1},{6,2},{7,3},{8,4},{9,5},{1... | collective-permute-start | bytes 1622024 | tf_op jit(solution)/shard_map/ppermute | solution.py:238
  23.8 2.1 %collective-permute-start.4 = (bf16[2,528,256]{2,1,0:T(8,128)(2,1)S(1)}, bf16[2,528,256]{2,1,0:T(8,128)(2,1)S(1)}, u32[]{:S(2)}, u32[]{:S(2)}) collective-permute-start(bf16[2,528,256]{2,1,0:T(8,128)(2,1)S(1)} %pad_maximum_fusion.2.refs_1_), channel_id=1, source_target_pairs={{0,4},{1,5},{2,6},{3,7},{4,8},{5,9},{6,10},{7,11},{8,12},{9,13},{1... | collective-permute-start | bytes 1622024 | tf_op jit(solution)/shard_map/ppermute | solution.py:238
  25.9 4.4 %collective-permute-start.5 = (bf16[2,528,256]{2,1,0:T(8,128)(2,1)S(1)}, bf16[2,528,256]{2,1,0:T(8,128)(2,1)S(1)}, u32[]{:S(2)}, u32[]{:S(2)}) collective-permute-start(bf16[2,528,256]{2,1,0:T(8,128)(2,1)S(1)} %pad_maximum_fusion.1.refs_0_), channel_id=1, source_target_pairs={{0,12},{1,13},{2,14},{3,15},{4,0},{5,1},{6,2},{7,3},{8,4},{9,5},{1... | collective-permute-start | bytes 1622024 | tf_op jit(solution)/shard_map/ppermute | solution.py:238
  30.3 3.4 %collective-permute-start.8 = (bf16[2,528,256]{2,1,0:T(8,128)(2,1)S(1)}, bf16[2,528,256]{2,1,0:T(8,128)(2,1)S(1)}, u32[]{:S(2)}, u32[]{:S(2)}) collective-permute-start(bf16[2,528,256]{2,1,0:T(8,128)(2,1)S(1)} %collective-permute-done.6.refs_5_), channel_id=1, source_target_pairs={{0,12},{1,13},{2,14},{3,15},{4,0},{5,1},{6,2},{7,3},{8,4},{9,5},{1... | collective-permute-start | bytes 1622024 | tf_op jit(solution)/shard_map/ppermute | solution.py:238
  36.1 3.1 %collective-permute-done.4.refs_3_ = bf16[2,528,256]{2,1,0:T(8,128)(2,1)S(1)} collective-permute-done((bf16[2,528,256]{2,1,0:T(8,128)(2,1)S(1)}, bf16[2,528,256]{2,1,0:T(8,128)(2,1)S(1)}, u32[]{:S(2)}, u32[]{:S(2)}) %collective-permute-start.4) | collective-permute-done | bytes 540704 | tf_op jit(solution)/shard_map/ppermute | solution.py:238
  39.2 3.2 %collective-permute-done.8.refs_7_ = bf16[2,528,256]{2,1,0:T(8,128)(2,1)S(1)} collective-permute-done((bf16[2,528,256]{2,1,0:T(8,128)(2,1)S(1)}, bf16[2,528,256]{2,1,0:T(8,128)(2,1)S(1)}, u32[]{:S(2)}, u32[]{:S(2)}) %collective-permute-start.8) | collective-permute-done | bytes 540704 | tf_op jit(solution)/shard_map/ppermute | solution.py:238
  42.4 2.9 %collective-permute-done.7.refs_6_ = bf16[2,528,256]{2,1,0:T(8,128)(2,1)S(1)} collective-permute-done((bf16[2,528,256]{2,1,0:T(8,128)(2,1)S(1)}, bf16[2,528,256]{2,1,0:T(8,128)(2,1)S(1)}, u32[]{:S(2)}, u32[]{:S(2)}) %collective-permute-start.7) | collective-permute-done | bytes 540704 | tf_op jit(solution)/shard_map/ppermute | solution.py:238
  45.3 5.3 %norm_qkv.1 = (bf16[512,128]{1,0:T(8,128)(2,1)S(1)}, bf16[1024,128]{1,0:T(8,128)(2,1)S(1)}) custom-call(s32[16]{0:T(128)S(1)} %fusion.1.blk_ref, bf16[2,528,256]{2,1,0:T(8,128)(2,1)S(1)} %pad_maximum_fusion.1.refs_0_, bf16[2,528,256]{2,1,0:T(8,128)(2,1)S(1)} %pad_maximum_fusion.2.refs_1_, bf16[2,528,256]{2,1,0:T(8,128)(2,1)S(1)} %collective-permute-done.3.refs_2_, ...), custom_call_target="tpu_custom_call" | custom-call | flops 1610612736 | bytes 8388608 | tf_op jit(solution)/shard_map/norm_qkv/pallas_call | solution.py:80
  50.5 3.5 %collective-permute-start.9 = (bf16[1024,128]{1,0:T(8,128)(2,1)S(1)}, bf16[1024,128]{1,0:T(8,128)(2,1)S(1)}, u32[]{:S(2)}, u32[]{:S(2)}) collective-permute-start(bf16[1024,128]{1,0:T(8,128)(2,1)S(1)} %get-tuple-element.25.refs_0_), channel_id=1, source_target_pairs={{0,32},{32,64},{64,96},{96,128},{128,160},{160,192},{192,224},{224... | collective-permute-start | bytes 786440 | tf_op jit(solution)/shard_map/ppermute | solution.py:267
  54.2 9.5 %collective-permute-start.13 = (bf16[1024,128]{1,0:T(8,128)(2,1)S(1)}, bf16[1024,128]{1,0:T(8,128)(2,1)S(1)}, u32[]{:S(2)}, u32[]{:S(2)}) collective-permute-start(bf16[1024,128]{1,0:T(8,128)(2,1)S(1)} %get-tuple-element.25.refs_0_), channel_id=1, source_target_pairs={{0,480},{32,0},{64,32},{96,64},{128,96},{160,128},{192,160},{224,1... | collective-permute-start | bytes 786440 | tf_op jit(solution)/shard_map/ppermute | solution.py:267
  65.4 6.5 %collective-permute-start.10 = (bf16[512,128]{1,0:T(8,128)(2,1)S(1)}, bf16[512,128]{1,0:T(8,128)(2,1)S(1)}, u32[]{:S(2)}, u32[]{:S(2)}) collective-permute-start(bf16[512,128]{1,0:T(8,128)(2,1)S(1)} %get-tuple-element.27), channel_id=1, source_target_pairs={{0,16},{16,0},{1,17},{17,1},{2,18},{18,2},{3,19},{19,3},{4,20},{20... | collective-permute-start | bytes 393224 | tf_op jit(solution)/shard_map/ppermute | solution.py:271
  73.8 4.6 %collective-permute-start.15 = (bf16[1024,128]{1,0:T(8,128)(2,1)S(1)}, bf16[1024,128]{1,0:T(8,128)(2,1)S(1)}, u32[]{:S(2)}, u32[]{:S(2)}) collective-permute-start(bf16[1024,128]{1,0:T(8,128)(2,1)S(1)} %collective-permute-done.13.refs_1_), channel_id=1, source_target_pairs={{0,480},{32,0},{64,32},{96,64},{128,96},{160,128},{192,160},{224,1... | collective-permute-start | bytes 786440 | tf_op jit(solution)/shard_map/ppermute | solution.py:267
  80.0 2.9 %collective-permute-done.11.refs_0_ = bf16[1024,128]{1,0:T(8,128)(2,1)S(1)} collective-permute-done((bf16[1024,128]{1,0:T(8,128)(2,1)S(1)}, bf16[1024,128]{1,0:T(8,128)(2,1)S(1)}, u32[]{:S(2)}, u32[]{:S(2)}) %collective-permute-start.11) | collective-permute-done | bytes 262176 | tf_op jit(solution)/shard_map/ppermute | solution.py:267
  84.8 4.6 %collective-permute-start.17 = (bf16[1024,128]{1,0:T(8,128)(2,1)S(1)}, bf16[1024,128]{1,0:T(8,128)(2,1)S(1)}, u32[]{:S(2)}, u32[]{:S(2)}) collective-permute-start(bf16[1024,128]{1,0:T(8,128)(2,1)S(1)} %collective-permute-done.15.refs_1_), channel_id=1, source_target_pairs={{0,480},{32,0},{64,32},{96,64},{128,96},{160,128},{192,160},{224,1... | collective-permute-start | bytes 786440 | tf_op jit(solution)/shard_map/ppermute | solution.py:267
  95.0 4.6 %collective-permute-start.19 = (bf16[1024,128]{1,0:T(8,128)(2,1)S(1)}, bf16[1024,128]{1,0:T(8,128)(2,1)S(1)}, u32[]{:S(2)}, u32[]{:S(2)}) collective-permute-start(bf16[1024,128]{1,0:T(8,128)(2,1)S(1)} %collective-permute-done.17.refs_1_), channel_id=1, source_target_pairs={{0,480},{32,0},{64,32},{96,64},{128,96},{160,128},{192,160},{224,1... | collective-permute-start | bytes 786440 | tf_op jit(solution)/shard_map/ppermute | solution.py:267
  104.2 4.6 %collective-permute-start.21 = (bf16[1024,128]{1,0:T(8,128)(2,1)S(1)}, bf16[1024,128]{1,0:T(8,128)(2,1)S(1)}, u32[]{:S(2)}, u32[]{:S(2)}) collective-permute-start(bf16[1024,128]{1,0:T(8,128)(2,1)S(1)} %collective-permute-done.19.refs_1_), channel_id=1, source_target_pairs={{0,480},{32,0},{64,32},{96,64},{128,96},{160,128},{192,160},{224,1... | collective-permute-start | bytes 786440 | tf_op jit(solution)/shard_map/ppermute | solution.py:267
  112.5 4.6 %collective-permute-start.23 = (bf16[1024,128]{1,0:T(8,128)(2,1)S(1)}, bf16[1024,128]{1,0:T(8,128)(2,1)S(1)}, u32[]{:S(2)}, u32[]{:S(2)}) collective-permute-start(bf16[1024,128]{1,0:T(8,128)(2,1)S(1)} %collective-permute-done.21.refs_1_), channel_id=1, source_target_pairs={{0,480},{32,0},{64,32},{96,64},{128,96},{160,128},{192,160},{224,1... | collective-permute-start | bytes 786440 | tf_op jit(solution)/shard_map/ppermute | solution.py:267
  120.8 4.6 %collective-permute-start.24 = (bf16[1024,128]{1,0:T(8,128)(2,1)S(1)}, bf16[1024,128]{1,0:T(8,128)(2,1)S(1)}, u32[]{:S(2)}, u32[]{:S(2)}) collective-permute-start(bf16[1024,128]{1,0:T(8,128)(2,1)S(1)} %collective-permute-done.23.refs_1_), channel_id=1, source_target_pairs={{0,480},{32,0},{64,32},{96,64},{128,96},{160,128},{192,160},{224,1... | collective-permute-start | bytes 786440 | tf_op jit(solution)/shard_map/ppermute | solution.py:267
  130.7 4.9 %collective-permute-done.22.refs_0_ = bf16[1024,128]{1,0:T(8,128)(2,1)S(1)} collective-permute-done((bf16[1024,128]{1,0:T(8,128)(2,1)S(1)}, bf16[1024,128]{1,0:T(8,128)(2,1)S(1)}, u32[]{:S(2)}, u32[]{:S(2)}) %collective-permute-start.22) | collective-permute-done | bytes 262176 | tf_op jit(solution)/shard_map/ppermute | solution.py:267
  136.9 9.1 %collective-permute-start.25 = (f32[136,512]{1,0:T(8,128)S(1)}, f32[136,512]{1,0:T(8,128)S(1)}, u32[]{:S(2)}, u32[]{:S(2)}) collective-permute-start(f32[136,512]{1,0:T(8,128)S(1)} %get-tuple-element.44), channel_id=1, source_target_pairs={{0,16},{16,0},{1,17},{17,1},{2,18},{18,2},{3,19},{19,3},{4,20},{20... | collective-permute-start | bytes 835592 | tf_op jit(solution)/shard_map/ppermute | solution.py:282
  (82 shorter events, 44.2 us)
Async XLA Ops:
  1.6 15.6 %collective-permute-start.1 = (bf16[528,256]{1,0:T(8,128)(2,1)S(1)}, bf16[528,256]{1,0:T(8,128)(2,1)S(1)}, u32[]{:S(2)}, u32[]{:S(2)}) collective-permute-start(bf16[528,256]{1,0:T(8,128)(2,1)S(1)} %get-tuple-element.61), channel_id=1, source_target_pairs={{0,3},{1,0},{2,1},{3,2},{4,7},{5,4},{6,5},{7,6},{8,11},{9,8},{10,9... | collective-permute-start | bytes 811016 | tf_op jit(solution)/shard_map/ppermute | solution.py:236
  7.1 10.1 %collective-permute-start.2 = (bf16[528,256]{1,0:T(8,128)(2,1)S(1)}, bf16[528,256]{1,0:T(8,128)(2,1)S(1)}, u32[]{:S(2)}, u32[]{:S(2)}) collective-permute-start(bf16[528,256]{1,0:T(8,128)(2,1)S(1)} %get-tuple-element.61), channel_id=1, source_target_pairs={{0,2},{1,3},{2,0},{3,1},{4,6},{5,7},{6,4},{7,5},{8,10},{9,11},{10,... | collective-permute-start | bytes 811016 | tf_op jit(solution)/shard_map/ppermute | solution.py:236
  9.4 12.3 %collective-permute-start = (bf16[528,256]{1,0:T(8,128)(2,1)S(1)}, bf16[528,256]{1,0:T(8,128)(2,1)S(1)}, u32[]{:S(2)}, u32[]{:S(2)}) collective-permute-start(bf16[528,256]{1,0:T(8,128)(2,1)S(1)} %get-tuple-element.61), channel_id=1, source_target_pairs={{0,1},{1,2},{2,3},{3,0},{4,5},{5,6},{6,7},{7,4},{8,9},{9,10},{10,1... | collective-permute-start | bytes 811016 | tf_op jit(solution)/shard_map/ppermute | solution.py:236
  17.3 13.0 %collective-permute-start.6 = (bf16[2,528,256]{2,1,0:T(8,128)(2,1)S(1)}, bf16[2,528,256]{2,1,0:T(8,128)(2,1)S(1)}, u32[]{:S(2)}, u32[]{:S(2)}) collective-permute-start(bf16[2,528,256]{2,1,0:T(8,128)(2,1)S(1)} %pad_maximum_fusion.2.refs_1_), channel_id=1, source_target_pairs={{0,12},{1,13},{2,14},{3,15},{4,0},{5,1},{6,2},{7,3},{8,4},{9,5},{1... | collective-permute-start | bytes 1622024 | tf_op jit(solution)/shard_map/ppermute | solution.py:238
  21.8 11.9 %collective-permute-start.3 = (bf16[2,528,256]{2,1,0:T(8,128)(2,1)S(1)}, bf16[2,528,256]{2,1,0:T(8,128)(2,1)S(1)}, u32[]{:S(2)}, u32[]{:S(2)}) collective-permute-start(bf16[2,528,256]{2,1,0:T(8,128)(2,1)S(1)} %pad_maximum_fusion.1.refs_0_), channel_id=1, source_target_pairs={{0,4},{1,5},{2,6},{3,7},{4,8},{5,9},{6,10},{7,11},{8,12},{9,13},{1... | collective-permute-start | bytes 1622024 | tf_op jit(solution)/shard_map/ppermute | solution.py:238
  23.8 15.4 %collective-permute-start.4 = (bf16[2,528,256]{2,1,0:T(8,128)(2,1)S(1)}, bf16[2,528,256]{2,1,0:T(8,128)(2,1)S(1)}, u32[]{:S(2)}, u32[]{:S(2)}) collective-permute-start(bf16[2,528,256]{2,1,0:T(8,128)(2,1)S(1)} %pad_maximum_fusion.2.refs_1_), channel_id=1, source_target_pairs={{0,4},{1,5},{2,6},{3,7},{4,8},{5,9},{6,10},{7,11},{8,12},{9,13},{1... | collective-permute-start | bytes 1622024 | tf_op jit(solution)/shard_map/ppermute | solution.py:238
  25.9 13.3 %collective-permute-start.5 = (bf16[2,528,256]{2,1,0:T(8,128)(2,1)S(1)}, bf16[2,528,256]{2,1,0:T(8,128)(2,1)S(1)}, u32[]{:S(2)}, u32[]{:S(2)}) collective-permute-start(bf16[2,528,256]{2,1,0:T(8,128)(2,1)S(1)} %pad_maximum_fusion.1.refs_0_), channel_id=1, source_target_pairs={{0,12},{1,13},{2,14},{3,15},{4,0},{5,1},{6,2},{7,3},{8,4},{9,5},{1... | collective-permute-start | bytes 1622024 | tf_op jit(solution)/shard_map/ppermute | solution.py:238
  30.3 12.1 %collective-permute-start.8 = (bf16[2,528,256]{2,1,0:T(8,128)(2,1)S(1)}, bf16[2,528,256]{2,1,0:T(8,128)(2,1)S(1)}, u32[]{:S(2)}, u32[]{:S(2)}) collective-permute-start(bf16[2,528,256]{2,1,0:T(8,128)(2,1)S(1)} %collective-permute-done.6.refs_5_), channel_id=1, source_target_pairs={{0,12},{1,13},{2,14},{3,15},{4,0},{5,1},{6,2},{7,3},{8,4},{9,5},{1... | collective-permute-start | bytes 1622024 | tf_op jit(solution)/shard_map/ppermute | solution.py:238
  33.7 11.6 %collective-permute-start.7 = (bf16[2,528,256]{2,1,0:T(8,128)(2,1)S(1)}, bf16[2,528,256]{2,1,0:T(8,128)(2,1)S(1)}, u32[]{:S(2)}, u32[]{:S(2)}) collective-permute-start(bf16[2,528,256]{2,1,0:T(8,128)(2,1)S(1)} %collective-permute-done.3.refs_2_), channel_id=1, source_target_pairs={{0,4},{1,5},{2,6},{3,7},{4,8},{5,9},{6,10},{7,11},{8,12},{9,13},{1... | collective-permute-start | bytes 1622024 | tf_op jit(solution)/shard_map/ppermute | solution.py:238
  50.5 14.9 %collective-permute-start.9 = (bf16[1024,128]{1,0:T(8,128)(2,1)S(1)}, bf16[1024,128]{1,0:T(8,128)(2,1)S(1)}, u32[]{:S(2)}, u32[]{:S(2)}) collective-permute-start(bf16[1024,128]{1,0:T(8,128)(2,1)S(1)} %get-tuple-element.25.refs_0_), channel_id=1, source_target_pairs={{0,32},{32,64},{64,96},{96,128},{128,160},{160,192},{192,224},{224... | collective-permute-start | bytes 786440 | tf_op jit(solution)/shard_map/ppermute | solution.py:267
  54.2 19.6 %collective-permute-start.13 = (bf16[1024,128]{1,0:T(8,128)(2,1)S(1)}, bf16[1024,128]{1,0:T(8,128)(2,1)S(1)}, u32[]{:S(2)}, u32[]{:S(2)}) collective-permute-start(bf16[1024,128]{1,0:T(8,128)(2,1)S(1)} %get-tuple-element.25.refs_0_), channel_id=1, source_target_pairs={{0,480},{32,0},{64,32},{96,64},{128,96},{160,128},{192,160},{224,1... | collective-permute-start | bytes 786440 | tf_op jit(solution)/shard_map/ppermute | solution.py:267
  65.4 13.0 %collective-permute-start.10 = (bf16[512,128]{1,0:T(8,128)(2,1)S(1)}, bf16[512,128]{1,0:T(8,128)(2,1)S(1)}, u32[]{:S(2)}, u32[]{:S(2)}) collective-permute-start(bf16[512,128]{1,0:T(8,128)(2,1)S(1)} %get-tuple-element.27), channel_id=1, source_target_pairs={{0,16},{16,0},{1,17},{17,1},{2,18},{18,2},{3,19},{19,3},{4,20},{20... | collective-permute-start | bytes 393224 | tf_op jit(solution)/shard_map/ppermute | solution.py:271
  71.9 11.0 %collective-permute-start.11 = (bf16[1024,128]{1,0:T(8,128)(2,1)S(1)}, bf16[1024,128]{1,0:T(8,128)(2,1)S(1)}, u32[]{:S(2)}, u32[]{:S(2)}) collective-permute-start(bf16[1024,128]{1,0:T(8,128)(2,1)S(1)} %collective-permute-done.9.refs_0_), channel_id=1, source_target_pairs={{0,32},{32,64},{64,96},{96,128},{128,160},{160,192},{192,224},{224... | collective-permute-start | bytes 786440 | tf_op jit(solution)/shard_map/ppermute | solution.py:267
  73.8 11.0 %collective-permute-start.15 = (bf16[1024,128]{1,0:T(8,128)(2,1)S(1)}, bf16[1024,128]{1,0:T(8,128)(2,1)S(1)}, u32[]{:S(2)}, u32[]{:S(2)}) collective-permute-start(bf16[1024,128]{1,0:T(8,128)(2,1)S(1)} %collective-permute-done.13.refs_1_), channel_id=1, source_target_pairs={{0,480},{32,0},{64,32},{96,64},{128,96},{160,128},{192,160},{224,1... | collective-permute-start | bytes 786440 | tf_op jit(solution)/shard_map/ppermute | solution.py:267
  82.9 10.1 %collective-permute-start.12 = (bf16[1024,128]{1,0:T(8,128)(2,1)S(1)}, bf16[1024,128]{1,0:T(8,128)(2,1)S(1)}, u32[]{:S(2)}, u32[]{:S(2)}) collective-permute-start(bf16[1024,128]{1,0:T(8,128)(2,1)S(1)} %collective-permute-done.11.refs_0_), channel_id=1, source_target_pairs={{0,32},{32,64},{64,96},{96,128},{128,160},{160,192},{192,224},{224... | collective-permute-start | bytes 786440 | tf_op jit(solution)/shard_map/ppermute | solution.py:267
  84.8 10.1 %collective-permute-start.17 = (bf16[1024,128]{1,0:T(8,128)(2,1)S(1)}, bf16[1024,128]{1,0:T(8,128)(2,1)S(1)}, u32[]{:S(2)}, u32[]{:S(2)}) collective-permute-start(bf16[1024,128]{1,0:T(8,128)(2,1)S(1)} %collective-permute-done.15.refs_1_), channel_id=1, source_target_pairs={{0,480},{32,0},{64,32},{96,64},{128,96},{160,128},{192,160},{224,1... | collective-permute-start | bytes 786440 | tf_op jit(solution)/shard_map/ppermute | solution.py:267
  93.0 9.2 %collective-permute-start.14 = (bf16[1024,128]{1,0:T(8,128)(2,1)S(1)}, bf16[1024,128]{1,0:T(8,128)(2,1)S(1)}, u32[]{:S(2)}, u32[]{:S(2)}) collective-permute-start(bf16[1024,128]{1,0:T(8,128)(2,1)S(1)} %collective-permute-done.12.refs_0_), channel_id=1, source_target_pairs={{0,32},{32,64},{64,96},{96,128},{128,160},{160,192},{192,224},{224... | collective-permute-start | bytes 786440 | tf_op jit(solution)/shard_map/ppermute | solution.py:267
  95.0 9.2 %collective-permute-start.19 = (bf16[1024,128]{1,0:T(8,128)(2,1)S(1)}, bf16[1024,128]{1,0:T(8,128)(2,1)S(1)}, u32[]{:S(2)}, u32[]{:S(2)}) collective-permute-start(bf16[1024,128]{1,0:T(8,128)(2,1)S(1)} %collective-permute-done.17.refs_1_), channel_id=1, source_target_pairs={{0,480},{32,0},{64,32},{96,64},{128,96},{160,128},{192,160},{224,1... | collective-permute-start | bytes 786440 | tf_op jit(solution)/shard_map/ppermute | solution.py:267
  102.3 8.3 %collective-permute-start.16 = (bf16[1024,128]{1,0:T(8,128)(2,1)S(1)}, bf16[1024,128]{1,0:T(8,128)(2,1)S(1)}, u32[]{:S(2)}, u32[]{:S(2)}) collective-permute-start(bf16[1024,128]{1,0:T(8,128)(2,1)S(1)} %collective-permute-done.14.refs_0_), channel_id=1, source_target_pairs={{0,32},{32,64},{64,96},{96,128},{128,160},{160,192},{192,224},{224... | collective-permute-start | bytes 786440 | tf_op jit(solution)/shard_map/ppermute | solution.py:267
  110.6 8.3 %collective-permute-start.18 = (bf16[1024,128]{1,0:T(8,128)(2,1)S(1)}, bf16[1024,128]{1,0:T(8,128)(2,1)S(1)}, u32[]{:S(2)}, u32[]{:S(2)}) collective-permute-start(bf16[1024,128]{1,0:T(8,128)(2,1)S(1)} %collective-permute-done.16.refs_0_), channel_id=1, source_target_pairs={{0,32},{32,64},{64,96},{96,128},{128,160},{160,192},{192,224},{224... | collective-permute-start | bytes 786440 | tf_op jit(solution)/shard_map/ppermute | solution.py:267
  118.9 8.3 %collective-permute-start.20 = (bf16[1024,128]{1,0:T(8,128)(2,1)S(1)}, bf16[1024,128]{1,0:T(8,128)(2,1)S(1)}, u32[]{:S(2)}, u32[]{:S(2)}) collective-permute-start(bf16[1024,128]{1,0:T(8,128)(2,1)S(1)} %collective-permute-done.18.refs_0_), channel_id=1, source_target_pairs={{0,32},{32,64},{64,96},{96,128},{128,160},{160,192},{192,224},{224... | collective-permute-start | bytes 786440 | tf_op jit(solution)/shard_map/ppermute | solution.py:267
  120.8 9.0 %collective-permute-start.24 = (bf16[1024,128]{1,0:T(8,128)(2,1)S(1)}, bf16[1024,128]{1,0:T(8,128)(2,1)S(1)}, u32[]{:S(2)}, u32[]{:S(2)}) collective-permute-start(bf16[1024,128]{1,0:T(8,128)(2,1)S(1)} %collective-permute-done.23.refs_1_), channel_id=1, source_target_pairs={{0,480},{32,0},{64,32},{96,64},{128,96},{160,128},{192,160},{224,1... | collective-permute-start | bytes 786440 | tf_op jit(solution)/shard_map/ppermute | solution.py:267
  127.2 8.3 %collective-permute-start.22 = (bf16[1024,128]{1,0:T(8,128)(2,1)S(1)}, bf16[1024,128]{1,0:T(8,128)(2,1)S(1)}, u32[]{:S(2)}, u32[]{:S(2)}) collective-permute-start(bf16[1024,128]{1,0:T(8,128)(2,1)S(1)} %collective-permute-done.20.refs_0_), channel_id=1, source_target_pairs={{0,32},{32,64},{64,96},{96,128},{128,160},{160,192},{192,224},{224... | collective-permute-start | bytes 786440 | tf_op jit(solution)/shard_map/ppermute | solution.py:267
  136.9 10.3 %collective-permute-start.25 = (f32[136,512]{1,0:T(8,128)S(1)}, f32[136,512]{1,0:T(8,128)S(1)}, u32[]{:S(2)}, u32[]{:S(2)}) collective-permute-start(f32[136,512]{1,0:T(8,128)S(1)} %get-tuple-element.44), channel_id=1, source_target_pairs={{0,16},{16,0},{1,17},{17,1},{2,18},{18,2},{3,19},{19,3},{4,20},{20... | collective-permute-start | bytes 835592 | tf_op jit(solution)/shard_map/ppermute | solution.py:282
  (8 other events, 31.1 us)

commit v3 on v2

--- a/solution.py
+++ b/solution.py
@@ -37,61 +37,129 @@
     angle = pos.astype(jnp.float32)[:, None] * freqs[None, :]
     cosine = jnp.cos(angle)
     sine = jnp.sin(angle)
-    return (
-        jnp.concatenate([cosine, cosine], axis=1),
-        jnp.concatenate([-sine, sine], axis=1),
-    )
-
-
-def qkv_kernel(blk_ref, *refs):
-    sets, (w_ref, cos_ref, sin_ref, q_ref, kv_ref, nrm) = refs[:8], refs[8:]
+    return cosine, sine
+
+
+def squares_and_scaled(sets, put):
     tile = 64
-
-    def norm_rows(i, carry):
+    count = 2 * len(sets)
+
+    def rows_of(i, carry):
         r = pl.multiple_of(i * tile, tile)
         acc = jnp.zeros((tile, FEAT), jnp.float32)
-        for b in range(16):
-            x = sets[b // 2][b % 2, pl.ds(r, tile), :].astype(jnp.float32)
-            acc = acc + x * x
-        scale = lax.rsqrt(jnp.sum(acc, axis=1, keepdims=True) / D + EPS)
-        for b in range(16):
+        for b in range(count):
             x = sets[b // 2][b % 2, pl.ds(r, tile), :].astype(jnp.float32)
             gain = sets[b // 2][b % 2, ROWS : ROWS + 1, :].astype(jnp.float32)
-            col = pl.multiple_of(blk_ref[b] * FEAT, FEAT)
-            nrm[pl.ds(r, tile), pl.ds(col, FEAT)] = (x * scale * gain).astype(jnp.bfloat16)
+            acc = acc + x * x
+            put(b, r, tile, (x * gain).astype(jnp.bfloat16))
+        put(None, r, tile, jnp.sum(acc, axis=1, keepdims=True))
         return carry
 
-    lax.fori_loop(0, ROWS // tile, norm_rows, 0)
-    out = jnp.dot(nrm[...], w_ref[...], preferred_element_type=jnp.float32)
-    cosine, sine = cos_ref[...], sin_ref[...]
+    lax.fori_loop(0, ROWS // tile, rows_of, 0)
+
+
+def fetch_rows(blk_ref, first, count, w_ref, w_some, sem):
+    fetches = []
+    for b in range(count):
+        row = pl.multiple_of(blk_ref[first + b] * FEAT, FEAT)
+        for s in range(3):
+            to = w_some.at[b * FEAT : (b + 1) * FEAT, s * HD : (s + 1) * HD]
+            fetches.append(
+                pltpu.make_async_copy(w_ref.at[s, pl.ds(row, FEAT), :], to, sem.at[3 * b + s])
+            )
+    for fetch in fetches:
+        fetch.start()
+    return fetches
+
+
+def early_kernel(blk_ref, *refs):
+    sets, (w_ref, out_ref, ssq_ref, xs, w_some, sem) = refs[:6], refs[6:]
+    fetches = fetch_rows(blk_ref, 0, 12, w_ref, w_some, sem)
+
+    def put(b, r, tile, value):
+        if b is None:
+            ssq_ref[pl.ds(r, tile), :] = jnp.broadcast_to(value, (tile, HD))
+        else:
+            xs[pl.ds(r, tile), b * FEAT : (b + 1) * FEAT] = value
+
+    squares_and_scaled(sets, put)
+    for fetch in fetches:
+        fetch.wait()
+    out_ref[...] = jnp.dot(xs[...], w_some[...], preferred_element_type=jnp.float32)
+
+
+def late_kernel(blk_ref, *refs):
+    sets = refs[:2]
+    w_ref, out_ref, ssq_ref, cos_ref, sin_ref, q_ref, kv_ref, xs, ssq, w_some, sem = refs[2:]
+    fetches = fetch_rows(blk_ref, 12, 4, w_ref, w_some, sem)
+
+    def put(b, r, tile, value):
+        if b is None:
+            ssq[pl.ds(r, tile), :] = jnp.broadcast_to(value, (tile, HD))
+        else:
+            xs[pl.ds(r, tile), b * FEAT : (b + 1) * FEAT] = value
+
+    squares_and_scaled(sets, put)
+    for fetch in fetches:
+        fetch.wait()
+    out = out_ref[...] + jnp.dot(xs[...], w_some[...], preferred_element_type=jnp.float32)
+    scale = lax.rsqrt((ssq_ref[...] + ssq[...]) / D + EPS)
+    cosine = jnp.concatenate([cos_ref[...], cos_ref[...]], axis=1)
+    sine = jnp.concatenate([-sin_ref[...], sin_ref[...]], axis=1)
 
     def rotate(v):
+        v = v * scale
         return (v * cosine + pltpu.roll(v, HD // 2, 1) * sine).astype(jnp.bfloat16)
 
     q_ref[...] = rotate(out[:, :HD])
     kv_ref[:ROWS, :] = rotate(out[:, HD : 2 * HD])
-    vt = out[:, 2 * HD :].T.astype(jnp.bfloat16)
+    vt = (out[:, 2 * HD :] * scale).T.astype(jnp.bfloat16)
     for b in range(ROWS // HD):
         kv_ref[ROWS + b * HD : ROWS + (b + 1) * HD, :] = vt[:, b * HD : (b + 1) * HD]
 
 
 def project(blk, sets, w, cosine, sine):
-    vmem = pl.BlockSpec(memory_space=pltpu.VMEM)
+    vmem, smem = pl.BlockSpec(memory_space=pltpu.VMEM), pl.BlockSpec(memory_space=pltpu.SMEM)
+    hbm = pl.BlockSpec(memory_space=pltpu.HBM)
+    params = pltpu.CompilerParams(vmem_limit_bytes=20 * 2**20)
+    cost = lambda blocks: pl.CostEstimate(
+        flops=2 * ROWS * blocks * FEAT * 3 * HD, bytes_accessed=blocks * 2**19, transcendentals=0
+    )
+    out, ssq = pl.pallas_call(
+        early_kernel,
+        out_shape=(
+            jax.ShapeDtypeStruct((ROWS, 3 * HD), jnp.float32),
+            jax.ShapeDtypeStruct((ROWS, HD), jnp.float32),
+        ),
+        in_specs=[smem] + [vmem] * 6 + [hbm],
+        out_specs=(vmem, vmem),
+        scratch_shapes=[
+            pltpu.VMEM((ROWS, 12 * FEAT), jnp.bfloat16),
+            pltpu.VMEM((12 * FEAT, 3 * HD), jnp.bfloat16),
+            pltpu.SemaphoreType.DMA((36,)),
+        ],
+        compiler_params=params,
+        cost_estimate=cost(12),
+        name="early_qkv",
+    )(blk, *sets[:6], w)
     return pl.pallas_call(
-        qkv_kernel,
+        late_kernel,
         out_shape=(
             jax.ShapeDtypeStruct((ROWS, HD), jnp.bfloat16),
             jax.ShapeDtypeStruct((2 * ROWS, HD), jnp.bfloat16),
         ),
-        in_specs=[pl.BlockSpec(memory_space=pltpu.SMEM)] + [vmem] * 11,
+        in_specs=[smem] + [vmem] * 2 + [hbm] + [vmem] * 4,
         out_specs=(vmem, vmem),
-        scratch_shapes=[pltpu.VMEM((ROWS, D), jnp.bfloat16)],
-        compiler_params=pltpu.CompilerParams(vmem_limit_bytes=40 * 2**20),
-        cost_estimate=pl.CostEstimate(
-            flops=2 * ROWS * D * 3 * HD, bytes_accessed=8 * 2**20, transcendentals=0
-        ),
-        name="norm_qkv",
-    )(blk, *sets, w, cosine, sine)
+        scratch_shapes=[
+            pltpu.VMEM((ROWS, 4 * FEAT), jnp.bfloat16),
+            pltpu.VMEM((ROWS, HD), jnp.float32),
+            pltpu.VMEM((4 * FEAT, 3 * HD), jnp.bfloat16),
+            pltpu.SemaphoreType.DMA((12,)),
+        ],
+        compiler_params=params,
+        cost_estimate=cost(4),
+        name="late_qkv",
+    )(blk, *sets[6:], w, out, ssq, cosine, sine)
 
 
 def attend_kernel(offs, fresh, last_call, meta_ref, q_ref, lo_ref, hi_ref, *refs):
@@ -187,7 +255,7 @@
         out_specs=(vmem, vmem) if last_call else vmem,
         scratch_shapes=[pltpu.VMEM(full, jnp.float32)] if last_call else [],
         input_output_aliases={4 + n: 0} if state and not last_call else {},
-        compiler_params=pltpu.CompilerParams(vmem_limit_bytes=40 * 2**20),
+        compiler_params=pltpu.CompilerParams(vmem_limit_bytes=20 * 2**20),
         cost_estimate=pl.CostEstimate(
             flops=4 * pairs * HD, bytes_accessed=2 * 2**20, transcendentals=pairs
         ),
@@ -205,9 +273,59 @@
 
 
 def merge(a, b):
+    vmem = pl.BlockSpec(memory_space=pltpu.VMEM)
     return pl.pallas_call(
-        merge_kernel, out_shape=jax.ShapeDtypeStruct((ROWS, HD), jnp.bfloat16), name="merge"
+        merge_kernel,
+        out_shape=jax.ShapeDtypeStruct((ROWS, HD), jnp.bfloat16),
+        in_specs=[vmem, vmem],
+        out_specs=vmem,
+        compiler_params=pltpu.CompilerParams(vmem_limit_bytes=4 * 2**20),
+        name="merge",
     )(a, b)
+
+
+def append_kernel(tok_ref, gain_ref, o_ref, gain, sem):
+    rows = pltpu.make_async_copy(tok_ref, o_ref.at[:ROWS], sem.at[0])
+    row = pltpu.make_async_copy(gain_ref, gain, sem.at[1])
+    rows.start()
+    row.start()
+    row.wait()
+    o_ref[ROWS:, :] = jnp.broadcast_to(gain[...][None, :], (PAD, FEAT))
+    rows.wait()
+
+
+def append(tokens, norm_gain):
+    return pl.pallas_call(
+        append_kernel,
+        out_shape=jax.ShapeDtypeStruct((ROWS + PAD, FEAT), jnp.bfloat16),
+        in_specs=[pl.BlockSpec(memory_space=pltpu.HBM)] * 2,
+        out_specs=pl.BlockSpec(memory_space=pltpu.VMEM),
+        scratch_shapes=[pltpu.VMEM((FEAT,), jnp.bfloat16), pltpu.SemaphoreType.DMA((2,))],
+        compiler_params=pltpu.CompilerParams(vmem_limit_bytes=4 * 2**20),
+        name="append",
+    )(tokens, norm_gain)
+
+
+def pair_kernel(u_ref, v_ref, o_ref, sem):
+    copies = [
+        pltpu.make_async_copy(ref, o_ref.at[i], sem.at[i]) for i, ref in enumerate((u_ref, v_ref))
+    ]
+    for copy in copies:
+        copy.start()
+    for copy in copies:
+        copy.wait()
+
+
+def pair(u, v):
+    return pl.pallas_call(
+        pair_kernel,
+        out_shape=jax.ShapeDtypeStruct((2,) + u.shape, u.dtype),
+        in_specs=[pl.BlockSpec(memory_space=pl.ANY)] * 2,
+        out_specs=pl.BlockSpec(memory_space=pltpu.VMEM),
+        scratch_shapes=[pltpu.SemaphoreType.DMA((2,))],
+        compiler_params=pltpu.CompilerParams(vmem_limit_bytes=4 * 2**20),
+        name="pair",
+    )(u, v)
 
 
 def plane_perm(d, first):
@@ -232,9 +350,9 @@
     y, x = lax.axis_index("y"), lax.axis_index("x")
     plane = ("core", "y", "x")
 
-    mine = jnp.concatenate([tokens, jnp.broadcast_to(norm_gain[None, :], (PAD, FEAT))], axis=0)
+    mine = append(tokens, norm_gain)
     side = {d: lax.ppermute(mine, plane, plane_perm(d, True)) for d in (1, -1, 2)}
-    a, b = jnp.stack([mine, side[1]]), jnp.stack([side[-1], side[2]])
+    a, b = pair(mine, side[1]), pair(side[-1], side[2])
     far = lambda v, d: lax.ppermute(v, plane, plane_perm(d, False))
     left_a, right_b = far(a, 1), far(b, -1)
     left_b, right_a = far(b, 1), far(a, -1)
@@ -260,8 +378,7 @@
     meta = jnp.where(slot % 4 < 2, low, high)
     meta = jnp.where(slot == 8, z, jnp.where(slot == 9, core, meta)).astype(jnp.int32)
 
-    w = jnp.concatenate([w_qkv[0], w_qkv[1], w_qkv[2]], axis=1)
-    q, kv = project(blk, sets, w, cosine, sine)
+    q, kv = project(blk, sets, w_qkv, cosine, sine)
 
     half = NZ // 2
     z_step = lambda v, d: lax.ppermute(v, "z", ring(NZ, d))

time: 151 us -> 147 us (0.974)
  waiting for transfers between devices: 27.1 us -> 23.3 us
  local copies, waits for them, and re-layouts: 4.2 us -> 1.62 us
  Pallas kernels: 15.1 us -> 17 us
    ppermute x6, waiting for transfers between devices: 9.18 us -> 3.34 us  [body(): far = lambda v, d: lax.ppermute(v, plane, plane_perm(d, False))]
    pallas_call x1 -> x5, Pallas kernels: 5.27 us -> 9.38 us  [the longest x1 4.63 us: project(): pl.pallas_call(early_kernel, out_shape=(jax.ShapeDtypeStruct((ROWS, 3 * H...]
    squeeze x1 -> x0, local copies, waits for them, and re-layouts: 2.11 us -> none  [body(): w = jnp.concatenate([w_qkv[0], w_qkv[1], w_qkv[2]], axis=1)]
  transfers between devices with their start and end apart: 26 -> 26, of which waited for: 12 -> 12; matrix products, arithmetic and copies ran while one was open for 4% -> 3% of each run, Pallas kernels for 5% -> 9%
where the time goes in v3:
time: 147 us; the launch traced here: 146 us
  starting transfers between devices  98.7 us (67%)
  waiting for transfers between devices  23.3 us (16%)
  Pallas kernels  17 us (12%)
  other arithmetic  4.97 us (3%)
  local copies, waits for them, and re-layouts  1.62 us (1%)
    ppermute x15, starting transfers between devices, body(): z_step = lambda v, d: lax.ppermute(v, 'z', ring(NZ, d))  53.8 us
    ppermute x6, starting transfers between devices, body(): far = lambda v, d: lax.ppermute(v, plane, plane_perm(d, False))  18.1 us
    ppermute x15, waiting for transfers between devices, body(): z_step = lambda v, d: lax.ppermute(v, 'z', ring(NZ, d))  18 us
    ppermute x3, starting transfers between devices, body(): lax.ppermute(mine, plane, plane_perm(d, True))  10.6 us
    ppermute x1, starting transfers between devices, body(): return merge(own, lax.ppermute(other, 'core', ring(2, 1)))  9.11 us
    ppermute x1, starting transfers between devices, body(): q2 = jnp.stack([q, lax.ppermute(q, 'core', ring(2, 1))], axis=0)  7.08 us
    pallas_call x9, Pallas kernels, attend(): pl.pallas_call(functools.partial(attend_kernel, offs, not state, last_cal...  6.87 us
    pallas_call x1, Pallas kernels, project(): pl.pallas_call(early_kernel, out_shape=(jax.ShapeDtypeStruct((ROWS, 3 * H...  4.63 us
  transfers between devices with their start and end apart: 26, of which 12 were waited for; matrix products, arithmetic and copies ran while one was open for 3% of the time, Pallas kernels for 9%

profile of v3, /device:TPU:1, one launch (start us, length us, event | category | flops | bytes accessed | tf_op | source)
XLA Modules:
  0.0 146.2 jit_solution(17233951799963013552)
XLA Ops:
  1.7 5.7 %collective-permute-start.3 = (bf16[528,256]{1,0:T(8,128)(2,1)S(1)}, bf16[528,256]{1,0:T(8,128)(2,1)}, u32[]{:S(2)}, u32[]{:S(2)}) collective-permute-start(bf16[528,256]{1,0:T(8,128)(2,1)S(1)} %append.1.u_ref), channel_id=1, source_target_pairs={{0,3},{1,0},{2,1},{3,2},{4,7},{5,4},{6,5},{7,6},{8,11},{9,8},{10,9... | collective-permute-start | bytes 811016 | tf_op jit(solution)/shard_map/ppermute | solution.py:354
  7.4 2.3 %collective-permute-start.4 = (bf16[528,256]{1,0:T(8,128)(2,1)S(1)}, bf16[528,256]{1,0:T(8,128)(2,1)}, u32[]{:S(2)}, u32[]{:S(2)}) collective-permute-start(bf16[528,256]{1,0:T(8,128)(2,1)S(1)} %append.1.u_ref), channel_id=1, source_target_pairs={{0,2},{1,3},{2,0},{3,1},{4,6},{5,7},{6,4},{7,5},{8,10},{9,11},{10,... | collective-permute-start | bytes 811016 | tf_op jit(solution)/shard_map/ppermute | solution.py:354
  9.7 2.6 %collective-permute-start = (bf16[528,256]{1,0:T(8,128)(2,1)S(1)}, bf16[528,256]{1,0:T(8,128)(2,1)}, u32[]{:S(2)}, u32[]{:S(2)}) collective-permute-start(bf16[528,256]{1,0:T(8,128)(2,1)S(1)} %append.1.u_ref), channel_id=1, source_target_pairs={{0,1},{1,2},{2,3},{3,0},{4,5},{5,6},{6,7},{7,4},{8,9},{9,10},{10,1... | collective-permute-start | bytes 811016 | tf_op jit(solution)/shard_map/ppermute | solution.py:354
  17.4 4.4 %collective-permute-start.5 = (bf16[2,528,256]{2,1,0:T(8,128)(2,1)S(1)}, bf16[2,528,256]{2,1,0:T(8,128)(2,1)S(1)}, u32[]{:S(2)}, u32[]{:S(2)}) collective-permute-start(bf16[2,528,256]{2,1,0:T(8,128)(2,1)S(1)} %pair.3.refs_1_), channel_id=1, source_target_pairs={{0,12},{1,13},{2,14},{3,15},{4,0},{5,1},{6,2},{7,3},{8,4},{9,5},{1... | collective-permute-start | bytes 1622024 | tf_op jit(solution)/shard_map/ppermute | solution.py:356
  24.8 2.1 %collective-permute-start.7 = (bf16[2,528,256]{2,1,0:T(8,128)(2,1)S(1)}, bf16[2,528,256]{2,1,0:T(8,128)(2,1)S(1)}, u32[]{:S(2)}, u32[]{:S(2)}) collective-permute-start(bf16[2,528,256]{2,1,0:T(8,128)(2,1)S(1)} %pair.3.refs_1_), channel_id=1, source_target_pairs={{0,4},{1,5},{2,6},{3,7},{4,8},{5,9},{6,10},{7,11},{8,12},{9,13},{1... | collective-permute-start | bytes 1622024 | tf_op jit(solution)/shard_map/ppermute | solution.py:356
  26.9 4.4 %collective-permute-start.8 = (bf16[2,528,256]{2,1,0:T(8,128)(2,1)S(1)}, bf16[2,528,256]{2,1,0:T(8,128)(2,1)S(1)}, u32[]{:S(2)}, u32[]{:S(2)}) collective-permute-start(bf16[2,528,256]{2,1,0:T(8,128)(2,1)S(1)} %pair.2.refs_0_), channel_id=1, source_target_pairs={{0,12},{1,13},{2,14},{3,15},{4,0},{5,1},{6,2},{7,3},{8,4},{9,5},{1... | collective-permute-start | bytes 1622024 | tf_op jit(solution)/shard_map/ppermute | solution.py:356
  31.3 3.4 %collective-permute-start.6 = (bf16[2,528,256]{2,1,0:T(8,128)(2,1)S(1)}, bf16[2,528,256]{2,1,0:T(8,128)(2,1)S(1)}, u32[]{:S(2)}, u32[]{:S(2)}) collective-permute-start(bf16[2,528,256]{2,1,0:T(8,128)(2,1)S(1)} %collective-permute-done.5.refs_5_), channel_id=1, source_target_pairs={{0,12},{1,13},{2,14},{3,15},{4,0},{5,1},{6,2},{7,3},{8,4},{9,5},{1... | collective-permute-start | bytes 1622024 | tf_op jit(solution)/shard_map/ppermute | solution.py:356
  34.7 1.9 %collective-permute-start.2 = (bf16[2,528,256]{2,1,0:T(8,128)(2,1)S(1)}, bf16[2,528,256]{2,1,0:T(8,128)(2,1)S(1)}, u32[]{:S(2)}, u32[]{:S(2)}) collective-permute-start(bf16[2,528,256]{2,1,0:T(8,128)(2,1)S(1)} %collective-permute-done.1.refs_2_), channel_id=1, source_target_pairs={{0,4},{1,5},{2,6},{3,7},{4,8},{5,9},{6,10},{7,11},{8,12},{9,13},{1... | collective-permute-start | bytes 1622024 | tf_op jit(solution)/shard_map/ppermute | solution.py:356
  38.3 1.9 %collective-permute-done.7.refs_3_ = bf16[2,528,256]{2,1,0:T(8,128)(2,1)S(1)} collective-permute-done((bf16[2,528,256]{2,1,0:T(8,128)(2,1)S(1)}, bf16[2,528,256]{2,1,0:T(8,128)(2,1)S(1)}, u32[]{:S(2)}, u32[]{:S(2)}) %collective-permute-start.7) | collective-permute-done | bytes 540704 | tf_op jit(solution)/shard_map/ppermute | solution.py:356
  40.2 4.6 %early_qkv.1 = (f32[512,384]{1,0:T(8,128)S(1)}, f32[512,128]{1,0:T(8,128)S(1)}) custom-call(s32[16]{0:T(128)S(1)} %fusion.blk_ref, bf16[2,528,256]{2,1,0:T(8,128)(2,1)S(1)} %pair.2.refs_0_, bf16[2,528,256]{2,1,0:T(8,128)(2,1)S(1)} %pair.3.refs_1_, bf16[2,528,256]{2,1,0:T(8,128)(2,1)S(1)} %collective-permute-done.1.refs_2_, ...), custom_call_target="tpu_custom_call" | custom-call | flops 1207959552 | bytes 6291456 | tf_op jit(solution)/shard_map/early_qkv/pallas_call | solution.py:128
  46.3 2.7 %late_qkv.1 = (bf16[512,128]{1,0:T(8,128)(2,1)S(1)}, bf16[1024,128]{1,0:T(8,128)(2,1)S(1)}) custom-call(s32[16]{0:T(128)S(1)} %fusion.blk_ref, bf16[2,528,256]{2,1,0:T(8,128)(2,1)S(1)} %collective-permute-done.2.refs_0_, bf16[2,528,256]{2,1,0:T(8,128)(2,1)S(1)} %collective-permute-done.6.refs_1_, bf16[3,4096,128]{2,1,0:T(8,128)(2,1)S(1)} %copy-done, ...), custom_call_target="tpu_custom_call" | custom-call | flops 402653184 | bytes 2097152 | tf_op jit(solution)/shard_map/late_qkv/pallas_call | solution.py:145
  48.9 3.5 %collective-permute-start.9 = (bf16[1024,128]{1,0:T(8,128)(2,1)S(1)}, bf16[1024,128]{1,0:T(8,128)(2,1)S(1)}, u32[]{:S(2)}, u32[]{:S(2)}) collective-permute-start(bf16[1024,128]{1,0:T(8,128)(2,1)S(1)} %get-tuple-element.29.refs_0_), channel_id=1, source_target_pairs={{0,32},{32,64},{64,96},{96,128},{128,160},{160,192},{192,224},{224... | collective-permute-start | bytes 786440 | tf_op jit(solution)/shard_map/ppermute | solution.py:384
  52.6 9.5 %collective-permute-start.13 = (bf16[1024,128]{1,0:T(8,128)(2,1)S(1)}, bf16[1024,128]{1,0:T(8,128)(2,1)S(1)}, u32[]{:S(2)}, u32[]{:S(2)}) collective-permute-start(bf16[1024,128]{1,0:T(8,128)(2,1)S(1)} %get-tuple-element.29.refs_0_), channel_id=1, source_target_pairs={{0,480},{32,0},{64,32},{96,64},{128,96},{160,128},{192,160},{224,1... | collective-permute-start | bytes 786440 | tf_op jit(solution)/shard_map/ppermute | solution.py:384
  63.8 7.1 %collective-permute-start.10 = (bf16[512,128]{1,0:T(8,128)(2,1)S(1)}, bf16[512,128]{1,0:T(8,128)(2,1)S(1)}, u32[]{:S(2)}, u32[]{:S(2)}) collective-permute-start(bf16[512,128]{1,0:T(8,128)(2,1)S(1)} %get-tuple-element.31), channel_id=1, source_target_pairs={{0,16},{16,0},{1,17},{17,1},{2,18},{18,2},{3,19},{19,3},{4,20},{20... | collective-permute-start | bytes 393224 | tf_op jit(solution)/shard_map/ppermute | solution.py:388
  72.9 4.6 %collective-permute-start.15 = (bf16[1024,128]{1,0:T(8,128)(2,1)S(1)}, bf16[1024,128]{1,0:T(8,128)(2,1)S(1)}, u32[]{:S(2)}, u32[]{:S(2)}) collective-permute-start(bf16[1024,128]{1,0:T(8,128)(2,1)S(1)} %collective-permute-done.13.refs_1_), channel_id=1, source_target_pairs={{0,480},{32,0},{64,32},{96,64},{128,96},{160,128},{192,160},{224,1... | collective-permute-start | bytes 786440 | tf_op jit(solution)/shard_map/ppermute | solution.py:384
  79.0 2.9 %collective-permute-done.11.refs_0_ = bf16[1024,128]{1,0:T(8,128)(2,1)S(1)} collective-permute-done((bf16[1024,128]{1,0:T(8,128)(2,1)S(1)}, bf16[1024,128]{1,0:T(8,128)(2,1)S(1)}, u32[]{:S(2)}, u32[]{:S(2)}) %collective-permute-start.11) | collective-permute-done | bytes 262176 | tf_op jit(solution)/shard_map/ppermute | solution.py:384
  83.9 4.6 %collective-permute-start.17 = (bf16[1024,128]{1,0:T(8,128)(2,1)S(1)}, bf16[1024,128]{1,0:T(8,128)(2,1)S(1)}, u32[]{:S(2)}, u32[]{:S(2)}) collective-permute-start(bf16[1024,128]{1,0:T(8,128)(2,1)S(1)} %collective-permute-done.15.refs_1_), channel_id=1, source_target_pairs={{0,480},{32,0},{64,32},{96,64},{128,96},{160,128},{192,160},{224,1... | collective-permute-start | bytes 786440 | tf_op jit(solution)/shard_map/ppermute | solution.py:384
  89.1 3.0 %collective-permute-done.12.refs_0_ = bf16[1024,128]{1,0:T(8,128)(2,1)S(1)} collective-permute-done((bf16[1024,128]{1,0:T(8,128)(2,1)S(1)}, bf16[1024,128]{1,0:T(8,128)(2,1)S(1)}, u32[]{:S(2)}, u32[]{:S(2)}) %collective-permute-start.12) | collective-permute-done | bytes 262176 | tf_op jit(solution)/shard_map/ppermute | solution.py:384
  94.0 4.6 %collective-permute-start.19 = (bf16[1024,128]{1,0:T(8,128)(2,1)S(1)}, bf16[1024,128]{1,0:T(8,128)(2,1)S(1)}, u32[]{:S(2)}, u32[]{:S(2)}) collective-permute-start(bf16[1024,128]{1,0:T(8,128)(2,1)S(1)} %collective-permute-done.17.refs_1_), channel_id=1, source_target_pairs={{0,480},{32,0},{64,32},{96,64},{128,96},{160,128},{192,160},{224,1... | collective-permute-start | bytes 786440 | tf_op jit(solution)/shard_map/ppermute | solution.py:384
  103.2 4.6 %collective-permute-start.21 = (bf16[1024,128]{1,0:T(8,128)(2,1)S(1)}, bf16[1024,128]{1,0:T(8,128)(2,1)S(1)}, u32[]{:S(2)}, u32[]{:S(2)}) collective-permute-start(bf16[1024,128]{1,0:T(8,128)(2,1)S(1)} %collective-permute-done.19.refs_1_), channel_id=1, source_target_pairs={{0,480},{32,0},{64,32},{96,64},{128,96},{160,128},{192,160},{224,1... | collective-permute-start | bytes 786440 | tf_op jit(solution)/shard_map/ppermute | solution.py:384
  111.5 4.6 %collective-permute-start.23 = (bf16[1024,128]{1,0:T(8,128)(2,1)S(1)}, bf16[1024,128]{1,0:T(8,128)(2,1)S(1)}, u32[]{:S(2)}, u32[]{:S(2)}) collective-permute-start(bf16[1024,128]{1,0:T(8,128)(2,1)S(1)} %collective-permute-done.21.refs_1_), channel_id=1, source_target_pairs={{0,480},{32,0},{64,32},{96,64},{128,96},{160,128},{192,160},{224,1... | collective-permute-start | bytes 786440 | tf_op jit(solution)/shard_map/ppermute | solution.py:384
  119.8 4.6 %collective-permute-start.24 = (bf16[1024,128]{1,0:T(8,128)(2,1)S(1)}, bf16[1024,128]{1,0:T(8,128)(2,1)S(1)}, u32[]{:S(2)}, u32[]{:S(2)}) collective-permute-start(bf16[1024,128]{1,0:T(8,128)(2,1)S(1)} %collective-permute-done.23.refs_1_), channel_id=1, source_target_pairs={{0,480},{32,0},{64,32},{96,64},{128,96},{160,128},{192,160},{224,1... | collective-permute-start | bytes 786440 | tf_op jit(solution)/shard_map/ppermute | solution.py:384
  129.4 5.1 %collective-permute-done.22.refs_0_ = bf16[1024,128]{1,0:T(8,128)(2,1)S(1)} collective-permute-done((bf16[1024,128]{1,0:T(8,128)(2,1)S(1)}, bf16[1024,128]{1,0:T(8,128)(2,1)S(1)}, u32[]{:S(2)}, u32[]{:S(2)}) %collective-permute-start.22) | collective-permute-done | bytes 262176 | tf_op jit(solution)/shard_map/ppermute | solution.py:384
  135.2 9.1 %collective-permute-start.25 = (f32[136,512]{1,0:T(8,128)S(1)}, f32[136,512]{1,0:T(8,128)S(1)}, u32[]{:S(2)}, u32[]{:S(2)}) collective-permute-start(f32[136,512]{1,0:T(8,128)S(1)} %get-tuple-element.48), channel_id=1, source_target_pairs={{0,16},{16,0},{1,17},{17,1},{2,18},{18,2},{3,19},{19,3},{4,20},{20... | collective-permute-start | bytes 835592 | tf_op jit(solution)/shard_map/ppermute | solution.py:399
  (74 shorter events, 42.1 us)
Async XLA Ops:
  1.7 13.8 %collective-permute-start.3 = (bf16[528,256]{1,0:T(8,128)(2,1)S(1)}, bf16[528,256]{1,0:T(8,128)(2,1)}, u32[]{:S(2)}, u32[]{:S(2)}) collective-permute-start(bf16[528,256]{1,0:T(8,128)(2,1)S(1)} %append.1.u_ref), channel_id=1, source_target_pairs={{0,3},{1,0},{2,1},{3,2},{4,7},{5,4},{6,5},{7,6},{8,11},{9,8},{10,9... | collective-permute-start | bytes 811016 | tf_op jit(solution)/shard_map/ppermute | solution.py:354
  7.4 8.9 %collective-permute-start.4 = (bf16[528,256]{1,0:T(8,128)(2,1)S(1)}, bf16[528,256]{1,0:T(8,128)(2,1)}, u32[]{:S(2)}, u32[]{:S(2)}) collective-permute-start(bf16[528,256]{1,0:T(8,128)(2,1)S(1)} %append.1.u_ref), channel_id=1, source_target_pairs={{0,2},{1,3},{2,0},{3,1},{4,6},{5,7},{6,4},{7,5},{8,10},{9,11},{10,... | collective-permute-start | bytes 811016 | tf_op jit(solution)/shard_map/ppermute | solution.py:354
  9.7 12.1 %collective-permute-start = (bf16[528,256]{1,0:T(8,128)(2,1)S(1)}, bf16[528,256]{1,0:T(8,128)(2,1)}, u32[]{:S(2)}, u32[]{:S(2)}) collective-permute-start(bf16[528,256]{1,0:T(8,128)(2,1)S(1)} %append.1.u_ref), channel_id=1, source_target_pairs={{0,1},{1,2},{2,3},{3,0},{4,5},{5,6},{6,7},{7,4},{8,9},{9,10},{10,1... | collective-permute-start | bytes 811016 | tf_op jit(solution)/shard_map/ppermute | solution.py:354
  17.4 13.9 %collective-permute-start.5 = (bf16[2,528,256]{2,1,0:T(8,128)(2,1)S(1)}, bf16[2,528,256]{2,1,0:T(8,128)(2,1)S(1)}, u32[]{:S(2)}, u32[]{:S(2)}) collective-permute-start(bf16[2,528,256]{2,1,0:T(8,128)(2,1)S(1)} %pair.3.refs_1_), channel_id=1, source_target_pairs={{0,12},{1,13},{2,14},{3,15},{4,0},{5,1},{6,2},{7,3},{8,4},{9,5},{1... | collective-permute-start | bytes 1622024 | tf_op jit(solution)/shard_map/ppermute | solution.py:356
  22.8 11.9 %collective-permute-start.1 = (bf16[2,528,256]{2,1,0:T(8,128)(2,1)S(1)}, bf16[2,528,256]{2,1,0:T(8,128)(2,1)S(1)}, u32[]{:S(2)}, u32[]{:S(2)}) collective-permute-start(bf16[2,528,256]{2,1,0:T(8,128)(2,1)S(1)} %pair.2.refs_0_), channel_id=1, source_target_pairs={{0,4},{1,5},{2,6},{3,7},{4,8},{5,9},{6,10},{7,11},{8,12},{9,13},{1... | collective-permute-start | bytes 1622024 | tf_op jit(solution)/shard_map/ppermute | solution.py:356
  24.8 15.4 %collective-permute-start.7 = (bf16[2,528,256]{2,1,0:T(8,128)(2,1)S(1)}, bf16[2,528,256]{2,1,0:T(8,128)(2,1)S(1)}, u32[]{:S(2)}, u32[]{:S(2)}) collective-permute-start(bf16[2,528,256]{2,1,0:T(8,128)(2,1)S(1)} %pair.3.refs_1_), channel_id=1, source_target_pairs={{0,4},{1,5},{2,6},{3,7},{4,8},{5,9},{6,10},{7,11},{8,12},{9,13},{1... | collective-permute-start | bytes 1622024 | tf_op jit(solution)/shard_map/ppermute | solution.py:356
  26.9 13.3 %collective-permute-start.8 = (bf16[2,528,256]{2,1,0:T(8,128)(2,1)S(1)}, bf16[2,528,256]{2,1,0:T(8,128)(2,1)S(1)}, u32[]{:S(2)}, u32[]{:S(2)}) collective-permute-start(bf16[2,528,256]{2,1,0:T(8,128)(2,1)S(1)} %pair.2.refs_0_), channel_id=1, source_target_pairs={{0,12},{1,13},{2,14},{3,15},{4,0},{5,1},{6,2},{7,3},{8,4},{9,5},{1... | collective-permute-start | bytes 1622024 | tf_op jit(solution)/shard_map/ppermute | solution.py:356
  31.3 13.6 %collective-permute-start.6 = (bf16[2,528,256]{2,1,0:T(8,128)(2,1)S(1)}, bf16[2,528,256]{2,1,0:T(8,128)(2,1)S(1)}, u32[]{:S(2)}, u32[]{:S(2)}) collective-permute-start(bf16[2,528,256]{2,1,0:T(8,128)(2,1)S(1)} %collective-permute-done.5.refs_5_), channel_id=1, source_target_pairs={{0,12},{1,13},{2,14},{3,15},{4,0},{5,1},{6,2},{7,3},{8,4},{9,5},{1... | collective-permute-start | bytes 1622024 | tf_op jit(solution)/shard_map/ppermute | solution.py:356
  34.7 11.6 %collective-permute-start.2 = (bf16[2,528,256]{2,1,0:T(8,128)(2,1)S(1)}, bf16[2,528,256]{2,1,0:T(8,128)(2,1)S(1)}, u32[]{:S(2)}, u32[]{:S(2)}) collective-permute-start(bf16[2,528,256]{2,1,0:T(8,128)(2,1)S(1)} %collective-permute-done.1.refs_2_), channel_id=1, source_target_pairs={{0,4},{1,5},{2,6},{3,7},{4,8},{5,9},{6,10},{7,11},{8,12},{9,13},{1... | collective-permute-start | bytes 1622024 | tf_op jit(solution)/shard_map/ppermute | solution.py:356
  48.9 14.9 %collective-permute-start.9 = (bf16[1024,128]{1,0:T(8,128)(2,1)S(1)}, bf16[1024,128]{1,0:T(8,128)(2,1)S(1)}, u32[]{:S(2)}, u32[]{:S(2)}) collective-permute-start(bf16[1024,128]{1,0:T(8,128)(2,1)S(1)} %get-tuple-element.29.refs_0_), channel_id=1, source_target_pairs={{0,32},{32,64},{64,96},{96,128},{128,160},{160,192},{192,224},{224... | collective-permute-start | bytes 786440 | tf_op jit(solution)/shard_map/ppermute | solution.py:384
  52.6 20.2 %collective-permute-start.13 = (bf16[1024,128]{1,0:T(8,128)(2,1)S(1)}, bf16[1024,128]{1,0:T(8,128)(2,1)S(1)}, u32[]{:S(2)}, u32[]{:S(2)}) collective-permute-start(bf16[1024,128]{1,0:T(8,128)(2,1)S(1)} %get-tuple-element.29.refs_0_), channel_id=1, source_target_pairs={{0,480},{32,0},{64,32},{96,64},{128,96},{160,128},{192,160},{224,1... | collective-permute-start | bytes 786440 | tf_op jit(solution)/shard_map/ppermute | solution.py:384
  63.8 13.6 %collective-permute-start.10 = (bf16[512,128]{1,0:T(8,128)(2,1)S(1)}, bf16[512,128]{1,0:T(8,128)(2,1)S(1)}, u32[]{:S(2)}, u32[]{:S(2)}) collective-permute-start(bf16[512,128]{1,0:T(8,128)(2,1)S(1)} %get-tuple-element.31), channel_id=1, source_target_pairs={{0,16},{16,0},{1,17},{17,1},{2,18},{18,2},{3,19},{19,3},{4,20},{20... | collective-permute-start | bytes 393224 | tf_op jit(solution)/shard_map/ppermute | solution.py:388
  70.9 11.0 %collective-permute-start.11 = (bf16[1024,128]{1,0:T(8,128)(2,1)S(1)}, bf16[1024,128]{1,0:T(8,128)(2,1)S(1)}, u32[]{:S(2)}, u32[]{:S(2)}) collective-permute-start(bf16[1024,128]{1,0:T(8,128)(2,1)S(1)} %collective-permute-done.9.refs_0_), channel_id=1, source_target_pairs={{0,32},{32,64},{64,96},{96,128},{128,160},{160,192},{192,224},{224... | collective-permute-start | bytes 786440 | tf_op jit(solution)/shard_map/ppermute | solution.py:384
  72.9 11.0 %collective-permute-start.15 = (bf16[1024,128]{1,0:T(8,128)(2,1)S(1)}, bf16[1024,128]{1,0:T(8,128)(2,1)S(1)}, u32[]{:S(2)}, u32[]{:S(2)}) collective-permute-start(bf16[1024,128]{1,0:T(8,128)(2,1)S(1)} %collective-permute-done.13.refs_1_), channel_id=1, source_target_pairs={{0,480},{32,0},{64,32},{96,64},{128,96},{160,128},{192,160},{224,1... | collective-permute-start | bytes 786440 | tf_op jit(solution)/shard_map/ppermute | solution.py:384
  81.9 10.1 %collective-permute-start.12 = (bf16[1024,128]{1,0:T(8,128)(2,1)S(1)}, bf16[1024,128]{1,0:T(8,128)(2,1)S(1)}, u32[]{:S(2)}, u32[]{:S(2)}) collective-permute-start(bf16[1024,128]{1,0:T(8,128)(2,1)S(1)} %collective-permute-done.11.refs_0_), channel_id=1, source_target_pairs={{0,32},{32,64},{64,96},{96,128},{128,160},{160,192},{192,224},{224... | collective-permute-start | bytes 786440 | tf_op jit(solution)/shard_map/ppermute | solution.py:384
  83.9 10.1 %collective-permute-start.17 = (bf16[1024,128]{1,0:T(8,128)(2,1)S(1)}, bf16[1024,128]{1,0:T(8,128)(2,1)S(1)}, u32[]{:S(2)}, u32[]{:S(2)}) collective-permute-start(bf16[1024,128]{1,0:T(8,128)(2,1)S(1)} %collective-permute-done.15.refs_1_), channel_id=1, source_target_pairs={{0,480},{32,0},{64,32},{96,64},{128,96},{160,128},{192,160},{224,1... | collective-permute-start | bytes 786440 | tf_op jit(solution)/shard_map/ppermute | solution.py:384
  92.1 9.2 %collective-permute-start.14 = (bf16[1024,128]{1,0:T(8,128)(2,1)S(1)}, bf16[1024,128]{1,0:T(8,128)(2,1)S(1)}, u32[]{:S(2)}, u32[]{:S(2)}) collective-permute-start(bf16[1024,128]{1,0:T(8,128)(2,1)S(1)} %collective-permute-done.12.refs_0_), channel_id=1, source_target_pairs={{0,32},{32,64},{64,96},{96,128},{128,160},{160,192},{192,224},{224... | collective-permute-start | bytes 786440 | tf_op jit(solution)/shard_map/ppermute | solution.py:384
  94.0 9.2 %collective-permute-start.19 = (bf16[1024,128]{1,0:T(8,128)(2,1)S(1)}, bf16[1024,128]{1,0:T(8,128)(2,1)S(1)}, u32[]{:S(2)}, u32[]{:S(2)}) collective-permute-start(bf16[1024,128]{1,0:T(8,128)(2,1)S(1)} %collective-permute-done.17.refs_1_), channel_id=1, source_target_pairs={{0,480},{32,0},{64,32},{96,64},{128,96},{160,128},{192,160},{224,1... | collective-permute-start | bytes 786440 | tf_op jit(solution)/shard_map/ppermute | solution.py:384
  101.3 8.3 %collective-permute-start.16 = (bf16[1024,128]{1,0:T(8,128)(2,1)S(1)}, bf16[1024,128]{1,0:T(8,128)(2,1)S(1)}, u32[]{:S(2)}, u32[]{:S(2)}) collective-permute-start(bf16[1024,128]{1,0:T(8,128)(2,1)S(1)} %collective-permute-done.14.refs_0_), channel_id=1, source_target_pairs={{0,32},{32,64},{64,96},{96,128},{128,160},{160,192},{192,224},{224... | collective-permute-start | bytes 786440 | tf_op jit(solution)/shard_map/ppermute | solution.py:384
  109.6 8.3 %collective-permute-start.18 = (bf16[1024,128]{1,0:T(8,128)(2,1)S(1)}, bf16[1024,128]{1,0:T(8,128)(2,1)S(1)}, u32[]{:S(2)}, u32[]{:S(2)}) collective-permute-start(bf16[1024,128]{1,0:T(8,128)(2,1)S(1)} %collective-permute-done.16.refs_0_), channel_id=1, source_target_pairs={{0,32},{32,64},{64,96},{96,128},{128,160},{160,192},{192,224},{224... | collective-permute-start | bytes 786440 | tf_op jit(solution)/shard_map/ppermute | solution.py:384
  117.9 8.3 %collective-permute-start.20 = (bf16[1024,128]{1,0:T(8,128)(2,1)S(1)}, bf16[1024,128]{1,0:T(8,128)(2,1)S(1)}, u32[]{:S(2)}, u32[]{:S(2)}) collective-permute-start(bf16[1024,128]{1,0:T(8,128)(2,1)S(1)} %collective-permute-done.18.refs_0_), channel_id=1, source_target_pairs={{0,32},{32,64},{64,96},{96,128},{128,160},{160,192},{192,224},{224... | collective-permute-start | bytes 786440 | tf_op jit(solution)/shard_map/ppermute | solution.py:384
  119.8 9.0 %collective-permute-start.24 = (bf16[1024,128]{1,0:T(8,128)(2,1)S(1)}, bf16[1024,128]{1,0:T(8,128)(2,1)S(1)}, u32[]{:S(2)}, u32[]{:S(2)}) collective-permute-start(bf16[1024,128]{1,0:T(8,128)(2,1)S(1)} %collective-permute-done.23.refs_1_), channel_id=1, source_target_pairs={{0,480},{32,0},{64,32},{96,64},{128,96},{160,128},{192,160},{224,1... | collective-permute-start | bytes 786440 | tf_op jit(solution)/shard_map/ppermute | solution.py:384
  126.2 8.3 %collective-permute-start.22 = (bf16[1024,128]{1,0:T(8,128)(2,1)S(1)}, bf16[1024,128]{1,0:T(8,128)(2,1)S(1)}, u32[]{:S(2)}, u32[]{:S(2)}) collective-permute-start(bf16[1024,128]{1,0:T(8,128)(2,1)S(1)} %collective-permute-done.20.refs_0_), channel_id=1, source_target_pairs={{0,32},{32,64},{64,96},{96,128},{128,160},{160,192},{192,224},{224... | collective-permute-start | bytes 786440 | tf_op jit(solution)/shard_map/ppermute | solution.py:384
  135.2 10.3 %collective-permute-start.25 = (f32[136,512]{1,0:T(8,128)S(1)}, f32[136,512]{1,0:T(8,128)S(1)}, u32[]{:S(2)}, u32[]{:S(2)}) collective-permute-start(f32[136,512]{1,0:T(8,128)S(1)} %get-tuple-element.48), channel_id=1, source_target_pairs={{0,16},{16,0},{1,17},{17,1},{2,18},{18,2},{3,19},{19,3},{4,20},{20... | collective-permute-start | bytes 835592 | tf_op jit(solution)/shard_map/ppermute | solution.py:399
  (6 other events, 64.5 us)

commit v4 on v2

--- a/solution.py
+++ b/solution.py
@@ -86,7 +86,7 @@
         in_specs=[pl.BlockSpec(memory_space=pltpu.SMEM)] + [vmem] * 11,
         out_specs=(vmem, vmem),
         scratch_shapes=[pltpu.VMEM((ROWS, D), jnp.bfloat16)],
-        compiler_params=pltpu.CompilerParams(vmem_limit_bytes=40 * 2**20),
+        compiler_params=pltpu.CompilerParams(vmem_limit_bytes=20 * 2**20),
         cost_estimate=pl.CostEstimate(
             flops=2 * ROWS * D * 3 * HD, bytes_accessed=8 * 2**20, transcendentals=0
         ),
@@ -187,7 +187,7 @@
         out_specs=(vmem, vmem) if last_call else vmem,
         scratch_shapes=[pltpu.VMEM(full, jnp.float32)] if last_call else [],
         input_output_aliases={4 + n: 0} if state and not last_call else {},
-        compiler_params=pltpu.CompilerParams(vmem_limit_bytes=40 * 2**20),
+        compiler_params=pltpu.CompilerParams(vmem_limit_bytes=20 * 2**20),
         cost_estimate=pl.CostEstimate(
             flops=4 * pairs * HD, bytes_accessed=2 * 2**20, transcendentals=pairs
         ),
@@ -205,8 +205,14 @@
 
 
 def merge(a, b):
+    vmem = pl.BlockSpec(memory_space=pltpu.VMEM)
     return pl.pallas_call(
-        merge_kernel, out_shape=jax.ShapeDtypeStruct((ROWS, HD), jnp.bfloat16), name="merge"
+        merge_kernel,
+        out_shape=jax.ShapeDtypeStruct((ROWS, HD), jnp.bfloat16),
+        in_specs=[vmem, vmem],
+        out_specs=vmem,
+        compiler_params=pltpu.CompilerParams(vmem_limit_bytes=4 * 2**20),
+        name="merge",
     )(a, b)
 
 

time: 151 us -> 148 us (0.980)
  no operation moved by 1% of the time
where the time goes in v4:
time: 148 us; the launch traced here: 147 us
  starting transfers between devices  97.8 us (66%)
  waiting for transfers between devices  27.1 us (18%)
  Pallas kernels  14.1 us (10%)
  other arithmetic  4.76 us (3%)
  local copies, waits for them, and re-layouts  2.79 us (2%)
    ppermute x15, starting transfers between devices, body(): z_step = lambda v, d: lax.ppermute(v, 'z', ring(NZ, d))  53.8 us
    ppermute x6, starting transfers between devices, body(): far = lambda v, d: lax.ppermute(v, plane, plane_perm(d, False))  18.1 us
    ppermute x15, waiting for transfers between devices, body(): z_step = lambda v, d: lax.ppermute(v, 'z', ring(NZ, d))  16.8 us
    ppermute x3, starting transfers between devices, body(): lax.ppermute(mine, plane, plane_perm(d, True))  10.3 us
    ppermute x6, waiting for transfers between devices, body(): far = lambda v, d: lax.ppermute(v, plane, plane_perm(d, False))  9.18 us
    ppermute x1, starting transfers between devices, body(): return merge(own, lax.ppermute(other, 'core', ring(2, 1)))  9.11 us
    pallas_call x9, Pallas kernels, attend(): pl.pallas_call(functools.partial(attend_kernel, offs, not state, last_cal...  8.06 us
    ppermute x1, starting transfers between devices, body(): q2 = jnp.stack([q, lax.ppermute(q, 'core', ring(2, 1))], axis=0)  6.46 us
  transfers between devices with their start and end apart: 26, of which 12 were waited for; matrix products, arithmetic and copies ran while one was open for 4% of the time, Pallas kernels for 5%

profile of v4, /device:TPU:1, one launch (start us, length us, event | category | flops | bytes accessed | tf_op | source)
XLA Modules:
  0.0 147.2 jit_solution(12518621416526073248)
XLA Ops:
  1.6 5.5 %collective-permute-start.1 = (bf16[528,256]{1,0:T(8,128)(2,1)S(1)}, bf16[528,256]{1,0:T(8,128)(2,1)S(1)}, u32[]{:S(2)}, u32[]{:S(2)}) collective-permute-start(bf16[528,256]{1,0:T(8,128)(2,1)S(1)} %get-tuple-element.61), channel_id=1, source_target_pairs={{0,3},{1,0},{2,1},{3,2},{4,7},{5,4},{6,5},{7,6},{8,11},{9,8},{10,9... | collective-permute-start | bytes 811016 | tf_op jit(solution)/shard_map/ppermute | solution.py:242
  7.1 2.3 %collective-permute-start.2 = (bf16[528,256]{1,0:T(8,128)(2,1)S(1)}, bf16[528,256]{1,0:T(8,128)(2,1)S(1)}, u32[]{:S(2)}, u32[]{:S(2)}) collective-permute-start(bf16[528,256]{1,0:T(8,128)(2,1)S(1)} %get-tuple-element.61), channel_id=1, source_target_pairs={{0,2},{1,3},{2,0},{3,1},{4,6},{5,7},{6,4},{7,5},{8,10},{9,11},{10,... | collective-permute-start | bytes 811016 | tf_op jit(solution)/shard_map/ppermute | solution.py:242
  9.4 2.6 %collective-permute-start = (bf16[528,256]{1,0:T(8,128)(2,1)S(1)}, bf16[528,256]{1,0:T(8,128)(2,1)S(1)}, u32[]{:S(2)}, u32[]{:S(2)}) collective-permute-start(bf16[528,256]{1,0:T(8,128)(2,1)S(1)} %get-tuple-element.61), channel_id=1, source_target_pairs={{0,1},{1,2},{2,3},{3,0},{4,5},{5,6},{6,7},{7,4},{8,9},{9,10},{10,1... | collective-permute-start | bytes 811016 | tf_op jit(solution)/shard_map/ppermute | solution.py:242
  13.6 2.1 %slice_bitcast_fusion.2 = (bf16[4096,128]{1,0:T(8,128)(2,1)S(1)}, bf16[4096,128]{1,0:T(8,128)(2,1)S(1)}, bf16[4096,128]{1,0:T(8,128)(2,1)S(1)}) fusion(bf16[3,4096,128]{2,1,0:T(8,128)(2,1)} %param.10), kind=kLoop, calls=%fused_computation.3 | loop fusion | bytes 6291456 | tf_op jit(solution)/shard_map/squeeze | solution.py:269
  17.3 4.4 %collective-permute-start.6 = (bf16[2,528,256]{2,1,0:T(8,128)(2,1)S(1)}, bf16[2,528,256]{2,1,0:T(8,128)(2,1)S(1)}, u32[]{:S(2)}, u32[]{:S(2)}) collective-permute-start(bf16[2,528,256]{2,1,0:T(8,128)(2,1)S(1)} %pad_maximum_fusion.2.refs_1_), channel_id=1, source_target_pairs={{0,12},{1,13},{2,14},{3,15},{4,0},{5,1},{6,2},{7,3},{8,4},{9,5},{1... | collective-permute-start | bytes 1622024 | tf_op jit(solution)/shard_map/ppermute | solution.py:244
  25.9 4.4 %collective-permute-start.5 = (bf16[2,528,256]{2,1,0:T(8,128)(2,1)S(1)}, bf16[2,528,256]{2,1,0:T(8,128)(2,1)S(1)}, u32[]{:S(2)}, u32[]{:S(2)}) collective-permute-start(bf16[2,528,256]{2,1,0:T(8,128)(2,1)S(1)} %pad_maximum_fusion.1.refs_0_), channel_id=1, source_target_pairs={{0,12},{1,13},{2,14},{3,15},{4,0},{5,1},{6,2},{7,3},{8,4},{9,5},{1... | collective-permute-start | bytes 1622024 | tf_op jit(solution)/shard_map/ppermute | solution.py:244
  30.3 3.4 %collective-permute-start.8 = (bf16[2,528,256]{2,1,0:T(8,128)(2,1)S(1)}, bf16[2,528,256]{2,1,0:T(8,128)(2,1)S(1)}, u32[]{:S(2)}, u32[]{:S(2)}) collective-permute-start(bf16[2,528,256]{2,1,0:T(8,128)(2,1)S(1)} %collective-permute-done.6.refs_5_), channel_id=1, source_target_pairs={{0,12},{1,13},{2,14},{3,15},{4,0},{5,1},{6,2},{7,3},{8,4},{9,5},{1... | collective-permute-start | bytes 1622024 | tf_op jit(solution)/shard_map/ppermute | solution.py:244
  36.1 3.1 %collective-permute-done.4.refs_3_ = bf16[2,528,256]{2,1,0:T(8,128)(2,1)S(1)} collective-permute-done((bf16[2,528,256]{2,1,0:T(8,128)(2,1)S(1)}, bf16[2,528,256]{2,1,0:T(8,128)(2,1)S(1)}, u32[]{:S(2)}, u32[]{:S(2)}) %collective-permute-start.4) | collective-permute-done | bytes 540704 | tf_op jit(solution)/shard_map/ppermute | solution.py:244
  39.2 3.2 %collective-permute-done.8.refs_7_ = bf16[2,528,256]{2,1,0:T(8,128)(2,1)S(1)} collective-permute-done((bf16[2,528,256]{2,1,0:T(8,128)(2,1)S(1)}, bf16[2,528,256]{2,1,0:T(8,128)(2,1)S(1)}, u32[]{:S(2)}, u32[]{:S(2)}) %collective-permute-start.8) | collective-permute-done | bytes 540704 | tf_op jit(solution)/shard_map/ppermute | solution.py:244
  42.4 2.9 %collective-permute-done.7.refs_6_ = bf16[2,528,256]{2,1,0:T(8,128)(2,1)S(1)} collective-permute-done((bf16[2,528,256]{2,1,0:T(8,128)(2,1)S(1)}, bf16[2,528,256]{2,1,0:T(8,128)(2,1)S(1)}, u32[]{:S(2)}, u32[]{:S(2)}) %collective-permute-start.7) | collective-permute-done | bytes 540704 | tf_op jit(solution)/shard_map/ppermute | solution.py:244
  45.3 5.3 %norm_qkv.1 = (bf16[512,128]{1,0:T(8,128)(2,1)S(1)}, bf16[1024,128]{1,0:T(8,128)(2,1)S(1)}) custom-call(s32[16]{0:T(128)S(1)} %fusion.1.blk_ref, bf16[2,528,256]{2,1,0:T(8,128)(2,1)S(1)} %pad_maximum_fusion.1.refs_0_, bf16[2,528,256]{2,1,0:T(8,128)(2,1)S(1)} %pad_maximum_fusion.2.refs_1_, bf16[2,528,256]{2,1,0:T(8,128)(2,1)S(1)} %collective-permute-done.3.refs_2_, ...), custom_call_target="tpu_custom_call" | custom-call | flops 1610612736 | bytes 8388608 | tf_op jit(solution)/shard_map/norm_qkv/pallas_call | solution.py:80
  50.5 3.5 %collective-permute-start.9 = (bf16[1024,128]{1,0:T(8,128)(2,1)S(1)}, bf16[1024,128]{1,0:T(8,128)(2,1)S(1)}, u32[]{:S(2)}, u32[]{:S(2)}) collective-permute-start(bf16[1024,128]{1,0:T(8,128)(2,1)S(1)} %get-tuple-element.25.refs_0_), channel_id=1, source_target_pairs={{0,32},{32,64},{64,96},{96,128},{128,160},{160,192},{192,224},{224... | collective-permute-start | bytes 786440 | tf_op jit(solution)/shard_map/ppermute | solution.py:273
  54.2 9.5 %collective-permute-start.13 = (bf16[1024,128]{1,0:T(8,128)(2,1)S(1)}, bf16[1024,128]{1,0:T(8,128)(2,1)S(1)}, u32[]{:S(2)}, u32[]{:S(2)}) collective-permute-start(bf16[1024,128]{1,0:T(8,128)(2,1)S(1)} %get-tuple-element.25.refs_0_), channel_id=1, source_target_pairs={{0,480},{32,0},{64,32},{96,64},{128,96},{160,128},{192,160},{224,1... | collective-permute-start | bytes 786440 | tf_op jit(solution)/shard_map/ppermute | solution.py:273
  65.4 6.5 %collective-permute-start.10 = (bf16[512,128]{1,0:T(8,128)(2,1)S(1)}, bf16[512,128]{1,0:T(8,128)(2,1)S(1)}, u32[]{:S(2)}, u32[]{:S(2)}) collective-permute-start(bf16[512,128]{1,0:T(8,128)(2,1)S(1)} %get-tuple-element.27), channel_id=1, source_target_pairs={{0,16},{16,0},{1,17},{17,1},{2,18},{18,2},{3,19},{19,3},{4,20},{20... | collective-permute-start | bytes 393224 | tf_op jit(solution)/shard_map/ppermute | solution.py:277
  73.8 4.6 %collective-permute-start.15 = (bf16[1024,128]{1,0:T(8,128)(2,1)S(1)}, bf16[1024,128]{1,0:T(8,128)(2,1)S(1)}, u32[]{:S(2)}, u32[]{:S(2)}) collective-permute-start(bf16[1024,128]{1,0:T(8,128)(2,1)S(1)} %collective-permute-done.13.refs_1_), channel_id=1, source_target_pairs={{0,480},{32,0},{64,32},{96,64},{128,96},{160,128},{192,160},{224,1... | collective-permute-start | bytes 786440 | tf_op jit(solution)/shard_map/ppermute | solution.py:273
  78.5 2.5 %attend.9.refs_2_ = f32[2,136,512]{2,1,0:T(8,128)S(1)} custom-call(s32[16]{0:T(128)S(1)} %compare_select_fusion.7.meta_ref, bf16[2,512,128]{2,1,0:T(8,128)(2,1)S(1)} %pad_maximum_fusion.6.q_ref, s32[2,1,512]{2,1,0:T(1,128)S(1)} %broadcast_in_dim.132.lo_ref, s32[2,1,512]{2,1,0:T(1,128)S(1)} %broadcast_in_dim.135.hi_ref, ...), custom_call_target="tpu_custom_call" | custom-call | flops 268435456 | bytes 2097152 | tf_op jit(solution)/shard_map/attend/pallas_call | solution.py:183
  84.8 4.6 %collective-permute-start.17 = (bf16[1024,128]{1,0:T(8,128)(2,1)S(1)}, bf16[1024,128]{1,0:T(8,128)(2,1)S(1)}, u32[]{:S(2)}, u32[]{:S(2)}) collective-permute-start(bf16[1024,128]{1,0:T(8,128)(2,1)S(1)} %collective-permute-done.15.refs_1_), channel_id=1, source_target_pairs={{0,480},{32,0},{64,32},{96,64},{128,96},{160,128},{192,160},{224,1... | collective-permute-start | bytes 786440 | tf_op jit(solution)/shard_map/ppermute | solution.py:273
  90.1 3.0 %collective-permute-done.12.refs_0_ = bf16[1024,128]{1,0:T(8,128)(2,1)S(1)} collective-permute-done((bf16[1024,128]{1,0:T(8,128)(2,1)S(1)}, bf16[1024,128]{1,0:T(8,128)(2,1)S(1)}, u32[]{:S(2)}, u32[]{:S(2)}) %collective-permute-start.12) | collective-permute-done | bytes 262176 | tf_op jit(solution)/shard_map/ppermute | solution.py:273
  95.0 4.6 %collective-permute-start.19 = (bf16[1024,128]{1,0:T(8,128)(2,1)S(1)}, bf16[1024,128]{1,0:T(8,128)(2,1)S(1)}, u32[]{:S(2)}, u32[]{:S(2)}) collective-permute-start(bf16[1024,128]{1,0:T(8,128)(2,1)S(1)} %collective-permute-done.17.refs_1_), channel_id=1, source_target_pairs={{0,480},{32,0},{64,32},{96,64},{128,96},{160,128},{192,160},{224,1... | collective-permute-start | bytes 786440 | tf_op jit(solution)/shard_map/ppermute | solution.py:273
  104.2 4.6 %collective-permute-start.21 = (bf16[1024,128]{1,0:T(8,128)(2,1)S(1)}, bf16[1024,128]{1,0:T(8,128)(2,1)S(1)}, u32[]{:S(2)}, u32[]{:S(2)}) collective-permute-start(bf16[1024,128]{1,0:T(8,128)(2,1)S(1)} %collective-permute-done.19.refs_1_), channel_id=1, source_target_pairs={{0,480},{32,0},{64,32},{96,64},{128,96},{160,128},{192,160},{224,1... | collective-permute-start | bytes 786440 | tf_op jit(solution)/shard_map/ppermute | solution.py:273
  112.5 4.6 %collective-permute-start.23 = (bf16[1024,128]{1,0:T(8,128)(2,1)S(1)}, bf16[1024,128]{1,0:T(8,128)(2,1)S(1)}, u32[]{:S(2)}, u32[]{:S(2)}) collective-permute-start(bf16[1024,128]{1,0:T(8,128)(2,1)S(1)} %collective-permute-done.21.refs_1_), channel_id=1, source_target_pairs={{0,480},{32,0},{64,32},{96,64},{128,96},{160,128},{192,160},{224,1... | collective-permute-start | bytes 786440 | tf_op jit(solution)/shard_map/ppermute | solution.py:273
  120.8 4.6 %collective-permute-start.24 = (bf16[1024,128]{1,0:T(8,128)(2,1)S(1)}, bf16[1024,128]{1,0:T(8,128)(2,1)S(1)}, u32[]{:S(2)}, u32[]{:S(2)}) collective-permute-start(bf16[1024,128]{1,0:T(8,128)(2,1)S(1)} %collective-permute-done.23.refs_1_), channel_id=1, source_target_pairs={{0,480},{32,0},{64,32},{96,64},{128,96},{160,128},{192,160},{224,1... | collective-permute-start | bytes 786440 | tf_op jit(solution)/shard_map/ppermute | solution.py:273
  130.7 4.9 %collective-permute-done.22.refs_0_ = bf16[1024,128]{1,0:T(8,128)(2,1)S(1)} collective-permute-done((bf16[1024,128]{1,0:T(8,128)(2,1)S(1)}, bf16[1024,128]{1,0:T(8,128)(2,1)S(1)}, u32[]{:S(2)}, u32[]{:S(2)}) %collective-permute-start.22) | collective-permute-done | bytes 262176 | tf_op jit(solution)/shard_map/ppermute | solution.py:273
  136.1 9.1 %collective-permute-start.25 = (f32[136,512]{1,0:T(8,128)S(1)}, f32[136,512]{1,0:T(8,128)S(1)}, u32[]{:S(2)}, u32[]{:S(2)}) collective-permute-start(f32[136,512]{1,0:T(8,128)S(1)} %get-tuple-element.44), channel_id=1, source_target_pairs={{0,16},{16,0},{1,17},{17,1},{2,18},{18,2},{3,19},{19,3},{4,20},{20... | collective-permute-start | bytes 835592 | tf_op jit(solution)/shard_map/ppermute | solution.py:288
  (78 shorter events, 41.2 us)
Async XLA Ops:
  1.6 15.6 %collective-permute-start.1 = (bf16[528,256]{1,0:T(8,128)(2,1)S(1)}, bf16[528,256]{1,0:T(8,128)(2,1)S(1)}, u32[]{:S(2)}, u32[]{:S(2)}) collective-permute-start(bf16[528,256]{1,0:T(8,128)(2,1)S(1)} %get-tuple-element.61), channel_id=1, source_target_pairs={{0,3},{1,0},{2,1},{3,2},{4,7},{5,4},{6,5},{7,6},{8,11},{9,8},{10,9... | collective-permute-start | bytes 811016 | tf_op jit(solution)/shard_map/ppermute | solution.py:242
  7.1 10.1 %collective-permute-start.2 = (bf16[528,256]{1,0:T(8,128)(2,1)S(1)}, bf16[528,256]{1,0:T(8,128)(2,1)S(1)}, u32[]{:S(2)}, u32[]{:S(2)}) collective-permute-start(bf16[528,256]{1,0:T(8,128)(2,1)S(1)} %get-tuple-element.61), channel_id=1, source_target_pairs={{0,2},{1,3},{2,0},{3,1},{4,6},{5,7},{6,4},{7,5},{8,10},{9,11},{10,... | collective-permute-start | bytes 811016 | tf_op jit(solution)/shard_map/ppermute | solution.py:242
  9.4 12.3 %collective-permute-start = (bf16[528,256]{1,0:T(8,128)(2,1)S(1)}, bf16[528,256]{1,0:T(8,128)(2,1)S(1)}, u32[]{:S(2)}, u32[]{:S(2)}) collective-permute-start(bf16[528,256]{1,0:T(8,128)(2,1)S(1)} %get-tuple-element.61), channel_id=1, source_target_pairs={{0,1},{1,2},{2,3},{3,0},{4,5},{5,6},{6,7},{7,4},{8,9},{9,10},{10,1... | collective-permute-start | bytes 811016 | tf_op jit(solution)/shard_map/ppermute | solution.py:242
  17.3 13.0 %collective-permute-start.6 = (bf16[2,528,256]{2,1,0:T(8,128)(2,1)S(1)}, bf16[2,528,256]{2,1,0:T(8,128)(2,1)S(1)}, u32[]{:S(2)}, u32[]{:S(2)}) collective-permute-start(bf16[2,528,256]{2,1,0:T(8,128)(2,1)S(1)} %pad_maximum_fusion.2.refs_1_), channel_id=1, source_target_pairs={{0,12},{1,13},{2,14},{3,15},{4,0},{5,1},{6,2},{7,3},{8,4},{9,5},{1... | collective-permute-start | bytes 1622024 | tf_op jit(solution)/shard_map/ppermute | solution.py:244
  21.8 11.9 %collective-permute-start.3 = (bf16[2,528,256]{2,1,0:T(8,128)(2,1)S(1)}, bf16[2,528,256]{2,1,0:T(8,128)(2,1)S(1)}, u32[]{:S(2)}, u32[]{:S(2)}) collective-permute-start(bf16[2,528,256]{2,1,0:T(8,128)(2,1)S(1)} %pad_maximum_fusion.1.refs_0_), channel_id=1, source_target_pairs={{0,4},{1,5},{2,6},{3,7},{4,8},{5,9},{6,10},{7,11},{8,12},{9,13},{1... | collective-permute-start | bytes 1622024 | tf_op jit(solution)/shard_map/ppermute | solution.py:244
  23.8 15.4 %collective-permute-start.4 = (bf16[2,528,256]{2,1,0:T(8,128)(2,1)S(1)}, bf16[2,528,256]{2,1,0:T(8,128)(2,1)S(1)}, u32[]{:S(2)}, u32[]{:S(2)}) collective-permute-start(bf16[2,528,256]{2,1,0:T(8,128)(2,1)S(1)} %pad_maximum_fusion.2.refs_1_), channel_id=1, source_target_pairs={{0,4},{1,5},{2,6},{3,7},{4,8},{5,9},{6,10},{7,11},{8,12},{9,13},{1... | collective-permute-start | bytes 1622024 | tf_op jit(solution)/shard_map/ppermute | solution.py:244
  25.9 13.3 %collective-permute-start.5 = (bf16[2,528,256]{2,1,0:T(8,128)(2,1)S(1)}, bf16[2,528,256]{2,1,0:T(8,128)(2,1)S(1)}, u32[]{:S(2)}, u32[]{:S(2)}) collective-permute-start(bf16[2,528,256]{2,1,0:T(8,128)(2,1)S(1)} %pad_maximum_fusion.1.refs_0_), channel_id=1, source_target_pairs={{0,12},{1,13},{2,14},{3,15},{4,0},{5,1},{6,2},{7,3},{8,4},{9,5},{1... | collective-permute-start | bytes 1622024 | tf_op jit(solution)/shard_map/ppermute | solution.py:244
  30.3 12.1 %collective-permute-start.8 = (bf16[2,528,256]{2,1,0:T(8,128)(2,1)S(1)}, bf16[2,528,256]{2,1,0:T(8,128)(2,1)S(1)}, u32[]{:S(2)}, u32[]{:S(2)}) collective-permute-start(bf16[2,528,256]{2,1,0:T(8,128)(2,1)S(1)} %collective-permute-done.6.refs_5_), channel_id=1, source_target_pairs={{0,12},{1,13},{2,14},{3,15},{4,0},{5,1},{6,2},{7,3},{8,4},{9,5},{1... | collective-permute-start | bytes 1622024 | tf_op jit(solution)/shard_map/ppermute | solution.py:244
  33.7 11.6 %collective-permute-start.7 = (bf16[2,528,256]{2,1,0:T(8,128)(2,1)S(1)}, bf16[2,528,256]{2,1,0:T(8,128)(2,1)S(1)}, u32[]{:S(2)}, u32[]{:S(2)}) collective-permute-start(bf16[2,528,256]{2,1,0:T(8,128)(2,1)S(1)} %collective-permute-done.3.refs_2_), channel_id=1, source_target_pairs={{0,4},{1,5},{2,6},{3,7},{4,8},{5,9},{6,10},{7,11},{8,12},{9,13},{1... | collective-permute-start | bytes 1622024 | tf_op jit(solution)/shard_map/ppermute | solution.py:244
  50.5 14.9 %collective-permute-start.9 = (bf16[1024,128]{1,0:T(8,128)(2,1)S(1)}, bf16[1024,128]{1,0:T(8,128)(2,1)S(1)}, u32[]{:S(2)}, u32[]{:S(2)}) collective-permute-start(bf16[1024,128]{1,0:T(8,128)(2,1)S(1)} %get-tuple-element.25.refs_0_), channel_id=1, source_target_pairs={{0,32},{32,64},{64,96},{96,128},{128,160},{160,192},{192,224},{224... | collective-permute-start | bytes 786440 | tf_op jit(solution)/shard_map/ppermute | solution.py:273
  54.2 19.6 %collective-permute-start.13 = (bf16[1024,128]{1,0:T(8,128)(2,1)S(1)}, bf16[1024,128]{1,0:T(8,128)(2,1)S(1)}, u32[]{:S(2)}, u32[]{:S(2)}) collective-permute-start(bf16[1024,128]{1,0:T(8,128)(2,1)S(1)} %get-tuple-element.25.refs_0_), channel_id=1, source_target_pairs={{0,480},{32,0},{64,32},{96,64},{128,96},{160,128},{192,160},{224,1... | collective-permute-start | bytes 786440 | tf_op jit(solution)/shard_map/ppermute | solution.py:273
  65.4 13.0 %collective-permute-start.10 = (bf16[512,128]{1,0:T(8,128)(2,1)S(1)}, bf16[512,128]{1,0:T(8,128)(2,1)S(1)}, u32[]{:S(2)}, u32[]{:S(2)}) collective-permute-start(bf16[512,128]{1,0:T(8,128)(2,1)S(1)} %get-tuple-element.27), channel_id=1, source_target_pairs={{0,16},{16,0},{1,17},{17,1},{2,18},{18,2},{3,19},{19,3},{4,20},{20... | collective-permute-start | bytes 393224 | tf_op jit(solution)/shard_map/ppermute | solution.py:277
  71.9 11.0 %collective-permute-start.11 = (bf16[1024,128]{1,0:T(8,128)(2,1)S(1)}, bf16[1024,128]{1,0:T(8,128)(2,1)S(1)}, u32[]{:S(2)}, u32[]{:S(2)}) collective-permute-start(bf16[1024,128]{1,0:T(8,128)(2,1)S(1)} %collective-permute-done.9.refs_0_), channel_id=1, source_target_pairs={{0,32},{32,64},{64,96},{96,128},{128,160},{160,192},{192,224},{224... | collective-permute-start | bytes 786440 | tf_op jit(solution)/shard_map/ppermute | solution.py:273
  73.8 11.0 %collective-permute-start.15 = (bf16[1024,128]{1,0:T(8,128)(2,1)S(1)}, bf16[1024,128]{1,0:T(8,128)(2,1)S(1)}, u32[]{:S(2)}, u32[]{:S(2)}) collective-permute-start(bf16[1024,128]{1,0:T(8,128)(2,1)S(1)} %collective-permute-done.13.refs_1_), channel_id=1, source_target_pairs={{0,480},{32,0},{64,32},{96,64},{128,96},{160,128},{192,160},{224,1... | collective-permute-start | bytes 786440 | tf_op jit(solution)/shard_map/ppermute | solution.py:273
  82.9 10.1 %collective-permute-start.12 = (bf16[1024,128]{1,0:T(8,128)(2,1)S(1)}, bf16[1024,128]{1,0:T(8,128)(2,1)S(1)}, u32[]{:S(2)}, u32[]{:S(2)}) collective-permute-start(bf16[1024,128]{1,0:T(8,128)(2,1)S(1)} %collective-permute-done.11.refs_0_), channel_id=1, source_target_pairs={{0,32},{32,64},{64,96},{96,128},{128,160},{160,192},{192,224},{224... | collective-permute-start | bytes 786440 | tf_op jit(solution)/shard_map/ppermute | solution.py:273
  84.8 10.1 %collective-permute-start.17 = (bf16[1024,128]{1,0:T(8,128)(2,1)S(1)}, bf16[1024,128]{1,0:T(8,128)(2,1)S(1)}, u32[]{:S(2)}, u32[]{:S(2)}) collective-permute-start(bf16[1024,128]{1,0:T(8,128)(2,1)S(1)} %collective-permute-done.15.refs_1_), channel_id=1, source_target_pairs={{0,480},{32,0},{64,32},{96,64},{128,96},{160,128},{192,160},{224,1... | collective-permute-start | bytes 786440 | tf_op jit(solution)/shard_map/ppermute | solution.py:273
  93.0 9.2 %collective-permute-start.14 = (bf16[1024,128]{1,0:T(8,128)(2,1)S(1)}, bf16[1024,128]{1,0:T(8,128)(2,1)S(1)}, u32[]{:S(2)}, u32[]{:S(2)}) collective-permute-start(bf16[1024,128]{1,0:T(8,128)(2,1)S(1)} %collective-permute-done.12.refs_0_), channel_id=1, source_target_pairs={{0,32},{32,64},{64,96},{96,128},{128,160},{160,192},{192,224},{224... | collective-permute-start | bytes 786440 | tf_op jit(solution)/shard_map/ppermute | solution.py:273
  95.0 9.2 %collective-permute-start.19 = (bf16[1024,128]{1,0:T(8,128)(2,1)S(1)}, bf16[1024,128]{1,0:T(8,128)(2,1)S(1)}, u32[]{:S(2)}, u32[]{:S(2)}) collective-permute-start(bf16[1024,128]{1,0:T(8,128)(2,1)S(1)} %collective-permute-done.17.refs_1_), channel_id=1, source_target_pairs={{0,480},{32,0},{64,32},{96,64},{128,96},{160,128},{192,160},{224,1... | collective-permute-start | bytes 786440 | tf_op jit(solution)/shard_map/ppermute | solution.py:273
  102.3 8.3 %collective-permute-start.16 = (bf16[1024,128]{1,0:T(8,128)(2,1)S(1)}, bf16[1024,128]{1,0:T(8,128)(2,1)S(1)}, u32[]{:S(2)}, u32[]{:S(2)}) collective-permute-start(bf16[1024,128]{1,0:T(8,128)(2,1)S(1)} %collective-permute-done.14.refs_0_), channel_id=1, source_target_pairs={{0,32},{32,64},{64,96},{96,128},{128,160},{160,192},{192,224},{224... | collective-permute-start | bytes 786440 | tf_op jit(solution)/shard_map/ppermute | solution.py:273
  110.6 8.3 %collective-permute-start.18 = (bf16[1024,128]{1,0:T(8,128)(2,1)S(1)}, bf16[1024,128]{1,0:T(8,128)(2,1)S(1)}, u32[]{:S(2)}, u32[]{:S(2)}) collective-permute-start(bf16[1024,128]{1,0:T(8,128)(2,1)S(1)} %collective-permute-done.16.refs_0_), channel_id=1, source_target_pairs={{0,32},{32,64},{64,96},{96,128},{128,160},{160,192},{192,224},{224... | collective-permute-start | bytes 786440 | tf_op jit(solution)/shard_map/ppermute | solution.py:273
  118.9 8.3 %collective-permute-start.20 = (bf16[1024,128]{1,0:T(8,128)(2,1)S(1)}, bf16[1024,128]{1,0:T(8,128)(2,1)S(1)}, u32[]{:S(2)}, u32[]{:S(2)}) collective-permute-start(bf16[1024,128]{1,0:T(8,128)(2,1)S(1)} %collective-permute-done.18.refs_0_), channel_id=1, source_target_pairs={{0,32},{32,64},{64,96},{96,128},{128,160},{160,192},{192,224},{224... | collective-permute-start | bytes 786440 | tf_op jit(solution)/shard_map/ppermute | solution.py:273
  120.8 9.0 %collective-permute-start.24 = (bf16[1024,128]{1,0:T(8,128)(2,1)S(1)}, bf16[1024,128]{1,0:T(8,128)(2,1)S(1)}, u32[]{:S(2)}, u32[]{:S(2)}) collective-permute-start(bf16[1024,128]{1,0:T(8,128)(2,1)S(1)} %collective-permute-done.23.refs_1_), channel_id=1, source_target_pairs={{0,480},{32,0},{64,32},{96,64},{128,96},{160,128},{192,160},{224,1... | collective-permute-start | bytes 786440 | tf_op jit(solution)/shard_map/ppermute | solution.py:273
  127.2 8.3 %collective-permute-start.22 = (bf16[1024,128]{1,0:T(8,128)(2,1)S(1)}, bf16[1024,128]{1,0:T(8,128)(2,1)S(1)}, u32[]{:S(2)}, u32[]{:S(2)}) collective-permute-start(bf16[1024,128]{1,0:T(8,128)(2,1)S(1)} %collective-permute-done.20.refs_0_), channel_id=1, source_target_pairs={{0,32},{32,64},{64,96},{96,128},{128,160},{160,192},{192,224},{224... | collective-permute-start | bytes 786440 | tf_op jit(solution)/shard_map/ppermute | solution.py:273
  136.1 10.3 %collective-permute-start.25 = (f32[136,512]{1,0:T(8,128)S(1)}, f32[136,512]{1,0:T(8,128)S(1)}, u32[]{:S(2)}, u32[]{:S(2)}) collective-permute-start(f32[136,512]{1,0:T(8,128)S(1)} %get-tuple-element.44), channel_id=1, source_target_pairs={{0,16},{16,0},{1,17},{17,1},{2,18},{18,2},{3,19},{19,3},{4,20},{20... | collective-permute-start | bytes 835592 | tf_op jit(solution)/shard_map/ppermute | solution.py:288
  (6 other events, 29.7 us)

commit v5 on v4

--- a/solution.py
+++ b/solution.py
@@ -44,25 +44,40 @@
 
 
 def qkv_kernel(blk_ref, *refs):
-    sets, (w_ref, cos_ref, sin_ref, q_ref, kv_ref, nrm) = refs[:8], refs[8:]
+    sets = refs[:8]
+    w_ref, cos_ref, sin_ref, q_ref, kv_ref, scale_ref = refs[8:14]
+    parts = refs[14:]
     tile = 64
 
-    def norm_rows(i, carry):
-        r = pl.multiple_of(i * tile, tile)
+    def squares(i, carry):
+        r = pl.ds(pl.multiple_of(i * tile, tile), tile)
         acc = jnp.zeros((tile, FEAT), jnp.float32)
         for b in range(16):
-            x = sets[b // 2][b % 2, pl.ds(r, tile), :].astype(jnp.float32)
+            x = sets[b // 2][b % 2, r, :].astype(jnp.float32)
             acc = acc + x * x
         scale = lax.rsqrt(jnp.sum(acc, axis=1, keepdims=True) / D + EPS)
-        for b in range(16):
-            x = sets[b // 2][b % 2, pl.ds(r, tile), :].astype(jnp.float32)
-            gain = sets[b // 2][b % 2, ROWS : ROWS + 1, :].astype(jnp.float32)
-            col = pl.multiple_of(blk_ref[b] * FEAT, FEAT)
-            nrm[pl.ds(r, tile), pl.ds(col, FEAT)] = (x * scale * gain).astype(jnp.bfloat16)
+        scale_ref[r, :] = jnp.broadcast_to(scale, (tile, HD))
         return carry
 
-    lax.fori_loop(0, ROWS // tile, norm_rows, 0)
-    out = jnp.dot(nrm[...], w_ref[...], preferred_element_type=jnp.float32)
+    lax.fori_loop(0, ROWS // tile, squares, 0)
+    scale = jnp.concatenate([scale_ref[...], scale_ref[...]], axis=1)
+
+    def fill(g):
+        for j in range(4):
+            blocks = sets[2 * g + j // 2]
+            x = blocks[j % 2, :ROWS, :].astype(jnp.float32)
+            gain = blocks[j % 2, ROWS : ROWS + 1, :].astype(jnp.float32)
+            parts[g][:, j * FEAT : (j + 1) * FEAT] = (x * scale * gain).astype(jnp.bfloat16)
+
+    fill(0)
+    out = None
+    for g in range(4):
+        rows = [pl.multiple_of(blk_ref[4 * g + j] * FEAT, FEAT) for j in range(4)]
+        w = jnp.concatenate([w_ref[pl.ds(row, FEAT), :] for row in rows], axis=0)
+        part = jnp.dot(parts[g][...], w, preferred_element_type=jnp.float32)
+        if g < 3:
+            fill(g + 1)
+        out = part if g == 0 else out + part
     cosine, sine = cos_ref[...], sin_ref[...]
 
     def rotate(v):
@@ -85,7 +100,8 @@
         ),
         in_specs=[pl.BlockSpec(memory_space=pltpu.SMEM)] + [vmem] * 11,
         out_specs=(vmem, vmem),
-        scratch_shapes=[pltpu.VMEM((ROWS, D), jnp.bfloat16)],
+        scratch_shapes=[pltpu.VMEM((ROWS, HD), jnp.float32)]
+        + [pltpu.VMEM((ROWS, 4 * FEAT), jnp.bfloat16)] * 4,
         compiler_params=pltpu.CompilerParams(vmem_limit_bytes=20 * 2**20),
         cost_estimate=pl.CostEstimate(
             flops=2 * ROWS * D * 3 * HD, bytes_accessed=8 * 2**20, transcendentals=0

time: 148 us -> 147 us (level)
  no operation moved by 1% of the time
where the time goes in v5:
time: 147 us; the launch traced here: 146 us
  starting transfers between devices  98 us (67%)
  waiting for transfers between devices  27.1 us (18%)
  Pallas kernels  13.1 us (9%)
  other arithmetic  4.76 us (3%)
  local copies, waits for them, and re-layouts  2.79 us (2%)
    ppermute x15, starting transfers between devices, body(): z_step = lambda v, d: lax.ppermute(v, 'z', ring(NZ, d))  53.9 us
    ppermute x6, starting transfers between devices, body(): far = lambda v, d: lax.ppermute(v, plane, plane_perm(d, False))  18.1 us
    ppermute x15, waiting for transfers between devices, body(): z_step = lambda v, d: lax.ppermute(v, 'z', ring(NZ, d))  16.8 us
    ppermute x3, starting transfers between devices, body(): lax.ppermute(mine, plane, plane_perm(d, True))  10.3 us
    ppermute x6, waiting for transfers between devices, body(): far = lambda v, d: lax.ppermute(v, plane, plane_perm(d, False))  9.18 us
    ppermute x1, starting transfers between devices, body(): return merge(own, lax.ppermute(other, 'core', ring(2, 1)))  9.11 us
    pallas_call x9, Pallas kernels, attend(): pl.pallas_call(functools.partial(attend_kernel, offs, not state, last_cal...  8.05 us
    ppermute x1, starting transfers between devices, body(): q2 = jnp.stack([q, lax.ppermute(q, 'core', ring(2, 1))], axis=0)  6.62 us
  transfers between devices with their start and end apart: 26, of which 12 were waited for; matrix products, arithmetic and copies ran while one was open for 4% of the time, Pallas kernels for 5%

profile of v5, /device:TPU:1, one launch (start us, length us, event | category | flops | bytes accessed | tf_op | source)
XLA Modules:
  0.0 146.4 jit_solution(7219516994264803072)
XLA Ops:
  1.6 5.5 %collective-permute-start.1 = (bf16[528,256]{1,0:T(8,128)(2,1)S(1)}, bf16[528,256]{1,0:T(8,128)(2,1)S(1)}, u32[]{:S(2)}, u32[]{:S(2)}) collective-permute-start(bf16[528,256]{1,0:T(8,128)(2,1)S(1)} %get-tuple-element.61), channel_id=1, source_target_pairs={{0,3},{1,0},{2,1},{3,2},{4,7},{5,4},{6,5},{7,6},{8,11},{9,8},{10,9... | collective-permute-start | bytes 811016 | tf_op jit(solution)/shard_map/ppermute | solution.py:258
  7.1 2.3 %collective-permute-start.2 = (bf16[528,256]{1,0:T(8,128)(2,1)S(1)}, bf16[528,256]{1,0:T(8,128)(2,1)S(1)}, u32[]{:S(2)}, u32[]{:S(2)}) collective-permute-start(bf16[528,256]{1,0:T(8,128)(2,1)S(1)} %get-tuple-element.61), channel_id=1, source_target_pairs={{0,2},{1,3},{2,0},{3,1},{4,6},{5,7},{6,4},{7,5},{8,10},{9,11},{10,... | collective-permute-start | bytes 811016 | tf_op jit(solution)/shard_map/ppermute | solution.py:258
  9.4 2.6 %collective-permute-start = (bf16[528,256]{1,0:T(8,128)(2,1)S(1)}, bf16[528,256]{1,0:T(8,128)(2,1)S(1)}, u32[]{:S(2)}, u32[]{:S(2)}) collective-permute-start(bf16[528,256]{1,0:T(8,128)(2,1)S(1)} %get-tuple-element.61), channel_id=1, source_target_pairs={{0,1},{1,2},{2,3},{3,0},{4,5},{5,6},{6,7},{7,4},{8,9},{9,10},{10,1... | collective-permute-start | bytes 811016 | tf_op jit(solution)/shard_map/ppermute | solution.py:258
  13.6 2.1 %slice_bitcast_fusion.2 = (bf16[4096,128]{1,0:T(8,128)(2,1)S(1)}, bf16[4096,128]{1,0:T(8,128)(2,1)S(1)}, bf16[4096,128]{1,0:T(8,128)(2,1)S(1)}) fusion(bf16[3,4096,128]{2,1,0:T(8,128)(2,1)} %param.10), kind=kLoop, calls=%fused_computation.3 | loop fusion | bytes 6291456 | tf_op jit(solution)/shard_map/squeeze | solution.py:285
  17.3 4.4 %collective-permute-start.6 = (bf16[2,528,256]{2,1,0:T(8,128)(2,1)S(1)}, bf16[2,528,256]{2,1,0:T(8,128)(2,1)S(1)}, u32[]{:S(2)}, u32[]{:S(2)}) collective-permute-start(bf16[2,528,256]{2,1,0:T(8,128)(2,1)S(1)} %pad_maximum_fusion.2.refs_1_), channel_id=1, source_target_pairs={{0,12},{1,13},{2,14},{3,15},{4,0},{5,1},{6,2},{7,3},{8,4},{9,5},{1... | collective-permute-start | bytes 1622024 | tf_op jit(solution)/shard_map/ppermute | solution.py:260
  23.8 2.1 %collective-permute-start.4 = (bf16[2,528,256]{2,1,0:T(8,128)(2,1)S(1)}, bf16[2,528,256]{2,1,0:T(8,128)(2,1)S(1)}, u32[]{:S(2)}, u32[]{:S(2)}) collective-permute-start(bf16[2,528,256]{2,1,0:T(8,128)(2,1)S(1)} %pad_maximum_fusion.2.refs_1_), channel_id=1, source_target_pairs={{0,4},{1,5},{2,6},{3,7},{4,8},{5,9},{6,10},{7,11},{8,12},{9,13},{1... | collective-permute-start | bytes 1622024 | tf_op jit(solution)/shard_map/ppermute | solution.py:260
  25.9 4.4 %collective-permute-start.5 = (bf16[2,528,256]{2,1,0:T(8,128)(2,1)S(1)}, bf16[2,528,256]{2,1,0:T(8,128)(2,1)S(1)}, u32[]{:S(2)}, u32[]{:S(2)}) collective-permute-start(bf16[2,528,256]{2,1,0:T(8,128)(2,1)S(1)} %pad_maximum_fusion.1.refs_0_), channel_id=1, source_target_pairs={{0,12},{1,13},{2,14},{3,15},{4,0},{5,1},{6,2},{7,3},{8,4},{9,5},{1... | collective-permute-start | bytes 1622024 | tf_op jit(solution)/shard_map/ppermute | solution.py:260
  30.3 3.4 %collective-permute-start.8 = (bf16[2,528,256]{2,1,0:T(8,128)(2,1)S(1)}, bf16[2,528,256]{2,1,0:T(8,128)(2,1)S(1)}, u32[]{:S(2)}, u32[]{:S(2)}) collective-permute-start(bf16[2,528,256]{2,1,0:T(8,128)(2,1)S(1)} %collective-permute-done.6.refs_5_), channel_id=1, source_target_pairs={{0,12},{1,13},{2,14},{3,15},{4,0},{5,1},{6,2},{7,3},{8,4},{9,5},{1... | collective-permute-start | bytes 1622024 | tf_op jit(solution)/shard_map/ppermute | solution.py:260
  36.1 3.1 %collective-permute-done.4.refs_3_ = bf16[2,528,256]{2,1,0:T(8,128)(2,1)S(1)} collective-permute-done((bf16[2,528,256]{2,1,0:T(8,128)(2,1)S(1)}, bf16[2,528,256]{2,1,0:T(8,128)(2,1)S(1)}, u32[]{:S(2)}, u32[]{:S(2)}) %collective-permute-start.4) | collective-permute-done | bytes 540704 | tf_op jit(solution)/shard_map/ppermute | solution.py:260
  39.2 3.2 %collective-permute-done.8.refs_7_ = bf16[2,528,256]{2,1,0:T(8,128)(2,1)S(1)} collective-permute-done((bf16[2,528,256]{2,1,0:T(8,128)(2,1)S(1)}, bf16[2,528,256]{2,1,0:T(8,128)(2,1)S(1)}, u32[]{:S(2)}, u32[]{:S(2)}) %collective-permute-start.8) | collective-permute-done | bytes 540704 | tf_op jit(solution)/shard_map/ppermute | solution.py:260
  42.4 2.9 %collective-permute-done.7.refs_6_ = bf16[2,528,256]{2,1,0:T(8,128)(2,1)S(1)} collective-permute-done((bf16[2,528,256]{2,1,0:T(8,128)(2,1)S(1)}, bf16[2,528,256]{2,1,0:T(8,128)(2,1)S(1)}, u32[]{:S(2)}, u32[]{:S(2)}) %collective-permute-start.7) | collective-permute-done | bytes 540704 | tf_op jit(solution)/shard_map/ppermute | solution.py:260
  45.3 4.3 %norm_qkv.1 = (bf16[512,128]{1,0:T(8,128)(2,1)S(1)}, bf16[1024,128]{1,0:T(8,128)(2,1)S(1)}) custom-call(s32[16]{0:T(128)S(1)} %fusion.1.blk_ref, bf16[2,528,256]{2,1,0:T(8,128)(2,1)S(1)} %pad_maximum_fusion.1.refs_0_, bf16[2,528,256]{2,1,0:T(8,128)(2,1)S(1)} %pad_maximum_fusion.2.refs_1_, bf16[2,528,256]{2,1,0:T(8,128)(2,1)S(1)} %collective-permute-done.3.refs_2_, ...), custom_call_target="tpu_custom_call" | custom-call | flops 1610612736 | bytes 8388608 | tf_op jit(solution)/shard_map/norm_qkv/pallas_call | solution.py:95
  49.6 3.5 %collective-permute-start.9 = (bf16[1024,128]{1,0:T(8,128)(2,1)S(1)}, bf16[1024,128]{1,0:T(8,128)(2,1)S(1)}, u32[]{:S(2)}, u32[]{:S(2)}) collective-permute-start(bf16[1024,128]{1,0:T(8,128)(2,1)S(1)} %get-tuple-element.25.refs_0_), channel_id=1, source_target_pairs={{0,32},{32,64},{64,96},{96,128},{128,160},{160,192},{192,224},{224... | collective-permute-start | bytes 786440 | tf_op jit(solution)/shard_map/ppermute | solution.py:289
  53.2 9.5 %collective-permute-start.13 = (bf16[1024,128]{1,0:T(8,128)(2,1)S(1)}, bf16[1024,128]{1,0:T(8,128)(2,1)S(1)}, u32[]{:S(2)}, u32[]{:S(2)}) collective-permute-start(bf16[1024,128]{1,0:T(8,128)(2,1)S(1)} %get-tuple-element.25.refs_0_), channel_id=1, source_target_pairs={{0,480},{32,0},{64,32},{96,64},{128,96},{160,128},{192,160},{224,1... | collective-permute-start | bytes 786440 | tf_op jit(solution)/shard_map/ppermute | solution.py:289
  64.4 6.6 %collective-permute-start.10 = (bf16[512,128]{1,0:T(8,128)(2,1)S(1)}, bf16[512,128]{1,0:T(8,128)(2,1)S(1)}, u32[]{:S(2)}, u32[]{:S(2)}) collective-permute-start(bf16[512,128]{1,0:T(8,128)(2,1)S(1)} %get-tuple-element.27), channel_id=1, source_target_pairs={{0,16},{16,0},{1,17},{17,1},{2,18},{18,2},{3,19},{19,3},{4,20},{20... | collective-permute-start | bytes 393224 | tf_op jit(solution)/shard_map/ppermute | solution.py:293
  73.0 4.6 %collective-permute-start.15 = (bf16[1024,128]{1,0:T(8,128)(2,1)S(1)}, bf16[1024,128]{1,0:T(8,128)(2,1)S(1)}, u32[]{:S(2)}, u32[]{:S(2)}) collective-permute-start(bf16[1024,128]{1,0:T(8,128)(2,1)S(1)} %collective-permute-done.13.refs_1_), channel_id=1, source_target_pairs={{0,480},{32,0},{64,32},{96,64},{128,96},{160,128},{192,160},{224,1... | collective-permute-start | bytes 786440 | tf_op jit(solution)/shard_map/ppermute | solution.py:289
  79.2 2.9 %collective-permute-done.11.refs_0_ = bf16[1024,128]{1,0:T(8,128)(2,1)S(1)} collective-permute-done((bf16[1024,128]{1,0:T(8,128)(2,1)S(1)}, bf16[1024,128]{1,0:T(8,128)(2,1)S(1)}, u32[]{:S(2)}, u32[]{:S(2)}) %collective-permute-start.11) | collective-permute-done | bytes 262176 | tf_op jit(solution)/shard_map/ppermute | solution.py:289
  84.0 4.6 %collective-permute-start.17 = (bf16[1024,128]{1,0:T(8,128)(2,1)S(1)}, bf16[1024,128]{1,0:T(8,128)(2,1)S(1)}, u32[]{:S(2)}, u32[]{:S(2)}) collective-permute-start(bf16[1024,128]{1,0:T(8,128)(2,1)S(1)} %collective-permute-done.15.refs_1_), channel_id=1, source_target_pairs={{0,480},{32,0},{64,32},{96,64},{128,96},{160,128},{192,160},{224,1... | collective-permute-start | bytes 786440 | tf_op jit(solution)/shard_map/ppermute | solution.py:289
  94.2 4.6 %collective-permute-start.19 = (bf16[1024,128]{1,0:T(8,128)(2,1)S(1)}, bf16[1024,128]{1,0:T(8,128)(2,1)S(1)}, u32[]{:S(2)}, u32[]{:S(2)}) collective-permute-start(bf16[1024,128]{1,0:T(8,128)(2,1)S(1)} %collective-permute-done.17.refs_1_), channel_id=1, source_target_pairs={{0,480},{32,0},{64,32},{96,64},{128,96},{160,128},{192,160},{224,1... | collective-permute-start | bytes 786440 | tf_op jit(solution)/shard_map/ppermute | solution.py:289
  103.4 4.6 %collective-permute-start.21 = (bf16[1024,128]{1,0:T(8,128)(2,1)S(1)}, bf16[1024,128]{1,0:T(8,128)(2,1)S(1)}, u32[]{:S(2)}, u32[]{:S(2)}) collective-permute-start(bf16[1024,128]{1,0:T(8,128)(2,1)S(1)} %collective-permute-done.19.refs_1_), channel_id=1, source_target_pairs={{0,480},{32,0},{64,32},{96,64},{128,96},{160,128},{192,160},{224,1... | collective-permute-start | bytes 786440 | tf_op jit(solution)/shard_map/ppermute | solution.py:289
  111.7 4.6 %collective-permute-start.23 = (bf16[1024,128]{1,0:T(8,128)(2,1)S(1)}, bf16[1024,128]{1,0:T(8,128)(2,1)S(1)}, u32[]{:S(2)}, u32[]{:S(2)}) collective-permute-start(bf16[1024,128]{1,0:T(8,128)(2,1)S(1)} %collective-permute-done.21.refs_1_), channel_id=1, source_target_pairs={{0,480},{32,0},{64,32},{96,64},{128,96},{160,128},{192,160},{224,1... | collective-permute-start | bytes 786440 | tf_op jit(solution)/shard_map/ppermute | solution.py:289
  120.0 4.6 %collective-permute-start.24 = (bf16[1024,128]{1,0:T(8,128)(2,1)S(1)}, bf16[1024,128]{1,0:T(8,128)(2,1)S(1)}, u32[]{:S(2)}, u32[]{:S(2)}) collective-permute-start(bf16[1024,128]{1,0:T(8,128)(2,1)S(1)} %collective-permute-done.23.refs_1_), channel_id=1, source_target_pairs={{0,480},{32,0},{64,32},{96,64},{128,96},{160,128},{192,160},{224,1... | collective-permute-start | bytes 786440 | tf_op jit(solution)/shard_map/ppermute | solution.py:289
  129.8 4.9 %collective-permute-done.22.refs_0_ = bf16[1024,128]{1,0:T(8,128)(2,1)S(1)} collective-permute-done((bf16[1024,128]{1,0:T(8,128)(2,1)S(1)}, bf16[1024,128]{1,0:T(8,128)(2,1)S(1)}, u32[]{:S(2)}, u32[]{:S(2)}) %collective-permute-start.22) | collective-permute-done | bytes 262176 | tf_op jit(solution)/shard_map/ppermute | solution.py:289
  135.3 9.1 %collective-permute-start.25 = (f32[136,512]{1,0:T(8,128)S(1)}, f32[136,512]{1,0:T(8,128)S(1)}, u32[]{:S(2)}, u32[]{:S(2)}) collective-permute-start(f32[136,512]{1,0:T(8,128)S(1)} %get-tuple-element.44), channel_id=1, source_target_pairs={{0,16},{16,0},{1,17},{17,1},{2,18},{18,2},{3,19},{19,3},{4,20},{20... | collective-permute-start | bytes 835592 | tf_op jit(solution)/shard_map/ppermute | solution.py:304
  (78 shorter events, 41.7 us)
Async XLA Ops:
  1.6 15.6 %collective-permute-start.1 = (bf16[528,256]{1,0:T(8,128)(2,1)S(1)}, bf16[528,256]{1,0:T(8,128)(2,1)S(1)}, u32[]{:S(2)}, u32[]{:S(2)}) collective-permute-start(bf16[528,256]{1,0:T(8,128)(2,1)S(1)} %get-tuple-element.61), channel_id=1, source_target_pairs={{0,3},{1,0},{2,1},{3,2},{4,7},{5,4},{6,5},{7,6},{8,11},{9,8},{10,9... | collective-permute-start | bytes 811016 | tf_op jit(solution)/shard_map/ppermute | solution.py:258
  7.1 10.1 %collective-permute-start.2 = (bf16[528,256]{1,0:T(8,128)(2,1)S(1)}, bf16[528,256]{1,0:T(8,128)(2,1)S(1)}, u32[]{:S(2)}, u32[]{:S(2)}) collective-permute-start(bf16[528,256]{1,0:T(8,128)(2,1)S(1)} %get-tuple-element.61), channel_id=1, source_target_pairs={{0,2},{1,3},{2,0},{3,1},{4,6},{5,7},{6,4},{7,5},{8,10},{9,11},{10,... | collective-permute-start | bytes 811016 | tf_op jit(solution)/shard_map/ppermute | solution.py:258
  9.4 12.3 %collective-permute-start = (bf16[528,256]{1,0:T(8,128)(2,1)S(1)}, bf16[528,256]{1,0:T(8,128)(2,1)S(1)}, u32[]{:S(2)}, u32[]{:S(2)}) collective-permute-start(bf16[528,256]{1,0:T(8,128)(2,1)S(1)} %get-tuple-element.61), channel_id=1, source_target_pairs={{0,1},{1,2},{2,3},{3,0},{4,5},{5,6},{6,7},{7,4},{8,9},{9,10},{10,1... | collective-permute-start | bytes 811016 | tf_op jit(solution)/shard_map/ppermute | solution.py:258
  17.3 13.0 %collective-permute-start.6 = (bf16[2,528,256]{2,1,0:T(8,128)(2,1)S(1)}, bf16[2,528,256]{2,1,0:T(8,128)(2,1)S(1)}, u32[]{:S(2)}, u32[]{:S(2)}) collective-permute-start(bf16[2,528,256]{2,1,0:T(8,128)(2,1)S(1)} %pad_maximum_fusion.2.refs_1_), channel_id=1, source_target_pairs={{0,12},{1,13},{2,14},{3,15},{4,0},{5,1},{6,2},{7,3},{8,4},{9,5},{1... | collective-permute-start | bytes 1622024 | tf_op jit(solution)/shard_map/ppermute | solution.py:260
  21.8 11.9 %collective-permute-start.3 = (bf16[2,528,256]{2,1,0:T(8,128)(2,1)S(1)}, bf16[2,528,256]{2,1,0:T(8,128)(2,1)S(1)}, u32[]{:S(2)}, u32[]{:S(2)}) collective-permute-start(bf16[2,528,256]{2,1,0:T(8,128)(2,1)S(1)} %pad_maximum_fusion.1.refs_0_), channel_id=1, source_target_pairs={{0,4},{1,5},{2,6},{3,7},{4,8},{5,9},{6,10},{7,11},{8,12},{9,13},{1... | collective-permute-start | bytes 1622024 | tf_op jit(solution)/shard_map/ppermute | solution.py:260
  23.8 15.4 %collective-permute-start.4 = (bf16[2,528,256]{2,1,0:T(8,128)(2,1)S(1)}, bf16[2,528,256]{2,1,0:T(8,128)(2,1)S(1)}, u32[]{:S(2)}, u32[]{:S(2)}) collective-permute-start(bf16[2,528,256]{2,1,0:T(8,128)(2,1)S(1)} %pad_maximum_fusion.2.refs_1_), channel_id=1, source_target_pairs={{0,4},{1,5},{2,6},{3,7},{4,8},{5,9},{6,10},{7,11},{8,12},{9,13},{1... | collective-permute-start | bytes 1622024 | tf_op jit(solution)/shard_map/ppermute | solution.py:260
  25.9 13.3 %collective-permute-start.5 = (bf16[2,528,256]{2,1,0:T(8,128)(2,1)S(1)}, bf16[2,528,256]{2,1,0:T(8,128)(2,1)S(1)}, u32[]{:S(2)}, u32[]{:S(2)}) collective-permute-start(bf16[2,528,256]{2,1,0:T(8,128)(2,1)S(1)} %pad_maximum_fusion.1.refs_0_), channel_id=1, source_target_pairs={{0,12},{1,13},{2,14},{3,15},{4,0},{5,1},{6,2},{7,3},{8,4},{9,5},{1... | collective-permute-start | bytes 1622024 | tf_op jit(solution)/shard_map/ppermute | solution.py:260
  30.3 12.1 %collective-permute-start.8 = (bf16[2,528,256]{2,1,0:T(8,128)(2,1)S(1)}, bf16[2,528,256]{2,1,0:T(8,128)(2,1)S(1)}, u32[]{:S(2)}, u32[]{:S(2)}) collective-permute-start(bf16[2,528,256]{2,1,0:T(8,128)(2,1)S(1)} %collective-permute-done.6.refs_5_), channel_id=1, source_target_pairs={{0,12},{1,13},{2,14},{3,15},{4,0},{5,1},{6,2},{7,3},{8,4},{9,5},{1... | collective-permute-start | bytes 1622024 | tf_op jit(solution)/shard_map/ppermute | solution.py:260
  33.7 11.6 %collective-permute-start.7 = (bf16[2,528,256]{2,1,0:T(8,128)(2,1)S(1)}, bf16[2,528,256]{2,1,0:T(8,128)(2,1)S(1)}, u32[]{:S(2)}, u32[]{:S(2)}) collective-permute-start(bf16[2,528,256]{2,1,0:T(8,128)(2,1)S(1)} %collective-permute-done.3.refs_2_), channel_id=1, source_target_pairs={{0,4},{1,5},{2,6},{3,7},{4,8},{5,9},{6,10},{7,11},{8,12},{9,13},{1... | collective-permute-start | bytes 1622024 | tf_op jit(solution)/shard_map/ppermute | solution.py:260
  49.6 14.9 %collective-permute-start.9 = (bf16[1024,128]{1,0:T(8,128)(2,1)S(1)}, bf16[1024,128]{1,0:T(8,128)(2,1)S(1)}, u32[]{:S(2)}, u32[]{:S(2)}) collective-permute-start(bf16[1024,128]{1,0:T(8,128)(2,1)S(1)} %get-tuple-element.25.refs_0_), channel_id=1, source_target_pairs={{0,32},{32,64},{64,96},{96,128},{128,160},{160,192},{192,224},{224... | collective-permute-start | bytes 786440 | tf_op jit(solution)/shard_map/ppermute | solution.py:289
  53.2 19.8 %collective-permute-start.13 = (bf16[1024,128]{1,0:T(8,128)(2,1)S(1)}, bf16[1024,128]{1,0:T(8,128)(2,1)S(1)}, u32[]{:S(2)}, u32[]{:S(2)}) collective-permute-start(bf16[1024,128]{1,0:T(8,128)(2,1)S(1)} %get-tuple-element.25.refs_0_), channel_id=1, source_target_pairs={{0,480},{32,0},{64,32},{96,64},{128,96},{160,128},{192,160},{224,1... | collective-permute-start | bytes 786440 | tf_op jit(solution)/shard_map/ppermute | solution.py:289
  64.4 13.2 %collective-permute-start.10 = (bf16[512,128]{1,0:T(8,128)(2,1)S(1)}, bf16[512,128]{1,0:T(8,128)(2,1)S(1)}, u32[]{:S(2)}, u32[]{:S(2)}) collective-permute-start(bf16[512,128]{1,0:T(8,128)(2,1)S(1)} %get-tuple-element.27), channel_id=1, source_target_pairs={{0,16},{16,0},{1,17},{17,1},{2,18},{18,2},{3,19},{19,3},{4,20},{20... | collective-permute-start | bytes 393224 | tf_op jit(solution)/shard_map/ppermute | solution.py:293
  71.1 11.0 %collective-permute-start.11 = (bf16[1024,128]{1,0:T(8,128)(2,1)S(1)}, bf16[1024,128]{1,0:T(8,128)(2,1)S(1)}, u32[]{:S(2)}, u32[]{:S(2)}) collective-permute-start(bf16[1024,128]{1,0:T(8,128)(2,1)S(1)} %collective-permute-done.9.refs_0_), channel_id=1, source_target_pairs={{0,32},{32,64},{64,96},{96,128},{128,160},{160,192},{192,224},{224... | collective-permute-start | bytes 786440 | tf_op jit(solution)/shard_map/ppermute | solution.py:289
  73.0 11.0 %collective-permute-start.15 = (bf16[1024,128]{1,0:T(8,128)(2,1)S(1)}, bf16[1024,128]{1,0:T(8,128)(2,1)S(1)}, u32[]{:S(2)}, u32[]{:S(2)}) collective-permute-start(bf16[1024,128]{1,0:T(8,128)(2,1)S(1)} %collective-permute-done.13.refs_1_), channel_id=1, source_target_pairs={{0,480},{32,0},{64,32},{96,64},{128,96},{160,128},{192,160},{224,1... | collective-permute-start | bytes 786440 | tf_op jit(solution)/shard_map/ppermute | solution.py:289
  82.1 10.1 %collective-permute-start.12 = (bf16[1024,128]{1,0:T(8,128)(2,1)S(1)}, bf16[1024,128]{1,0:T(8,128)(2,1)S(1)}, u32[]{:S(2)}, u32[]{:S(2)}) collective-permute-start(bf16[1024,128]{1,0:T(8,128)(2,1)S(1)} %collective-permute-done.11.refs_0_), channel_id=1, source_target_pairs={{0,32},{32,64},{64,96},{96,128},{128,160},{160,192},{192,224},{224... | collective-permute-start | bytes 786440 | tf_op jit(solution)/shard_map/ppermute | solution.py:289
  84.0 10.1 %collective-permute-start.17 = (bf16[1024,128]{1,0:T(8,128)(2,1)S(1)}, bf16[1024,128]{1,0:T(8,128)(2,1)S(1)}, u32[]{:S(2)}, u32[]{:S(2)}) collective-permute-start(bf16[1024,128]{1,0:T(8,128)(2,1)S(1)} %collective-permute-done.15.refs_1_), channel_id=1, source_target_pairs={{0,480},{32,0},{64,32},{96,64},{128,96},{160,128},{192,160},{224,1... | collective-permute-start | bytes 786440 | tf_op jit(solution)/shard_map/ppermute | solution.py:289
  92.2 9.2 %collective-permute-start.14 = (bf16[1024,128]{1,0:T(8,128)(2,1)S(1)}, bf16[1024,128]{1,0:T(8,128)(2,1)S(1)}, u32[]{:S(2)}, u32[]{:S(2)}) collective-permute-start(bf16[1024,128]{1,0:T(8,128)(2,1)S(1)} %collective-permute-done.12.refs_0_), channel_id=1, source_target_pairs={{0,32},{32,64},{64,96},{96,128},{128,160},{160,192},{192,224},{224... | collective-permute-start | bytes 786440 | tf_op jit(solution)/shard_map/ppermute | solution.py:289
  94.2 9.2 %collective-permute-start.19 = (bf16[1024,128]{1,0:T(8,128)(2,1)S(1)}, bf16[1024,128]{1,0:T(8,128)(2,1)S(1)}, u32[]{:S(2)}, u32[]{:S(2)}) collective-permute-start(bf16[1024,128]{1,0:T(8,128)(2,1)S(1)} %collective-permute-done.17.refs_1_), channel_id=1, source_target_pairs={{0,480},{32,0},{64,32},{96,64},{128,96},{160,128},{192,160},{224,1... | collective-permute-start | bytes 786440 | tf_op jit(solution)/shard_map/ppermute | solution.py:289
  101.4 8.3 %collective-permute-start.16 = (bf16[1024,128]{1,0:T(8,128)(2,1)S(1)}, bf16[1024,128]{1,0:T(8,128)(2,1)S(1)}, u32[]{:S(2)}, u32[]{:S(2)}) collective-permute-start(bf16[1024,128]{1,0:T(8,128)(2,1)S(1)} %collective-permute-done.14.refs_0_), channel_id=1, source_target_pairs={{0,32},{32,64},{64,96},{96,128},{128,160},{160,192},{192,224},{224... | collective-permute-start | bytes 786440 | tf_op jit(solution)/shard_map/ppermute | solution.py:289
  109.8 8.3 %collective-permute-start.18 = (bf16[1024,128]{1,0:T(8,128)(2,1)S(1)}, bf16[1024,128]{1,0:T(8,128)(2,1)S(1)}, u32[]{:S(2)}, u32[]{:S(2)}) collective-permute-start(bf16[1024,128]{1,0:T(8,128)(2,1)S(1)} %collective-permute-done.16.refs_0_), channel_id=1, source_target_pairs={{0,32},{32,64},{64,96},{96,128},{128,160},{160,192},{192,224},{224... | collective-permute-start | bytes 786440 | tf_op jit(solution)/shard_map/ppermute | solution.py:289
  118.1 8.3 %collective-permute-start.20 = (bf16[1024,128]{1,0:T(8,128)(2,1)S(1)}, bf16[1024,128]{1,0:T(8,128)(2,1)S(1)}, u32[]{:S(2)}, u32[]{:S(2)}) collective-permute-start(bf16[1024,128]{1,0:T(8,128)(2,1)S(1)} %collective-permute-done.18.refs_0_), channel_id=1, source_target_pairs={{0,32},{32,64},{64,96},{96,128},{128,160},{160,192},{192,224},{224... | collective-permute-start | bytes 786440 | tf_op jit(solution)/shard_map/ppermute | solution.py:289
  120.0 9.0 %collective-permute-start.24 = (bf16[1024,128]{1,0:T(8,128)(2,1)S(1)}, bf16[1024,128]{1,0:T(8,128)(2,1)S(1)}, u32[]{:S(2)}, u32[]{:S(2)}) collective-permute-start(bf16[1024,128]{1,0:T(8,128)(2,1)S(1)} %collective-permute-done.23.refs_1_), channel_id=1, source_target_pairs={{0,480},{32,0},{64,32},{96,64},{128,96},{160,128},{192,160},{224,1... | collective-permute-start | bytes 786440 | tf_op jit(solution)/shard_map/ppermute | solution.py:289
  126.4 8.3 %collective-permute-start.22 = (bf16[1024,128]{1,0:T(8,128)(2,1)S(1)}, bf16[1024,128]{1,0:T(8,128)(2,1)S(1)}, u32[]{:S(2)}, u32[]{:S(2)}) collective-permute-start(bf16[1024,128]{1,0:T(8,128)(2,1)S(1)} %collective-permute-done.20.refs_0_), channel_id=1, source_target_pairs={{0,32},{32,64},{64,96},{96,128},{128,160},{160,192},{192,224},{224... | collective-permute-start | bytes 786440 | tf_op jit(solution)/shard_map/ppermute | solution.py:289
  135.3 10.3 %collective-permute-start.25 = (f32[136,512]{1,0:T(8,128)S(1)}, f32[136,512]{1,0:T(8,128)S(1)}, u32[]{:S(2)}, u32[]{:S(2)}) collective-permute-start(f32[136,512]{1,0:T(8,128)S(1)} %get-tuple-element.44), channel_id=1, source_target_pairs={{0,16},{16,0},{1,17},{17,1},{2,18},{18,2},{3,19},{19,3},{4,20},{20... | collective-permute-start | bytes 835592 | tf_op jit(solution)/shard_map/ppermute | solution.py:304
  (6 other events, 29.7 us)

commit v6 on v5

--- a/solution.py
+++ b/solution.py
@@ -148,11 +148,9 @@
         alpha = jnp.exp2((m_old - m_new) * C2)
         total = st[t, HD + 1 : HD + 2, cols] * alpha
         acc = st[t, :HD, cols] * alpha
-        shift = m_new * C2
-        for j, s, ok in zip(js, ss, oks):
+        shift = jnp.maximum(m_new, 0.1 * NEG) * C2
+        for j, s in zip(js, ss):
             p = jnp.exp2(s * C2 - shift)
-            if masked:
-                p = jnp.where(ok, p, 0.0)
             total = total + jnp.sum(p, axis=0, keepdims=True)
             vt = jnp.concatenate(
                 [kvs[j][ROWS + b * HD : ROWS + (b + 1) * HD, :] for b in range(ROWS // HD)], axis=1

time: 147 us -> 147 us (level)
  no operation moved by 1% of the time
where the time goes in v6:
time: 147 us; the launch traced here: 146 us
  starting transfers between devices  98 us (67%)
  waiting for transfers between devices  27.8 us (19%)
  Pallas kernels  12.5 us (9%)
  other arithmetic  4.76 us (3%)
  local copies, waits for them, and re-layouts  2.79 us (2%)
    ppermute x15, starting transfers between devices, body(): z_step = lambda v, d: lax.ppermute(v, 'z', ring(NZ, d))  53.9 us
    ppermute x6, starting transfers between devices, body(): far = lambda v, d: lax.ppermute(v, plane, plane_perm(d, False))  18.1 us
    ppermute x15, waiting for transfers between devices, body(): z_step = lambda v, d: lax.ppermute(v, 'z', ring(NZ, d))  17.4 us
    ppermute x3, starting transfers between devices, body(): lax.ppermute(mine, plane, plane_perm(d, True))  10.3 us
    ppermute x6, waiting for transfers between devices, body(): far = lambda v, d: lax.ppermute(v, plane, plane_perm(d, False))  9.18 us
    ppermute x1, starting transfers between devices, body(): return merge(own, lax.ppermute(other, 'core', ring(2, 1)))  9.11 us
    pallas_call x9, Pallas kernels, attend(): pl.pallas_call(functools.partial(attend_kernel, offs, not state, last_cal...  7.42 us
    ppermute x1, starting transfers between devices, body(): q2 = jnp.stack([q, lax.ppermute(q, 'core', ring(2, 1))], axis=0)  6.62 us
  transfers between devices with their start and end apart: 26, of which 12 were waited for; matrix products, arithmetic and copies ran while one was open for 4% of the time, Pallas kernels for 5%

profile of v6, /device:TPU:1, one launch (start us, length us, event | category | flops | bytes accessed | tf_op | source)
XLA Modules:
  0.0 146.4 jit_solution(2915867155858930051)
XLA Ops:
  1.6 5.5 %collective-permute-start.1 = (bf16[528,256]{1,0:T(8,128)(2,1)S(1)}, bf16[528,256]{1,0:T(8,128)(2,1)S(1)}, u32[]{:S(2)}, u32[]{:S(2)}) collective-permute-start(bf16[528,256]{1,0:T(8,128)(2,1)S(1)} %get-tuple-element.61), channel_id=1, source_target_pairs={{0,3},{1,0},{2,1},{3,2},{4,7},{5,4},{6,5},{7,6},{8,11},{9,8},{10,9... | collective-permute-start | bytes 811016 | tf_op jit(solution)/shard_map/ppermute | solution.py:256
  7.1 2.3 %collective-permute-start.2 = (bf16[528,256]{1,0:T(8,128)(2,1)S(1)}, bf16[528,256]{1,0:T(8,128)(2,1)S(1)}, u32[]{:S(2)}, u32[]{:S(2)}) collective-permute-start(bf16[528,256]{1,0:T(8,128)(2,1)S(1)} %get-tuple-element.61), channel_id=1, source_target_pairs={{0,2},{1,3},{2,0},{3,1},{4,6},{5,7},{6,4},{7,5},{8,10},{9,11},{10,... | collective-permute-start | bytes 811016 | tf_op jit(solution)/shard_map/ppermute | solution.py:256
  9.4 2.6 %collective-permute-start = (bf16[528,256]{1,0:T(8,128)(2,1)S(1)}, bf16[528,256]{1,0:T(8,128)(2,1)S(1)}, u32[]{:S(2)}, u32[]{:S(2)}) collective-permute-start(bf16[528,256]{1,0:T(8,128)(2,1)S(1)} %get-tuple-element.61), channel_id=1, source_target_pairs={{0,1},{1,2},{2,3},{3,0},{4,5},{5,6},{6,7},{7,4},{8,9},{9,10},{10,1... | collective-permute-start | bytes 811016 | tf_op jit(solution)/shard_map/ppermute | solution.py:256
  13.6 2.1 %slice_bitcast_fusion.2 = (bf16[4096,128]{1,0:T(8,128)(2,1)S(1)}, bf16[4096,128]{1,0:T(8,128)(2,1)S(1)}, bf16[4096,128]{1,0:T(8,128)(2,1)S(1)}) fusion(bf16[3,4096,128]{2,1,0:T(8,128)(2,1)} %param.10), kind=kLoop, calls=%fused_computation.3 | loop fusion | bytes 6291456 | tf_op jit(solution)/shard_map/squeeze | solution.py:283
  17.3 4.4 %collective-permute-start.6 = (bf16[2,528,256]{2,1,0:T(8,128)(2,1)S(1)}, bf16[2,528,256]{2,1,0:T(8,128)(2,1)S(1)}, u32[]{:S(2)}, u32[]{:S(2)}) collective-permute-start(bf16[2,528,256]{2,1,0:T(8,128)(2,1)S(1)} %pad_maximum_fusion.2.refs_1_), channel_id=1, source_target_pairs={{0,12},{1,13},{2,14},{3,15},{4,0},{5,1},{6,2},{7,3},{8,4},{9,5},{1... | collective-permute-start | bytes 1622024 | tf_op jit(solution)/shard_map/ppermute | solution.py:258
  25.9 4.4 %collective-permute-start.5 = (bf16[2,528,256]{2,1,0:T(8,128)(2,1)S(1)}, bf16[2,528,256]{2,1,0:T(8,128)(2,1)S(1)}, u32[]{:S(2)}, u32[]{:S(2)}) collective-permute-start(bf16[2,528,256]{2,1,0:T(8,128)(2,1)S(1)} %pad_maximum_fusion.1.refs_0_), channel_id=1, source_target_pairs={{0,12},{1,13},{2,14},{3,15},{4,0},{5,1},{6,2},{7,3},{8,4},{9,5},{1... | collective-permute-start | bytes 1622024 | tf_op jit(solution)/shard_map/ppermute | solution.py:258
  30.3 3.4 %collective-permute-start.8 = (bf16[2,528,256]{2,1,0:T(8,128)(2,1)S(1)}, bf16[2,528,256]{2,1,0:T(8,128)(2,1)S(1)}, u32[]{:S(2)}, u32[]{:S(2)}) collective-permute-start(bf16[2,528,256]{2,1,0:T(8,128)(2,1)S(1)} %collective-permute-done.6.refs_5_), channel_id=1, source_target_pairs={{0,12},{1,13},{2,14},{3,15},{4,0},{5,1},{6,2},{7,3},{8,4},{9,5},{1... | collective-permute-start | bytes 1622024 | tf_op jit(solution)/shard_map/ppermute | solution.py:258
  36.1 3.1 %collective-permute-done.4.refs_3_ = bf16[2,528,256]{2,1,0:T(8,128)(2,1)S(1)} collective-permute-done((bf16[2,528,256]{2,1,0:T(8,128)(2,1)S(1)}, bf16[2,528,256]{2,1,0:T(8,128)(2,1)S(1)}, u32[]{:S(2)}, u32[]{:S(2)}) %collective-permute-start.4) | collective-permute-done | bytes 540704 | tf_op jit(solution)/shard_map/ppermute | solution.py:258
  39.2 3.2 %collective-permute-done.8.refs_7_ = bf16[2,528,256]{2,1,0:T(8,128)(2,1)S(1)} collective-permute-done((bf16[2,528,256]{2,1,0:T(8,128)(2,1)S(1)}, bf16[2,528,256]{2,1,0:T(8,128)(2,1)S(1)}, u32[]{:S(2)}, u32[]{:S(2)}) %collective-permute-start.8) | collective-permute-done | bytes 540704 | tf_op jit(solution)/shard_map/ppermute | solution.py:258
  42.4 2.9 %collective-permute-done.7.refs_6_ = bf16[2,528,256]{2,1,0:T(8,128)(2,1)S(1)} collective-permute-done((bf16[2,528,256]{2,1,0:T(8,128)(2,1)S(1)}, bf16[2,528,256]{2,1,0:T(8,128)(2,1)S(1)}, u32[]{:S(2)}, u32[]{:S(2)}) %collective-permute-start.7) | collective-permute-done | bytes 540704 | tf_op jit(solution)/shard_map/ppermute | solution.py:258
  45.3 4.3 %norm_qkv.1 = (bf16[512,128]{1,0:T(8,128)(2,1)S(1)}, bf16[1024,128]{1,0:T(8,128)(2,1)S(1)}) custom-call(s32[16]{0:T(128)S(1)} %fusion.1.blk_ref, bf16[2,528,256]{2,1,0:T(8,128)(2,1)S(1)} %pad_maximum_fusion.1.refs_0_, bf16[2,528,256]{2,1,0:T(8,128)(2,1)S(1)} %pad_maximum_fusion.2.refs_1_, bf16[2,528,256]{2,1,0:T(8,128)(2,1)S(1)} %collective-permute-done.3.refs_2_, ...), custom_call_target="tpu_custom_call" | custom-call | flops 1610612736 | bytes 8388608 | tf_op jit(solution)/shard_map/norm_qkv/pallas_call | solution.py:95
  49.6 3.5 %collective-permute-start.9 = (bf16[1024,128]{1,0:T(8,128)(2,1)S(1)}, bf16[1024,128]{1,0:T(8,128)(2,1)S(1)}, u32[]{:S(2)}, u32[]{:S(2)}) collective-permute-start(bf16[1024,128]{1,0:T(8,128)(2,1)S(1)} %get-tuple-element.25.refs_0_), channel_id=1, source_target_pairs={{0,32},{32,64},{64,96},{96,128},{128,160},{160,192},{192,224},{224... | collective-permute-start | bytes 786440 | tf_op jit(solution)/shard_map/ppermute | solution.py:287
  53.2 9.5 %collective-permute-start.13 = (bf16[1024,128]{1,0:T(8,128)(2,1)S(1)}, bf16[1024,128]{1,0:T(8,128)(2,1)S(1)}, u32[]{:S(2)}, u32[]{:S(2)}) collective-permute-start(bf16[1024,128]{1,0:T(8,128)(2,1)S(1)} %get-tuple-element.25.refs_0_), channel_id=1, source_target_pairs={{0,480},{32,0},{64,32},{96,64},{128,96},{160,128},{192,160},{224,1... | collective-permute-start | bytes 786440 | tf_op jit(solution)/shard_map/ppermute | solution.py:287
  64.4 6.6 %collective-permute-start.10 = (bf16[512,128]{1,0:T(8,128)(2,1)S(1)}, bf16[512,128]{1,0:T(8,128)(2,1)S(1)}, u32[]{:S(2)}, u32[]{:S(2)}) collective-permute-start(bf16[512,128]{1,0:T(8,128)(2,1)S(1)} %get-tuple-element.27), channel_id=1, source_target_pairs={{0,16},{16,0},{1,17},{17,1},{2,18},{18,2},{3,19},{19,3},{4,20},{20... | collective-permute-start | bytes 393224 | tf_op jit(solution)/shard_map/ppermute | solution.py:291
  73.0 4.6 %collective-permute-start.15 = (bf16[1024,128]{1,0:T(8,128)(2,1)S(1)}, bf16[1024,128]{1,0:T(8,128)(2,1)S(1)}, u32[]{:S(2)}, u32[]{:S(2)}) collective-permute-start(bf16[1024,128]{1,0:T(8,128)(2,1)S(1)} %collective-permute-done.13.refs_1_), channel_id=1, source_target_pairs={{0,480},{32,0},{64,32},{96,64},{128,96},{160,128},{192,160},{224,1... | collective-permute-start | bytes 786440 | tf_op jit(solution)/shard_map/ppermute | solution.py:287
  79.0 3.1 %collective-permute-done.11.refs_0_ = bf16[1024,128]{1,0:T(8,128)(2,1)S(1)} collective-permute-done((bf16[1024,128]{1,0:T(8,128)(2,1)S(1)}, bf16[1024,128]{1,0:T(8,128)(2,1)S(1)}, u32[]{:S(2)}, u32[]{:S(2)}) %collective-permute-start.11) | collective-permute-done | bytes 262176 | tf_op jit(solution)/shard_map/ppermute | solution.py:287
  84.0 4.6 %collective-permute-start.17 = (bf16[1024,128]{1,0:T(8,128)(2,1)S(1)}, bf16[1024,128]{1,0:T(8,128)(2,1)S(1)}, u32[]{:S(2)}, u32[]{:S(2)}) collective-permute-start(bf16[1024,128]{1,0:T(8,128)(2,1)S(1)} %collective-permute-done.15.refs_1_), channel_id=1, source_target_pairs={{0,480},{32,0},{64,32},{96,64},{128,96},{160,128},{192,160},{224,1... | collective-permute-start | bytes 786440 | tf_op jit(solution)/shard_map/ppermute | solution.py:287
  90.0 2.2 %collective-permute-done.12.refs_0_ = bf16[1024,128]{1,0:T(8,128)(2,1)S(1)} collective-permute-done((bf16[1024,128]{1,0:T(8,128)(2,1)S(1)}, bf16[1024,128]{1,0:T(8,128)(2,1)S(1)}, u32[]{:S(2)}, u32[]{:S(2)}) %collective-permute-start.12) | collective-permute-done | bytes 262176 | tf_op jit(solution)/shard_map/ppermute | solution.py:287
  94.2 4.6 %collective-permute-start.19 = (bf16[1024,128]{1,0:T(8,128)(2,1)S(1)}, bf16[1024,128]{1,0:T(8,128)(2,1)S(1)}, u32[]{:S(2)}, u32[]{:S(2)}) collective-permute-start(bf16[1024,128]{1,0:T(8,128)(2,1)S(1)} %collective-permute-done.17.refs_1_), channel_id=1, source_target_pairs={{0,480},{32,0},{64,32},{96,64},{128,96},{160,128},{192,160},{224,1... | collective-permute-start | bytes 786440 | tf_op jit(solution)/shard_map/ppermute | solution.py:287
  103.4 4.6 %collective-permute-start.21 = (bf16[1024,128]{1,0:T(8,128)(2,1)S(1)}, bf16[1024,128]{1,0:T(8,128)(2,1)S(1)}, u32[]{:S(2)}, u32[]{:S(2)}) collective-permute-start(bf16[1024,128]{1,0:T(8,128)(2,1)S(1)} %collective-permute-done.19.refs_1_), channel_id=1, source_target_pairs={{0,480},{32,0},{64,32},{96,64},{128,96},{160,128},{192,160},{224,1... | collective-permute-start | bytes 786440 | tf_op jit(solution)/shard_map/ppermute | solution.py:287
  111.7 4.6 %collective-permute-start.23 = (bf16[1024,128]{1,0:T(8,128)(2,1)S(1)}, bf16[1024,128]{1,0:T(8,128)(2,1)S(1)}, u32[]{:S(2)}, u32[]{:S(2)}) collective-permute-start(bf16[1024,128]{1,0:T(8,128)(2,1)S(1)} %collective-permute-done.21.refs_1_), channel_id=1, source_target_pairs={{0,480},{32,0},{64,32},{96,64},{128,96},{160,128},{192,160},{224,1... | collective-permute-start | bytes 786440 | tf_op jit(solution)/shard_map/ppermute | solution.py:287
  120.0 4.6 %collective-permute-start.24 = (bf16[1024,128]{1,0:T(8,128)(2,1)S(1)}, bf16[1024,128]{1,0:T(8,128)(2,1)S(1)}, u32[]{:S(2)}, u32[]{:S(2)}) collective-permute-start(bf16[1024,128]{1,0:T(8,128)(2,1)S(1)} %collective-permute-done.23.refs_1_), channel_id=1, source_target_pairs={{0,480},{32,0},{64,32},{96,64},{128,96},{160,128},{192,160},{224,1... | collective-permute-start | bytes 786440 | tf_op jit(solution)/shard_map/ppermute | solution.py:287
  129.6 5.1 %collective-permute-done.22.refs_0_ = bf16[1024,128]{1,0:T(8,128)(2,1)S(1)} collective-permute-done((bf16[1024,128]{1,0:T(8,128)(2,1)S(1)}, bf16[1024,128]{1,0:T(8,128)(2,1)S(1)}, u32[]{:S(2)}, u32[]{:S(2)}) %collective-permute-start.22) | collective-permute-done | bytes 262176 | tf_op jit(solution)/shard_map/ppermute | solution.py:287
  135.3 9.1 %collective-permute-start.25 = (f32[136,512]{1,0:T(8,128)S(1)}, f32[136,512]{1,0:T(8,128)S(1)}, u32[]{:S(2)}, u32[]{:S(2)}) collective-permute-start(f32[136,512]{1,0:T(8,128)S(1)} %get-tuple-element.44), channel_id=1, source_target_pairs={{0,16},{16,0},{1,17},{17,1},{2,18},{18,2},{3,19},{19,3},{4,20},{20... | collective-permute-start | bytes 835592 | tf_op jit(solution)/shard_map/ppermute | solution.py:302
  (78 shorter events, 41.2 us)
Async XLA Ops:
  1.6 15.6 %collective-permute-start.1 = (bf16[528,256]{1,0:T(8,128)(2,1)S(1)}, bf16[528,256]{1,0:T(8,128)(2,1)S(1)}, u32[]{:S(2)}, u32[]{:S(2)}) collective-permute-start(bf16[528,256]{1,0:T(8,128)(2,1)S(1)} %get-tuple-element.61), channel_id=1, source_target_pairs={{0,3},{1,0},{2,1},{3,2},{4,7},{5,4},{6,5},{7,6},{8,11},{9,8},{10,9... | collective-permute-start | bytes 811016 | tf_op jit(solution)/shard_map/ppermute | solution.py:256
  7.1 10.1 %collective-permute-start.2 = (bf16[528,256]{1,0:T(8,128)(2,1)S(1)}, bf16[528,256]{1,0:T(8,128)(2,1)S(1)}, u32[]{:S(2)}, u32[]{:S(2)}) collective-permute-start(bf16[528,256]{1,0:T(8,128)(2,1)S(1)} %get-tuple-element.61), channel_id=1, source_target_pairs={{0,2},{1,3},{2,0},{3,1},{4,6},{5,7},{6,4},{7,5},{8,10},{9,11},{10,... | collective-permute-start | bytes 811016 | tf_op jit(solution)/shard_map/ppermute | solution.py:256
  9.4 12.3 %collective-permute-start = (bf16[528,256]{1,0:T(8,128)(2,1)S(1)}, bf16[528,256]{1,0:T(8,128)(2,1)S(1)}, u32[]{:S(2)}, u32[]{:S(2)}) collective-permute-start(bf16[528,256]{1,0:T(8,128)(2,1)S(1)} %get-tuple-element.61), channel_id=1, source_target_pairs={{0,1},{1,2},{2,3},{3,0},{4,5},{5,6},{6,7},{7,4},{8,9},{9,10},{10,1... | collective-permute-start | bytes 811016 | tf_op jit(solution)/shard_map/ppermute | solution.py:256
  17.3 13.0 %collective-permute-start.6 = (bf16[2,528,256]{2,1,0:T(8,128)(2,1)S(1)}, bf16[2,528,256]{2,1,0:T(8,128)(2,1)S(1)}, u32[]{:S(2)}, u32[]{:S(2)}) collective-permute-start(bf16[2,528,256]{2,1,0:T(8,128)(2,1)S(1)} %pad_maximum_fusion.2.refs_1_), channel_id=1, source_target_pairs={{0,12},{1,13},{2,14},{3,15},{4,0},{5,1},{6,2},{7,3},{8,4},{9,5},{1... | collective-permute-start | bytes 1622024 | tf_op jit(solution)/shard_map/ppermute | solution.py:258
  21.8 11.9 %collective-permute-start.3 = (bf16[2,528,256]{2,1,0:T(8,128)(2,1)S(1)}, bf16[2,528,256]{2,1,0:T(8,128)(2,1)S(1)}, u32[]{:S(2)}, u32[]{:S(2)}) collective-permute-start(bf16[2,528,256]{2,1,0:T(8,128)(2,1)S(1)} %pad_maximum_fusion.1.refs_0_), channel_id=1, source_target_pairs={{0,4},{1,5},{2,6},{3,7},{4,8},{5,9},{6,10},{7,11},{8,12},{9,13},{1... | collective-permute-start | bytes 1622024 | tf_op jit(solution)/shard_map/ppermute | solution.py:258
  23.8 15.4 %collective-permute-start.4 = (bf16[2,528,256]{2,1,0:T(8,128)(2,1)S(1)}, bf16[2,528,256]{2,1,0:T(8,128)(2,1)S(1)}, u32[]{:S(2)}, u32[]{:S(2)}) collective-permute-start(bf16[2,528,256]{2,1,0:T(8,128)(2,1)S(1)} %pad_maximum_fusion.2.refs_1_), channel_id=1, source_target_pairs={{0,4},{1,5},{2,6},{3,7},{4,8},{5,9},{6,10},{7,11},{8,12},{9,13},{1... | collective-permute-start | bytes 1622024 | tf_op jit(solution)/shard_map/ppermute | solution.py:258
  25.9 13.3 %collective-permute-start.5 = (bf16[2,528,256]{2,1,0:T(8,128)(2,1)S(1)}, bf16[2,528,256]{2,1,0:T(8,128)(2,1)S(1)}, u32[]{:S(2)}, u32[]{:S(2)}) collective-permute-start(bf16[2,528,256]{2,1,0:T(8,128)(2,1)S(1)} %pad_maximum_fusion.1.refs_0_), channel_id=1, source_target_pairs={{0,12},{1,13},{2,14},{3,15},{4,0},{5,1},{6,2},{7,3},{8,4},{9,5},{1... | collective-permute-start | bytes 1622024 | tf_op jit(solution)/shard_map/ppermute | solution.py:258
  30.3 12.1 %collective-permute-start.8 = (bf16[2,528,256]{2,1,0:T(8,128)(2,1)S(1)}, bf16[2,528,256]{2,1,0:T(8,128)(2,1)S(1)}, u32[]{:S(2)}, u32[]{:S(2)}) collective-permute-start(bf16[2,528,256]{2,1,0:T(8,128)(2,1)S(1)} %collective-permute-done.6.refs_5_), channel_id=1, source_target_pairs={{0,12},{1,13},{2,14},{3,15},{4,0},{5,1},{6,2},{7,3},{8,4},{9,5},{1... | collective-permute-start | bytes 1622024 | tf_op jit(solution)/shard_map/ppermute | solution.py:258
  33.7 11.6 %collective-permute-start.7 = (bf16[2,528,256]{2,1,0:T(8,128)(2,1)S(1)}, bf16[2,528,256]{2,1,0:T(8,128)(2,1)S(1)}, u32[]{:S(2)}, u32[]{:S(2)}) collective-permute-start(bf16[2,528,256]{2,1,0:T(8,128)(2,1)S(1)} %collective-permute-done.3.refs_2_), channel_id=1, source_target_pairs={{0,4},{1,5},{2,6},{3,7},{4,8},{5,9},{6,10},{7,11},{8,12},{9,13},{1... | collective-permute-start | bytes 1622024 | tf_op jit(solution)/shard_map/ppermute | solution.py:258
  49.6 14.9 %collective-permute-start.9 = (bf16[1024,128]{1,0:T(8,128)(2,1)S(1)}, bf16[1024,128]{1,0:T(8,128)(2,1)S(1)}, u32[]{:S(2)}, u32[]{:S(2)}) collective-permute-start(bf16[1024,128]{1,0:T(8,128)(2,1)S(1)} %get-tuple-element.25.refs_0_), channel_id=1, source_target_pairs={{0,32},{32,64},{64,96},{96,128},{128,160},{160,192},{192,224},{224... | collective-permute-start | bytes 786440 | tf_op jit(solution)/shard_map/ppermute | solution.py:287
  53.2 19.8 %collective-permute-start.13 = (bf16[1024,128]{1,0:T(8,128)(2,1)S(1)}, bf16[1024,128]{1,0:T(8,128)(2,1)S(1)}, u32[]{:S(2)}, u32[]{:S(2)}) collective-permute-start(bf16[1024,128]{1,0:T(8,128)(2,1)S(1)} %get-tuple-element.25.refs_0_), channel_id=1, source_target_pairs={{0,480},{32,0},{64,32},{96,64},{128,96},{160,128},{192,160},{224,1... | collective-permute-start | bytes 786440 | tf_op jit(solution)/shard_map/ppermute | solution.py:287
  64.4 13.2 %collective-permute-start.10 = (bf16[512,128]{1,0:T(8,128)(2,1)S(1)}, bf16[512,128]{1,0:T(8,128)(2,1)S(1)}, u32[]{:S(2)}, u32[]{:S(2)}) collective-permute-start(bf16[512,128]{1,0:T(8,128)(2,1)S(1)} %get-tuple-element.27), channel_id=1, source_target_pairs={{0,16},{16,0},{1,17},{17,1},{2,18},{18,2},{3,19},{19,3},{4,20},{20... | collective-permute-start | bytes 393224 | tf_op jit(solution)/shard_map/ppermute | solution.py:291
  71.1 11.0 %collective-permute-start.11 = (bf16[1024,128]{1,0:T(8,128)(2,1)S(1)}, bf16[1024,128]{1,0:T(8,128)(2,1)S(1)}, u32[]{:S(2)}, u32[]{:S(2)}) collective-permute-start(bf16[1024,128]{1,0:T(8,128)(2,1)S(1)} %collective-permute-done.9.refs_0_), channel_id=1, source_target_pairs={{0,32},{32,64},{64,96},{96,128},{128,160},{160,192},{192,224},{224... | collective-permute-start | bytes 786440 | tf_op jit(solution)/shard_map/ppermute | solution.py:287
  73.0 11.0 %collective-permute-start.15 = (bf16[1024,128]{1,0:T(8,128)(2,1)S(1)}, bf16[1024,128]{1,0:T(8,128)(2,1)S(1)}, u32[]{:S(2)}, u32[]{:S(2)}) collective-permute-start(bf16[1024,128]{1,0:T(8,128)(2,1)S(1)} %collective-permute-done.13.refs_1_), channel_id=1, source_target_pairs={{0,480},{32,0},{64,32},{96,64},{128,96},{160,128},{192,160},{224,1... | collective-permute-start | bytes 786440 | tf_op jit(solution)/shard_map/ppermute | solution.py:287
  82.1 10.1 %collective-permute-start.12 = (bf16[1024,128]{1,0:T(8,128)(2,1)S(1)}, bf16[1024,128]{1,0:T(8,128)(2,1)S(1)}, u32[]{:S(2)}, u32[]{:S(2)}) collective-permute-start(bf16[1024,128]{1,0:T(8,128)(2,1)S(1)} %collective-permute-done.11.refs_0_), channel_id=1, source_target_pairs={{0,32},{32,64},{64,96},{96,128},{128,160},{160,192},{192,224},{224... | collective-permute-start | bytes 786440 | tf_op jit(solution)/shard_map/ppermute | solution.py:287
  84.0 10.1 %collective-permute-start.17 = (bf16[1024,128]{1,0:T(8,128)(2,1)S(1)}, bf16[1024,128]{1,0:T(8,128)(2,1)S(1)}, u32[]{:S(2)}, u32[]{:S(2)}) collective-permute-start(bf16[1024,128]{1,0:T(8,128)(2,1)S(1)} %collective-permute-done.15.refs_1_), channel_id=1, source_target_pairs={{0,480},{32,0},{64,32},{96,64},{128,96},{160,128},{192,160},{224,1... | collective-permute-start | bytes 786440 | tf_op jit(solution)/shard_map/ppermute | solution.py:287
  92.2 9.2 %collective-permute-start.14 = (bf16[1024,128]{1,0:T(8,128)(2,1)S(1)}, bf16[1024,128]{1,0:T(8,128)(2,1)S(1)}, u32[]{:S(2)}, u32[]{:S(2)}) collective-permute-start(bf16[1024,128]{1,0:T(8,128)(2,1)S(1)} %collective-permute-done.12.refs_0_), channel_id=1, source_target_pairs={{0,32},{32,64},{64,96},{96,128},{128,160},{160,192},{192,224},{224... | collective-permute-start | bytes 786440 | tf_op jit(solution)/shard_map/ppermute | solution.py:287
  94.2 9.2 %collective-permute-start.19 = (bf16[1024,128]{1,0:T(8,128)(2,1)S(1)}, bf16[1024,128]{1,0:T(8,128)(2,1)S(1)}, u32[]{:S(2)}, u32[]{:S(2)}) collective-permute-start(bf16[1024,128]{1,0:T(8,128)(2,1)S(1)} %collective-permute-done.17.refs_1_), channel_id=1, source_target_pairs={{0,480},{32,0},{64,32},{96,64},{128,96},{160,128},{192,160},{224,1... | collective-permute-start | bytes 786440 | tf_op jit(solution)/shard_map/ppermute | solution.py:287
  101.4 8.3 %collective-permute-start.16 = (bf16[1024,128]{1,0:T(8,128)(2,1)S(1)}, bf16[1024,128]{1,0:T(8,128)(2,1)S(1)}, u32[]{:S(2)}, u32[]{:S(2)}) collective-permute-start(bf16[1024,128]{1,0:T(8,128)(2,1)S(1)} %collective-permute-done.14.refs_0_), channel_id=1, source_target_pairs={{0,32},{32,64},{64,96},{96,128},{128,160},{160,192},{192,224},{224... | collective-permute-start | bytes 786440 | tf_op jit(solution)/shard_map/ppermute | solution.py:287
  109.8 8.3 %collective-permute-start.18 = (bf16[1024,128]{1,0:T(8,128)(2,1)S(1)}, bf16[1024,128]{1,0:T(8,128)(2,1)S(1)}, u32[]{:S(2)}, u32[]{:S(2)}) collective-permute-start(bf16[1024,128]{1,0:T(8,128)(2,1)S(1)} %collective-permute-done.16.refs_0_), channel_id=1, source_target_pairs={{0,32},{32,64},{64,96},{96,128},{128,160},{160,192},{192,224},{224... | collective-permute-start | bytes 786440 | tf_op jit(solution)/shard_map/ppermute | solution.py:287
  118.1 8.3 %collective-permute-start.20 = (bf16[1024,128]{1,0:T(8,128)(2,1)S(1)}, bf16[1024,128]{1,0:T(8,128)(2,1)S(1)}, u32[]{:S(2)}, u32[]{:S(2)}) collective-permute-start(bf16[1024,128]{1,0:T(8,128)(2,1)S(1)} %collective-permute-done.18.refs_0_), channel_id=1, source_target_pairs={{0,32},{32,64},{64,96},{96,128},{128,160},{160,192},{192,224},{224... | collective-permute-start | bytes 786440 | tf_op jit(solution)/shard_map/ppermute | solution.py:287
  120.0 9.0 %collective-permute-start.24 = (bf16[1024,128]{1,0:T(8,128)(2,1)S(1)}, bf16[1024,128]{1,0:T(8,128)(2,1)S(1)}, u32[]{:S(2)}, u32[]{:S(2)}) collective-permute-start(bf16[1024,128]{1,0:T(8,128)(2,1)S(1)} %collective-permute-done.23.refs_1_), channel_id=1, source_target_pairs={{0,480},{32,0},{64,32},{96,64},{128,96},{160,128},{192,160},{224,1... | collective-permute-start | bytes 786440 | tf_op jit(solution)/shard_map/ppermute | solution.py:287
  126.4 8.3 %collective-permute-start.22 = (bf16[1024,128]{1,0:T(8,128)(2,1)S(1)}, bf16[1024,128]{1,0:T(8,128)(2,1)S(1)}, u32[]{:S(2)}, u32[]{:S(2)}) collective-permute-start(bf16[1024,128]{1,0:T(8,128)(2,1)S(1)} %collective-permute-done.20.refs_0_), channel_id=1, source_target_pairs={{0,32},{32,64},{64,96},{96,128},{128,160},{160,192},{192,224},{224... | collective-permute-start | bytes 786440 | tf_op jit(solution)/shard_map/ppermute | solution.py:287
  135.3 10.3 %collective-permute-start.25 = (f32[136,512]{1,0:T(8,128)S(1)}, f32[136,512]{1,0:T(8,128)S(1)}, u32[]{:S(2)}, u32[]{:S(2)}) collective-permute-start(f32[136,512]{1,0:T(8,128)S(1)} %get-tuple-element.44), channel_id=1, source_target_pairs={{0,16},{16,0},{1,17},{17,1},{2,18},{18,2},{3,19},{19,3},{4,20},{20... | collective-permute-start | bytes 835592 | tf_op jit(solution)/shard_map/ppermute | solution.py:302
  (6 other events, 29.7 us)
